TPU v7x, 128 devices: a whole 4x4x4 slice. The times are simulated.
128 devices in a mesh: wide: 16 (over z, x), narrow: 8 (over y, core).
Axes of the slice: x: 4, y: 4, z: 4, core: 2. Of those that a mesh axis runs over, the one named last changes fastest.
Arguments:
- tokens: bfloat16 [1024, 16384], P(None, ('narrow', 'wide')), may hold values from -6 to 6
- gate_weight: bfloat16 [16384, 26624], P('narrow', 'wide'), may hold values from -0.0625 to 0.0625
- up_weight: bfloat16 [16384, 26624], P('narrow', 'wide'), may hold values from -0.0625 to 0.0625
- down_weight: bfloat16 [26624, 16384], P('wide', 'narrow'), may hold values from -0.0546875 to 0.0546875
Outputs:
- mixed: bfloat16 [1024, 16384], P(None, ('narrow', 'wide'))
All inputs are finite; a program needn't handle non-finite values.
Results may differ from a plain program's by a relative error of at most 0.005.
Values may be sent and summed in bfloat16 or wider, within the bound.
No kernel may reach another device: no remote copies, remote signals or barrier semaphores. Data moves between devices by JAX's collectives and lax.ppermute only.
A program may use at most 128 MiB of HBM per device.

v0:
```python
import functools

import jax
import jax.numpy as jnp
from jax import lax
from jax.experimental import pallas as pl
from jax.experimental.pallas import tpu as pltpu
from jax.sharding import PartitionSpec as P

LANES = 128
LIMIT = 16 << 20
F32, BF16 = jnp.float32, jnp.bfloat16
VMEM = pl.BlockSpec(memory_space=pltpu.VMEM)
SMEM = pl.BlockSpec(memory_space=pltpu.SMEM)
HBM = pl.BlockSpec(memory_space=pltpu.HBM)


def from_wide(axis, bits, array):
    step = bits * 4 if axis == "z" else bits
    return lax.ppermute(array, "wide", [(i ^ step, i) for i in range(16)])


def from_y(bits, array):
    return lax.ppermute(array, "narrow", [(i ^ (bits * 2), i) for i in range(8)])


def swap(array):
    return lax.ppermute(array, "narrow", [(i ^ 1, i) for i in range(8)])


def after(value, *earlier):
    return lax.optimization_barrier((value, *earlier))[0]


def call(kernel, name, out_shape, in_specs, operands, scratch=(), micros=0, many=True):
    return pl.pallas_call(
        kernel,
        out_shape=out_shape,
        in_specs=in_specs,
        out_specs=[VMEM] * len(out_shape) if many else VMEM,
        scratch_shapes=scratch,
        compiler_params=pltpu.CompilerParams(vmem_limit_bytes=LIMIT),
        cost_estimate=pl.CostEstimate(flops=micros * 10**9, bytes_accessed=0, transcendentals=0),
        name=name,
    )(*operands)


def load_kernel(*refs):
    count = len(refs) // 2
    copies = [pltpu.make_async_copy(refs[i], refs[count + i], refs[-1].at[i]) for i in range(count)]
    for copy in copies:
        copy.start()
    for copy in copies:
        copy.wait()


def load(*arrays):
    out = call(
        load_kernel,
        "load",
        [pltpu.VMEM(a.shape, a.dtype) for a in arrays],
        [HBM] * len(arrays),
        [pltpu.with_memory_space_constraint(a, pltpu.HBM) for a in arrays],
        scratch=[pltpu.SemaphoreType.DMA((len(arrays),))],
        micros=5,
    )
    return [pltpu.with_memory_space_constraint(a, pltpu.VMEM) for a in out]


def line_of(axis, rows):
    one, three, two = (from_wide(axis, bits, rows) for bits in (1, 3, 2))
    return [rows, one, two, three]


def assemble_kernel(first, place, own, one, two_a, two_b, three, out):
    z, x, y, c = place[0], place[1], place[2], place[3]
    block = out.shape[0] // 8
    for outer in range(4):
        for inner in range(4):
            if first == "z":
                column = (z ^ inner) * 4 + (x ^ outer)
            else:
                column = (z ^ outer) * 4 + (x ^ inner)
            columns = pl.ds(pl.multiple_of(column * LANES, LANES), LANES)
            if outer == 2:
                part, index = (two_a, inner) if inner < 2 else (two_b, inner - 2)
            else:
                part, index = (own, one, None, three)[outer], inner
            for side in range(2):
                core = 1 - c if side == 0 else c
                for j in range(4):
                    rows = pl.ds(pl.multiple_of(((y ^ j) * 2 + core) * block, block), block)
                    at = (side * 4 + j) * block
                    out[at : at + block, columns] = part[index, rows, :]


def assemble(first, place, parts, rows, depth):
    return call(
        functools.partial(assemble_kernel, first),
        "assemble_" + first,
        jax.ShapeDtypeStruct((rows, depth), BF16),
        [SMEM] + [VMEM] * len(parts),
        [place, *parts],
        many=False,
    )


def project_other_kernel(rows, gate_weight, up_weight, out):
    units = gate_weight.shape[1]
    half = rows.shape[0] // 2
    for t in range(0, units, LANES):
        weights = jnp.concatenate([gate_weight[:, t : t + LANES], up_weight[:, t : t + LANES]], axis=1)
        term = jnp.dot(rows[:half, :], weights, preferred_element_type=F32)
        out[:, t : t + LANES] = term[:, :LANES]
        out[:, units + t : units + t + LANES] = term[:, LANES:]


def project_other(rows, gate_weight, up_weight):
    half = rows.shape[0] // 2
    units = gate_weight.shape[1]
    shape = jax.ShapeDtypeStruct((half, 2 * units), F32)
    return call(
        project_other_kernel, "project_other", shape, [VMEM] * 3, [rows, gate_weight, up_weight], micros=4, many=False
    )


def project_own_kernel(rows, gate_weight, up_weight, received, own, to_one, to_three, keep_one, keep_three):
    units = gate_weight.shape[1]
    half = rows.shape[0] // 2
    quarter = half // 4
    eighth = quarter // 2
    for t in range(0, units, LANES):
        weights = jnp.concatenate([gate_weight[:, t : t + LANES], up_weight[:, t : t + LANES]], axis=1)
        term = jnp.dot(rows[half:, :], weights, preferred_element_type=F32)
        for part in range(2):
            columns = slice(t + part * units, t + part * units + LANES)
            block = term[:, part * LANES : (part + 1) * LANES] + received[:, columns]
            at = lambda j, h: block[j * quarter + h * eighth : j * quarter + (h + 1) * eighth]
            own[:, columns] = block[:quarter]
            to_one[:eighth, columns] = at(2, 0).astype(BF16)
            to_one[eighth:, columns] = at(1, 0).astype(BF16)
            to_three[:eighth, columns] = at(2, 1).astype(BF16)
            to_three[eighth:, columns] = at(3, 1).astype(BF16)
            keep_one[:, columns] = at(1, 1)
            keep_three[:, columns] = at(3, 0)


def project_own(rows, gate_weight, up_weight, received):
    half = rows.shape[0] // 2
    units = gate_weight.shape[1]
    shapes = [
        jax.ShapeDtypeStruct((count, 2 * units), dtype)
        for count, dtype in ((half // 4, F32), (half // 4, BF16), (half // 4, BF16), (half // 8, F32), (half // 8, F32))
    ]
    return call(project_own_kernel, "project_own", shapes, [VMEM] * 4, [rows, gate_weight, up_weight, received], micros=4)


def relay_kernel(keep_one, keep_three, from_one, from_three, to_one, to_three):
    half = keep_one.shape[0]
    to_one[...] = (keep_one[...] + from_three[:half, :].astype(F32)).astype(BF16)
    to_three[...] = (keep_three[...] + from_one[:half, :].astype(F32)).astype(BF16)


def relay(parts, from_one, from_three):
    keeps = parts[3:]
    shape = jax.ShapeDtypeStruct(keeps[0].shape, BF16)
    return call(relay_kernel, "relay", [shape] * 2, [VMEM] * 4, [*keeps, from_one, from_three])


def sum_of(h, own, from_one, from_three, relay_one, relay_three):
    half = relay_one.shape[0]
    direct, relayed = (from_one, relay_three) if h == 0 else (from_three, relay_one)
    return own[h * half : (h + 1) * half, :] + direct[half:, :].astype(F32) + relayed[...].astype(F32)


def hidden_kernel(*refs):
    parts, out = refs[:-1], refs[-1]
    units = out.shape[1]
    half = out.shape[0] // 2
    for h in range(2):
        total = sum_of(h, *parts)
        gate, up = total[:, :units], total[:, units:]
        out[h * half : (h + 1) * half, :] = (gate / (1.0 + jnp.exp(-gate)) * up).astype(BF16)


def hidden_of(parts):
    rows, columns = parts[0].shape
    return call(
        hidden_kernel, "hidden", jax.ShapeDtypeStruct((rows, columns // 2), BF16), [VMEM] * 5, parts, many=False
    )


def down_kernel(first, place, rows, down_weight, own, to_one, to_three, keep_one, keep_three):
    z, x = place[0], place[1]
    half = rows.shape[0] // 2
    for outer in (2, 1, 3, 0):
        for pair in (0, 2):
            weights = []
            for inner in (pair, pair + 1):
                dz, dx = (outer, inner) if first == "z" else (inner, outer)
                column = ((z ^ dz) * 4 + (x ^ dx)) * LANES
                weights.append(down_weight[:, pl.ds(pl.multiple_of(column, LANES), LANES)])
            term = jnp.dot(rows[...], jnp.concatenate(weights, axis=1), preferred_element_type=F32)
            columns = slice(pair * LANES, (pair + 2) * LANES)
            if outer == 0:
                own[:, columns] = term
            elif outer == 1:
                to_one[half:, columns] = term[:half].astype(BF16)
                keep_one[:, columns] = term[half:]
            elif outer == 2:
                to_one[:half, columns] = term[:half].astype(BF16)
                to_three[:half, columns] = term[half:].astype(BF16)
            else:
                keep_three[:, columns] = term[:half]
                to_three[half:, columns] = term[half:].astype(BF16)


def down(first, place, rows, down_weight):
    count = rows.shape[0]
    width = down_weight.shape[1] // 4
    shapes = [
        jax.ShapeDtypeStruct((n, width), dtype)
        for n, dtype in ((count, F32), (count, BF16), (count, BF16), (count // 2, F32), (count // 2, F32))
    ]
    return call(
        functools.partial(down_kernel, first),
        "down_" + first,
        shapes,
        [SMEM, VMEM, VMEM],
        [place, rows, down_weight],
        micros=4,
    )


def add_kernel(own, from_one, from_three, relay_one, relay_three, *outs):
    half = relay_one.shape[0]
    for h in range(2):
        total = sum_of(h, own, from_one, from_three, relay_one, relay_three)
        for i, out in enumerate(outs):
            out[h * half : (h + 1) * half, :] = total[:, i * LANES : (i + 1) * LANES].astype(out.dtype)


def add_line(parts):
    shapes = [jax.ShapeDtypeStruct((parts[0].shape[0], LANES), F32 if j == 0 else BF16) for j in range(4)]
    return call(add_kernel, "add_line", shapes, [VMEM] * 5, parts)


def send(axis, parts):
    return [parts[0]] + [from_wide(axis, bits, parts[bits]) for bits in (1, 2, 3)]


def last_kernel(place, *refs):
    parts, out = refs[:-1], refs[-1]
    y, c = place[2], place[3]
    rows = parts[0].shape[0]
    block = rows // 8
    for chunk in range(2):
        total = parts[4 * chunk][...]
        for k in range(1, 4):
            total = total + parts[4 * chunk + k][...].astype(F32)
        total = total.astype(BF16)
        for side in range(2):
            core = c if side == 0 else 1 - c
            for j in range(4):
                at = chunk * rows + ((y ^ j) * 2 + core) * block
                value = total[(side * 4 + j) * block : (side * 4 + j + 1) * block]
                out[pl.ds(pl.multiple_of(at, block), block), :] = value


def last(place, parts):
    shape = jax.ShapeDtypeStruct((2 * parts[0].shape[0], LANES), BF16)
    return call(last_kernel, "last", shape, [SMEM] + [VMEM] * 8, [place, *parts], many=False)


def body(tokens, gate_weight, up_weight, down_weight):
    wide, narrow = lax.axis_index("wide"), lax.axis_index("narrow")
    place = jnp.stack([wide // 4, wide % 4, narrow // 2, narrow % 2]).astype(jnp.int32)
    depth = gate_weight.shape[0]
    rows = tokens.shape[0] // 2
    both = range(2)
    tokens = after(tokens, place)
    lines = [line_of(axis, tokens[at * rows : (at + 1) * rows]) for at, axis in enumerate("zx")]
    lines[0] = after(lines[0], lines[1][1])
    stacks = [jnp.stack(line) for line in lines]
    nexts = [[from_wide(axis, bits, stack) for bits in (1, 3)] for axis, stack in zip("xz", stacks)]
    *weights, down_weight = load(*after((gate_weight, up_weight, down_weight), stacks))
    nexts[0] = after(nexts[0], down_weight)
    planes = [
        [stack, one, from_wide(axis, 1, three[:2]), from_wide(axis, 3, one[2:]), three]
        for axis, stack, (one, three) in zip("xz", stacks, nexts)
    ]
    chunks = [assemble(axis, place, plane, rows, depth) for axis, plane in zip("zx", planes)]
    others = []
    for at in both:
        others.append(project_other(after(chunks[at], *others), *weights))
    received = [swap(array) for array in others]
    parts = []
    for at in both:
        parts.append(project_own(after(chunks[at], others[1], *[p[0] for p in parts]), *weights, received[at]))
    def first_round(exchange, parts):
        return exchange(1, parts[1]), exchange(3, parts[2])

    def second_round(exchange, pair):
        return exchange(1, pair[0]), exchange(3, pair[1])

    together = lax.optimization_barrier
    half = parts[0][0].shape[0] // 2
    first = [first_round(from_y, p) for p in parts]
    second = [second_round(from_y, relay(parts[0], *after(first[0], parts[1][0]))), None]
    first[1], second[0] = together((first[1], second[0]))
    hidden = [hidden_of([parts[0][0], *first[0], *second[0]]), None]
    near = [[from_y(bits, hidden[0]) for bits in (1, 3)], None]
    second[1] = second_round(from_y, relay(parts[1], *first[1]))
    near[0], second[1] = together((near[0], second[1]))
    hidden[1] = hidden_of([parts[1][0], *first[1], *second[1]])
    near[1] = [from_y(bits, hidden[1]) for bits in (1, 3)]
    far = [second_round(from_y, (near[0][1][:half], near[0][0][half:])), None]
    near[1], far[0] = together((near[1], far[0]))
    parts = []
    for at, axis in enumerate("zx"):
        if at == 1:
            far[1] = after(second_round(from_y, (near[1][1][:half], near[1][0][half:])), parts[0][0])
        rows_here = jnp.concatenate([hidden[at], near[at][0], *far[at], near[at][1]])
        parts.append(down(axis, place, jnp.concatenate([rows_here, swap(rows_here)]), down_weight))
    along = [functools.partial(from_wide, axis) for axis in "zx"]
    first = [first_round(exchange, p) for exchange, p in zip(along, parts)]
    second[0] = second_round(along[0], relay(parts[0], *after(first[0], parts[1][0])))
    first[1], second[0] = together((first[1], second[0]))
    second[1] = second_round(along[1], relay(parts[1], *first[1]))
    final = send("x", add_line([parts[0][0], *first[0], *second[0]]))
    second[1], final = together((second[1], final))
    return last(place, final + send("z", add_line([parts[1][0], *first[1], *second[1]])))


def solution(mesh):
    return jax.shard_map(
        body,
        mesh=mesh,
        in_specs=(
            P(None, ("narrow", "wide")),
            P("narrow", "wide"),
            P("narrow", "wide"),
            P("wide", "narrow"),
        ),
        out_specs=P(None, ("narrow", "wide")),
        check_vma=False,
    )
```

profile of v0, /device:TPU:0, one launch (start us, length us, event | category | flops | bytes accessed | tf_op | source)
XLA Modules:
  0.0 161.8 jit_solution(10259254608267658894)
XLA Ops:
  0.1 1.0 fusion
  1.1 1.7 %collective-permute-start = (bf16[512,128]{1,0:T(8,128)(2,1)S(1)}, bf16[512,128]{1,0:T(8,128)(2,1)S(1)}, u32[]{:S(2)}, u32[]{:S(2)}) collective-permute-start(bf16[512,128]{1,0:T(8,128)(2,1)S(1)} %get-tuple-element.167), channel_id=1, source_target_pairs={{8,0},{0,8},{24,16},{16,24},{40,32},{32,40},{56,48},{48,56},{72,64... | collective-permute-start | bytes 393224 | tf_op jit(solution)/shard_map/ppermute | solution.py:20
  2.7 1.9 %collective-permute-start.7 = (bf16[512,128]{1,0:T(8,128)(2,1)S(1)}, bf16[512,128]{1,0:T(8,128)(2,1)S(1)}, u32[]{:S(2)}, u32[]{:S(2)}) collective-permute-start(bf16[512,128]{1,0:T(8,128)(2,1)S(1)} %get-tuple-element.86), channel_id=1, source_target_pairs={{32,0},{40,8},{48,16},{56,24},{0,32},{8,40},{16,48},{24,56},{96,64... | collective-permute-start | bytes 393224 | tf_op jit(solution)/shard_map/ppermute | solution.py:20
  4.7 3.6 %collective-permute-start.8 = (bf16[512,128]{1,0:T(8,128)(2,1)S(1)}, bf16[512,128]{1,0:T(8,128)(2,1)S(1)}, u32[]{:S(2)}, u32[]{:S(2)}) collective-permute-start(bf16[512,128]{1,0:T(8,128)(2,1)S(1)} %get-tuple-element.86), channel_id=1, source_target_pairs={{64,0},{72,8},{80,16},{88,24},{96,32},{104,40},{112,48},{120,56},{... | collective-permute-start | bytes 393224 | tf_op jit(solution)/shard_map/ppermute | solution.py:20
  8.3 2.7 %collective-permute-start.1 = (bf16[512,128]{1,0:T(8,128)(2,1)S(1)}, bf16[512,128]{1,0:T(8,128)(2,1)S(1)}, u32[]{:S(2)}, u32[]{:S(2)}) collective-permute-start(bf16[512,128]{1,0:T(8,128)(2,1)S(1)} %get-tuple-element.167), channel_id=1, source_target_pairs={{16,0},{24,8},{0,16},{8,24},{48,32},{56,40},{32,48},{40,56},{80,64... | collective-permute-start | bytes 393224 | tf_op jit(solution)/shard_map/ppermute | solution.py:20
  11.5 2.6 %collective-permute-done.8 = bf16[512,128]{1,0:T(8,128)(2,1)S(1)} collective-permute-done((bf16[512,128]{1,0:T(8,128)(2,1)S(1)}, bf16[512,128]{1,0:T(8,128)(2,1)S(1)}, u32[]{:S(2)}, u32[]{:S(2)}) %collective-permute-start.8) | collective-permute-done | bytes 131104 | tf_op jit(solution)/shard_map/ppermute | solution.py:20
  14.1 1.9 %collective-permute-done.9 = bf16[512,128]{1,0:T(8,128)(2,1)S(1)} collective-permute-done((bf16[512,128]{1,0:T(8,128)(2,1)S(1)}, bf16[512,128]{1,0:T(8,128)(2,1)S(1)}, u32[]{:S(2)}, u32[]{:S(2)}) %collective-permute-start.9) | collective-permute-done | bytes 131104 | tf_op jit(solution)/shard_map/ppermute | solution.py:20
  16.7 2.8 %collective-permute-start.11 = (bf16[4,512,128]{2,1,0:T(8,128)(2,1)S(1)}, bf16[4,512,128]{2,1,0:T(8,128)(2,1)S(1)}, u32[]{:S(2)}, u32[]{:S(2)}) collective-permute-start(bf16[4,512,128]{2,1,0:T(8,128)(2,1)S(1)} %pad_maximum_fusion.1.own), channel_id=1, source_target_pairs={{24,0},{16,8},{8,16},{0,24},{56,32},{48,40},{40,48},{32,56},{88,64... | collective-permute-start | bytes 1572872 | tf_op jit(solution)/shard_map/ppermute | solution.py:20
  19.5 1.8 %collective-permute-start.4 = (bf16[4,512,128]{2,1,0:T(8,128)(2,1)S(1)}, bf16[4,512,128]{2,1,0:T(8,128)(2,1)S(1)}, u32[]{:S(2)}, u32[]{:S(2)}) collective-permute-start(bf16[4,512,128]{2,1,0:T(8,128)(2,1)S(1)} %pad_maximum_fusion.own), channel_id=1, source_target_pairs={{96,0},{104,8},{112,16},{120,24},{64,32},{72,40},{80,48},{88,56},{... | collective-permute-start | bytes 1572872 | tf_op jit(solution)/shard_map/ppermute | solution.py:20
  21.3 6.8 %load.1 = (bf16[2048,1664]{1,0:T(8,128)(2,1)S(1)}, bf16[2048,1664]{1,0:T(8,128)(2,1)S(1)}, bf16[1664,2048]{1,0:T(8,128)(2,1)S(1)}) custom-call(bf16[2048,1664]{1,0:T(8,128)(2,1)} %refs_0_, bf16[2048,1664]{1,0:T(8,128)(2,1)} %refs_1_, bf16[1664,2048]{1,0:T(8,128)(2,1)} %refs_2_), custom_call_target="tpu_custom_call" | custom-call | flops 5000000000 | tf_op jit(solution)/shard_map/load/pallas_call | solution.py:36
  28.2 1.0 collective-permute-done.10.one
  29.1 1.5 collective-permute-done.11.three
  31.0 2.6 %collective-permute-start.13 = (bf16[2,512,128]{2,1,0:T(8,128)(2,1)S(1)}, bf16[2,512,128]{2,1,0:T(8,128)(2,1)S(1)}, u32[]{:S(2)}, u32[]{:S(2)}) collective-permute-start(bf16[2,512,128]{2,1,0:T(8,128)(2,1)S(1)} %slice.35), channel_id=1, source_target_pairs={{24,0},{16,8},{8,16},{0,24},{56,32},{48,40},{40,48},{32,56},{88,64... | collective-permute-start | bytes 786440 | tf_op jit(solution)/shard_map/ppermute | solution.py:20
  33.7 1.3 collective-permute-start.6
  35.1 2.0 %collective-permute-done.12.two_a = bf16[2,512,128]{2,1,0:T(8,128)(2,1)S(1)} collective-permute-done((bf16[2,512,128]{2,1,0:T(8,128)(2,1)S(1)}, bf16[2,512,128]{2,1,0:T(8,128)(2,1)S(1)}, u32[]{:S(2)}, u32[]{:S(2)}) %collective-permute-start.12) | collective-permute-done | bytes 262176 | tf_op jit(solution)/shard_map/ppermute | solution.py:20
  37.1 1.6 collective-permute-done.13.two_b
  38.7 1.2 assemble_z.1.rows
  39.8 3.9 %project_other.2 = f32[256,3328]{1,0:T(8,128)S(1)} custom-call(bf16[512,2048]{1,0:T(8,128)(2,1)S(1)} %assemble_z.1.rows, bf16[2048,1664]{1,0:T(8,128)(2,1)S(1)} %get-tuple-element.96.gate_weight, bf16[2048,1664]{1,0:T(8,128)(2,1)S(1)} %get-tuple-element.97.up_weight), custom_call_target="tpu_custom_call" | custom-call | flops 4000000000 | tf_op jit(solution)/shard_map/project_other/pallas_call | solution.py:36
  43.8 1.2 assemble_x.1.rows
  45.0 3.9 %project_other.3 = f32[256,3328]{1,0:T(8,128)S(1)} custom-call(bf16[512,2048]{1,0:T(8,128)(2,1)S(1)} %assemble_x.1.rows, bf16[2048,1664]{1,0:T(8,128)(2,1)S(1)} %get-tuple-element.96.gate_weight, bf16[2048,1664]{1,0:T(8,128)(2,1)S(1)} %get-tuple-element.97.up_weight), custom_call_target="tpu_custom_call" | custom-call | flops 4000000000 | tf_op jit(solution)/shard_map/project_other/pallas_call | solution.py:36
  49.8 3.9 %project_own.2 = (f32[64,3328]{1,0:T(8,128)S(1)}, bf16[64,3328]{1,0:T(8,128)(2,1)S(1)}, bf16[64,3328]{1,0:T(8,128)(2,1)S(1)}, f32[32,3328]{1,0:T(8,128)S(1)}, f32[32,3328]{1,0:T(8,128)S(1)}) custom-call(bf16[512,2048]{1,0:T(8,128)(2,1)S(1)} %assemble_z.1.rows, bf16[2048,1664]{1,0:T(8,128)(2,1)S(1)} %get-tuple-element.96.gate_weight, ...), custom_call_target="tpu_custom_call" | custom-call | flops 4000000000 | tf_op jit(solution)/shard_map/project_own/pallas_call | solution.py:36
  53.8 1.7 %collective-permute-start.18 = (bf16[64,3328]{1,0:T(8,128)(2,1)S(1)}, bf16[64,3328]{1,0:T(8,128)(2,1)S(1)}, u32[]{:S(2)}, u32[]{:S(2)}) collective-permute-start(bf16[64,3328]{1,0:T(8,128)(2,1)S(1)} %get-tuple-element.107), channel_id=1, source_target_pairs={{2,0},{3,1},{0,2},{1,3},{6,4},{7,5},{4,6},{5,7},{10,8},{11,9},{8,1... | collective-permute-start | bytes 1277960 | tf_op jit(solution)/shard_map/ppermute | solution.py:24
  55.4 2.2 %collective-permute-start.19 = (bf16[64,3328]{1,0:T(8,128)(2,1)S(1)}, bf16[64,3328]{1,0:T(8,128)(2,1)S(1)}, u32[]{:S(2)}, u32[]{:S(2)}) collective-permute-start(bf16[64,3328]{1,0:T(8,128)(2,1)S(1)} %get-tuple-element.108), channel_id=1, source_target_pairs={{6,0},{7,1},{4,2},{5,3},{2,4},{3,5},{0,6},{1,7},{14,8},{15,9},{12,... | collective-permute-start | bytes 1277960 | tf_op jit(solution)/shard_map/ppermute | solution.py:24
  57.6 3.9 %project_own.3 = (f32[64,3328]{1,0:T(8,128)S(1)}, bf16[64,3328]{1,0:T(8,128)(2,1)S(1)}, bf16[64,3328]{1,0:T(8,128)(2,1)S(1)}, f32[32,3328]{1,0:T(8,128)S(1)}, f32[32,3328]{1,0:T(8,128)S(1)}) custom-call(bf16[512,2048]{1,0:T(8,128)(2,1)S(1)} %assemble_x.1.rows, bf16[2048,1664]{1,0:T(8,128)(2,1)S(1)} %get-tuple-element.96.gate_weight, ...), custom_call_target="tpu_custom_call" | custom-call | flops 4000000000 | tf_op jit(solution)/shard_map/project_own/pallas_call | solution.py:36
  61.5 0.8 collective-permute-start.16
  62.3 0.8 collective-permute-start.17
  63.1 3.4 %collective-permute-done.18.from_one.refs_1_ = bf16[64,3328]{1,0:T(8,128)(2,1)S(1)} collective-permute-done((bf16[64,3328]{1,0:T(8,128)(2,1)S(1)}, bf16[64,3328]{1,0:T(8,128)(2,1)S(1)}, u32[]{:S(2)}, u32[]{:S(2)}) %collective-permute-start.18) | collective-permute-done | bytes 426016 | tf_op jit(solution)/shard_map/ppermute | solution.py:24
  66.5 2.8 %collective-permute-done.19.from_three.refs_2_ = bf16[64,3328]{1,0:T(8,128)(2,1)S(1)} collective-permute-done((bf16[64,3328]{1,0:T(8,128)(2,1)S(1)}, bf16[64,3328]{1,0:T(8,128)(2,1)S(1)}, u32[]{:S(2)}, u32[]{:S(2)}) %collective-permute-start.19) | collective-permute-done | bytes 426016 | tf_op jit(solution)/shard_map/ppermute | solution.py:24
  69.5 2.3 %collective-permute-start.21 = (bf16[32,3328]{1,0:T(8,128)(2,1)S(1)}, bf16[32,3328]{1,0:T(8,128)(2,1)S(1)}, u32[]{:S(2)}, u32[]{:S(2)}) collective-permute-start(bf16[32,3328]{1,0:T(8,128)(2,1)S(1)} %get-tuple-element.112), channel_id=1, source_target_pairs={{6,0},{7,1},{4,2},{5,3},{2,4},{3,5},{0,6},{1,7},{14,8},{15,9},{12,... | collective-permute-start | bytes 638984 | tf_op jit(solution)/shard_map/ppermute | solution.py:24
  71.8 3.8 %collective-permute-done.16.from_one.refs_1_ = bf16[64,3328]{1,0:T(8,128)(2,1)S(1)} collective-permute-done((bf16[64,3328]{1,0:T(8,128)(2,1)S(1)}, bf16[64,3328]{1,0:T(8,128)(2,1)S(1)}, u32[]{:S(2)}, u32[]{:S(2)}) %collective-permute-start.16) | collective-permute-done | bytes 426016 | tf_op jit(solution)/shard_map/ppermute | solution.py:24
  75.6 2.8 %collective-permute-done.17.from_three.refs_2_ = bf16[64,3328]{1,0:T(8,128)(2,1)S(1)} collective-permute-done((bf16[64,3328]{1,0:T(8,128)(2,1)S(1)}, bf16[64,3328]{1,0:T(8,128)(2,1)S(1)}, u32[]{:S(2)}, u32[]{:S(2)}) %collective-permute-start.17) | collective-permute-done | bytes 426016 | tf_op jit(solution)/shard_map/ppermute | solution.py:24
  78.5 0.9 collective-permute-done.20.refs_3_
  79.4 2.5 %collective-permute-done.21.refs_4_ = bf16[32,3328]{1,0:T(8,128)(2,1)S(1)} collective-permute-done((bf16[32,3328]{1,0:T(8,128)(2,1)S(1)}, bf16[32,3328]{1,0:T(8,128)(2,1)S(1)}, u32[]{:S(2)}, u32[]{:S(2)}) %collective-permute-start.21) | collective-permute-done | bytes 213024 | tf_op jit(solution)/shard_map/ppermute | solution.py:24
  82.2 2.3 %collective-permute-start.23 = (bf16[64,1664]{1,0:T(8,128)(2,1)S(1)}, bf16[64,1664]{1,0:T(8,128)(2,1)S(1)}, u32[]{:S(2)}, u32[]{:S(2)}) collective-permute-start(bf16[64,1664]{1,0:T(8,128)(2,1)S(1)} %hidden.2), channel_id=1, source_target_pairs={{6,0},{7,1},{4,2},{5,3},{2,4},{3,5},{0,6},{1,7},{14,8},{15,9},{12,... | collective-permute-start | bytes 638984 | tf_op jit(solution)/shard_map/ppermute | solution.py:24
  84.6 1.4 collective-permute-start.24
  86.0 1.1 collective-permute-start.25
  87.1 5.9 %collective-permute-done.24.refs_3_ = bf16[32,3328]{1,0:T(8,128)(2,1)S(1)} collective-permute-done((bf16[32,3328]{1,0:T(8,128)(2,1)S(1)}, bf16[32,3328]{1,0:T(8,128)(2,1)S(1)}, u32[]{:S(2)}, u32[]{:S(2)}) %collective-permute-start.24) | collective-permute-done | bytes 213024 | tf_op jit(solution)/shard_map/ppermute | solution.py:24
  92.9 1.3 collective-permute-done.25.refs_4_
  95.0 2.2 %collective-permute-start.27 = (bf16[64,1664]{1,0:T(8,128)(2,1)S(1)}, bf16[64,1664]{1,0:T(8,128)(2,1)S(1)}, u32[]{:S(2)}, u32[]{:S(2)}) collective-permute-start(bf16[64,1664]{1,0:T(8,128)(2,1)S(1)} %hidden.3), channel_id=1, source_target_pairs={{6,0},{7,1},{4,2},{5,3},{2,4},{3,5},{0,6},{1,7},{14,8},{15,9},{12,... | collective-permute-start | bytes 638984 | tf_op jit(solution)/shard_map/ppermute | solution.py:24
  97.2 1.1 collective-permute-start.28
  98.3 1.1 collective-permute-start.29
  99.4 2.9 %collective-permute-done.28 = bf16[32,1664]{1,0:T(8,128)(2,1)S(1)} collective-permute-done((bf16[32,1664]{1,0:T(8,128)(2,1)S(1)}, bf16[32,1664]{1,0:T(8,128)(2,1)S(1)}, u32[]{:S(2)}, u32[]{:S(2)}) %collective-permute-start.28) | collective-permute-done | bytes 106528 | tf_op jit(solution)/shard_map/ppermute | solution.py:24
  102.4 1.9 %collective-permute-done.29 = bf16[32,1664]{1,0:T(8,128)(2,1)S(1)} collective-permute-done((bf16[32,1664]{1,0:T(8,128)(2,1)S(1)}, bf16[32,1664]{1,0:T(8,128)(2,1)S(1)}, u32[]{:S(2)}, u32[]{:S(2)}) %collective-permute-start.29) | collective-permute-done | bytes 106528 | tf_op jit(solution)/shard_map/ppermute | solution.py:24
  104.6 2.0 %collective-permute-start.31 = (bf16[32,1664]{1,0:T(8,128)(2,1)S(1)}, bf16[32,1664]{1,0:T(8,128)(2,1)S(1)}, u32[]{:S(2)}, u32[]{:S(2)}) collective-permute-start(bf16[32,1664]{1,0:T(8,128)(2,1)S(1)} %slice.39), channel_id=1, source_target_pairs={{6,0},{7,1},{4,2},{5,3},{2,4},{3,5},{0,6},{1,7},{14,8},{15,9},{12,... | collective-permute-start | bytes 319496 | tf_op jit(solution)/shard_map/ppermute | solution.py:24
  106.9 4.7 %down_z.1 = (f32[512,512]{1,0:T(8,128)S(1)}, bf16[512,512]{1,0:T(8,128)(2,1)S(1)}, bf16[512,512]{1,0:T(8,128)(2,1)S(1)}, f32[256,512]{1,0:T(8,128)S(1)}, f32[256,512]{1,0:T(8,128)S(1)}) custom-call(s32[4]{0:T(128)S(1)} %pad_add_fusion.place, bf16[512,1664]{1,0:T(8,128)(2,1)S(1)} %constant_dynamic-update-slice_fusion.5.rows, ...), custom_call_target="tpu_custom_call" | custom-call | flops 4000000000 | tf_op jit(solution)/shard_map/down_z/pallas_call | solution.py:36
  111.9 2.0 %collective-permute-start.37 = (bf16[512,512]{1,0:T(8,128)(2,1)S(1)}, bf16[512,512]{1,0:T(8,128)(2,1)S(1)}, u32[]{:S(2)}, u32[]{:S(2)}) collective-permute-start(bf16[512,512]{1,0:T(8,128)(2,1)S(1)} %get-tuple-element.139), channel_id=1, source_target_pairs={{96,0},{104,8},{112,16},{120,24},{64,32},{72,40},{80,48},{88,56},{... | collective-permute-start | bytes 1572872 | tf_op jit(solution)/shard_map/ppermute | solution.py:20
  114.3 4.7 %down_x.1 = (f32[512,512]{1,0:T(8,128)S(1)}, bf16[512,512]{1,0:T(8,128)(2,1)S(1)}, bf16[512,512]{1,0:T(8,128)(2,1)S(1)}, f32[256,512]{1,0:T(8,128)S(1)}, f32[256,512]{1,0:T(8,128)S(1)}) custom-call(s32[4]{0:T(128)S(1)} %pad_add_fusion.place, bf16[512,1664]{1,0:T(8,128)(2,1)S(1)} %constant_dynamic-update-slice_fusion.16.rows, ...), custom_call_target="tpu_custom_call" | custom-call | flops 4000000000 | tf_op jit(solution)/shard_map/down_x/pallas_call | solution.py:36
  119.7 2.6 %collective-permute-start.35 = (bf16[512,512]{1,0:T(8,128)(2,1)S(1)}, bf16[512,512]{1,0:T(8,128)(2,1)S(1)}, u32[]{:S(2)}, u32[]{:S(2)}) collective-permute-start(bf16[512,512]{1,0:T(8,128)(2,1)S(1)} %get-tuple-element.135), channel_id=1, source_target_pairs={{24,0},{16,8},{8,16},{0,24},{56,32},{48,40},{40,48},{32,56},{88,64... | collective-permute-start | bytes 1572872 | tf_op jit(solution)/shard_map/ppermute | solution.py:20
  122.4 3.8 %collective-permute-done.36.from_one = bf16[512,512]{1,0:T(8,128)(2,1)S(1)} collective-permute-done((bf16[512,512]{1,0:T(8,128)(2,1)S(1)}, bf16[512,512]{1,0:T(8,128)(2,1)S(1)}, u32[]{:S(2)}, u32[]{:S(2)}) %collective-permute-start.36) | collective-permute-done | bytes 524320 | tf_op jit(solution)/shard_map/ppermute | solution.py:20
  126.1 1.2 collective-permute-done.37.from_three
  128.1 2.0 %collective-permute-start.39 = (bf16[256,512]{1,0:T(8,128)(2,1)S(1)}, bf16[256,512]{1,0:T(8,128)(2,1)S(1)}, u32[]{:S(2)}, u32[]{:S(2)}) collective-permute-start(bf16[256,512]{1,0:T(8,128)(2,1)S(1)} %get-tuple-element.144), channel_id=1, source_target_pairs={{96,0},{104,8},{112,16},{120,24},{64,32},{72,40},{80,48},{88,56},{... | collective-permute-start | bytes 786440 | tf_op jit(solution)/shard_map/ppermute | solution.py:20
  130.0 5.2 %collective-permute-done.38.relay_one = bf16[256,512]{1,0:T(8,128)(2,1)S(1)} collective-permute-done((bf16[256,512]{1,0:T(8,128)(2,1)S(1)}, bf16[256,512]{1,0:T(8,128)(2,1)S(1)}, u32[]{:S(2)}, u32[]{:S(2)}) %collective-permute-start.38) | collective-permute-done | bytes 262176 | tf_op jit(solution)/shard_map/ppermute | solution.py:20
  135.3 1.3 collective-permute-done.39.relay_three
  136.7 0.8 collective-permute-start.40
  137.4 2.6 %collective-permute-start.41 = (bf16[256,512]{1,0:T(8,128)(2,1)S(1)}, bf16[256,512]{1,0:T(8,128)(2,1)S(1)}, u32[]{:S(2)}, u32[]{:S(2)}) collective-permute-start(bf16[256,512]{1,0:T(8,128)(2,1)S(1)} %get-tuple-element.148), channel_id=1, source_target_pairs={{24,0},{16,8},{8,16},{0,24},{56,32},{48,40},{40,48},{32,56},{88,64... | collective-permute-start | bytes 786440 | tf_op jit(solution)/shard_map/ppermute | solution.py:20
  140.9 1.5 collective-permute-start.43
  142.4 2.6 %collective-permute-start.44 = (bf16[512,128]{1,0:T(8,128)(2,1)S(1)}, bf16[512,128]{1,0:T(8,128)(2,1)S(1)}, u32[]{:S(2)}, u32[]{:S(2)}) collective-permute-start(bf16[512,128]{1,0:T(8,128)(2,1)S(1)} %get-tuple-element.154), channel_id=1, source_target_pairs={{24,0},{16,8},{8,16},{0,24},{56,32},{48,40},{40,48},{32,56},{88,64... | collective-permute-start | bytes 393224 | tf_op jit(solution)/shard_map/ppermute | solution.py:20
  145.0 2.3 %collective-permute-done.42.refs_1_ = bf16[512,128]{1,0:T(8,128)(2,1)S(1)} collective-permute-done((bf16[512,128]{1,0:T(8,128)(2,1)S(1)}, bf16[512,128]{1,0:T(8,128)(2,1)S(1)}, u32[]{:S(2)}, u32[]{:S(2)}) %collective-permute-start.42) | collective-permute-done | bytes 131104 | tf_op jit(solution)/shard_map/ppermute | solution.py:20
  147.4 3.3 %collective-permute-done.43.refs_2_ = bf16[512,128]{1,0:T(8,128)(2,1)S(1)} collective-permute-done((bf16[512,128]{1,0:T(8,128)(2,1)S(1)}, bf16[512,128]{1,0:T(8,128)(2,1)S(1)}, u32[]{:S(2)}, u32[]{:S(2)}) %collective-permute-start.43) | collective-permute-done | bytes 131104 | tf_op jit(solution)/shard_map/ppermute | solution.py:20
  151.6 2.6 %collective-permute-start.46 = (bf16[512,128]{1,0:T(8,128)(2,1)S(1)}, bf16[512,128]{1,0:T(8,128)(2,1)S(1)}, u32[]{:S(2)}, u32[]{:S(2)}) collective-permute-start(bf16[512,128]{1,0:T(8,128)(2,1)S(1)} %get-tuple-element.163), channel_id=1, source_target_pairs={{64,0},{72,8},{80,16},{88,24},{96,32},{104,40},{112,48},{120,56},{... | collective-permute-start | bytes 393224 | tf_op jit(solution)/shard_map/ppermute | solution.py:20
  154.2 1.5 collective-permute-start.47
  156.0 2.6 %collective-permute-done.46.refs_6_ = bf16[512,128]{1,0:T(8,128)(2,1)S(1)} collective-permute-done((bf16[512,128]{1,0:T(8,128)(2,1)S(1)}, bf16[512,128]{1,0:T(8,128)(2,1)S(1)}, u32[]{:S(2)}, u32[]{:S(2)}) %collective-permute-start.46) | collective-permute-done | bytes 131104 | tf_op jit(solution)/shard_map/ppermute | solution.py:20
  158.6 1.8 %collective-permute-done.47.refs_7_ = bf16[512,128]{1,0:T(8,128)(2,1)S(1)} collective-permute-done((bf16[512,128]{1,0:T(8,128)(2,1)S(1)}, bf16[512,128]{1,0:T(8,128)(2,1)S(1)}, u32[]{:S(2)}, u32[]{:S(2)}) %collective-permute-start.47) | collective-permute-done | bytes 131104 | tf_op jit(solution)/shard_map/ppermute | solution.py:20
  160.4 1.4 last.1
  (74 shorter events, 9.2 us)
Async XLA Ops:
  1.1 9.9 %collective-permute-start = (bf16[512,128]{1,0:T(8,128)(2,1)S(1)}, bf16[512,128]{1,0:T(8,128)(2,1)S(1)}, u32[]{:S(2)}, u32[]{:S(2)}) collective-permute-start(bf16[512,128]{1,0:T(8,128)(2,1)S(1)} %get-tuple-element.167), channel_id=1, source_target_pairs={{8,0},{0,8},{24,16},{16,24},{40,32},{32,40},{56,48},{48,56},{72,64... | collective-permute-start | bytes 393224 | tf_op jit(solution)/shard_map/ppermute | solution.py:20
  2.7 8.7 %collective-permute-start.7 = (bf16[512,128]{1,0:T(8,128)(2,1)S(1)}, bf16[512,128]{1,0:T(8,128)(2,1)S(1)}, u32[]{:S(2)}, u32[]{:S(2)}) collective-permute-start(bf16[512,128]{1,0:T(8,128)(2,1)S(1)} %get-tuple-element.86), channel_id=1, source_target_pairs={{32,0},{40,8},{48,16},{56,24},{0,32},{8,40},{16,48},{24,56},{96,64... | collective-permute-start | bytes 393224 | tf_op jit(solution)/shard_map/ppermute | solution.py:20
  4.7 9.4 %collective-permute-start.8 = (bf16[512,128]{1,0:T(8,128)(2,1)S(1)}, bf16[512,128]{1,0:T(8,128)(2,1)S(1)}, u32[]{:S(2)}, u32[]{:S(2)}) collective-permute-start(bf16[512,128]{1,0:T(8,128)(2,1)S(1)} %get-tuple-element.86), channel_id=1, source_target_pairs={{64,0},{72,8},{80,16},{88,24},{96,32},{104,40},{112,48},{120,56},{... | collective-permute-start | bytes 393224 | tf_op jit(solution)/shard_map/ppermute | solution.py:20
  8.2 7.7 %collective-permute-start.9 = (bf16[512,128]{1,0:T(8,128)(2,1)S(1)}, bf16[512,128]{1,0:T(8,128)(2,1)S(1)}, u32[]{:S(2)}, u32[]{:S(2)}) collective-permute-start(bf16[512,128]{1,0:T(8,128)(2,1)S(1)} %get-tuple-element.86), channel_id=1, source_target_pairs={{96,0},{104,8},{112,16},{120,24},{64,32},{72,40},{80,48},{88,56},{... | collective-permute-start | bytes 393224 | tf_op jit(solution)/shard_map/ppermute | solution.py:20
  8.3 11.2 %collective-permute-start.1 = (bf16[512,128]{1,0:T(8,128)(2,1)S(1)}, bf16[512,128]{1,0:T(8,128)(2,1)S(1)}, u32[]{:S(2)}, u32[]{:S(2)}) collective-permute-start(bf16[512,128]{1,0:T(8,128)(2,1)S(1)} %get-tuple-element.167), channel_id=1, source_target_pairs={{16,0},{24,8},{0,16},{8,24},{48,32},{56,40},{32,48},{40,56},{80,64... | collective-permute-start | bytes 393224 | tf_op jit(solution)/shard_map/ppermute | solution.py:20
  11.0 8.5 %collective-permute-start.2 = (bf16[512,128]{1,0:T(8,128)(2,1)S(1)}, bf16[512,128]{1,0:T(8,128)(2,1)S(1)}, u32[]{:S(2)}, u32[]{:S(2)}) collective-permute-start(bf16[512,128]{1,0:T(8,128)(2,1)S(1)} %get-tuple-element.167), channel_id=1, source_target_pairs={{24,0},{16,8},{8,16},{0,24},{56,32},{48,40},{40,48},{32,56},{88,64... | collective-permute-start | bytes 393224 | tf_op jit(solution)/shard_map/ppermute | solution.py:20
  16.1 13.1 %collective-permute-start.10 = (bf16[4,512,128]{2,1,0:T(8,128)(2,1)S(1)}, bf16[4,512,128]{2,1,0:T(8,128)(2,1)S(1)}, u32[]{:S(2)}, u32[]{:S(2)}) collective-permute-start(bf16[4,512,128]{2,1,0:T(8,128)(2,1)S(1)} %pad_maximum_fusion.1.own), channel_id=1, source_target_pairs={{8,0},{0,8},{24,16},{16,24},{40,32},{32,40},{56,48},{48,56},{72,64... | collective-permute-start | bytes 1572872 | tf_op jit(solution)/shard_map/ppermute | solution.py:20
  16.7 13.9 %collective-permute-start.11 = (bf16[4,512,128]{2,1,0:T(8,128)(2,1)S(1)}, bf16[4,512,128]{2,1,0:T(8,128)(2,1)S(1)}, u32[]{:S(2)}, u32[]{:S(2)}) collective-permute-start(bf16[4,512,128]{2,1,0:T(8,128)(2,1)S(1)} %pad_maximum_fusion.1.own), channel_id=1, source_target_pairs={{24,0},{16,8},{8,16},{0,24},{56,32},{48,40},{40,48},{32,56},{88,64... | collective-permute-start | bytes 1572872 | tf_op jit(solution)/shard_map/ppermute | solution.py:20
  19.5 14.1 %collective-permute-start.4 = (bf16[4,512,128]{2,1,0:T(8,128)(2,1)S(1)}, bf16[4,512,128]{2,1,0:T(8,128)(2,1)S(1)}, u32[]{:S(2)}, u32[]{:S(2)}) collective-permute-start(bf16[4,512,128]{2,1,0:T(8,128)(2,1)S(1)} %pad_maximum_fusion.own), channel_id=1, source_target_pairs={{96,0},{104,8},{112,16},{120,24},{64,32},{72,40},{80,48},{88,56},{... | collective-permute-start | bytes 1572872 | tf_op jit(solution)/shard_map/ppermute | solution.py:20
  21.3 12.4 %collective-permute-start.3 = (bf16[4,512,128]{2,1,0:T(8,128)(2,1)S(1)}, bf16[4,512,128]{2,1,0:T(8,128)(2,1)S(1)}, u32[]{:S(2)}, u32[]{:S(2)}) collective-permute-start(bf16[4,512,128]{2,1,0:T(8,128)(2,1)S(1)} %pad_maximum_fusion.own), channel_id=1, source_target_pairs={{32,0},{40,8},{48,16},{56,24},{0,32},{8,40},{16,48},{24,56},{96,64... | collective-permute-start | bytes 1572872 | tf_op jit(solution)/shard_map/ppermute | solution.py:20
  30.6 6.5 %collective-permute-start.12 = (bf16[2,512,128]{2,1,0:T(8,128)(2,1)S(1)}, bf16[2,512,128]{2,1,0:T(8,128)(2,1)S(1)}, u32[]{:S(2)}, u32[]{:S(2)}) collective-permute-start(bf16[2,512,128]{2,1,0:T(8,128)(2,1)S(1)} %slice.34), channel_id=1, source_target_pairs={{8,0},{0,8},{24,16},{16,24},{40,32},{32,40},{56,48},{48,56},{72,64... | collective-permute-start | bytes 786440 | tf_op jit(solution)/shard_map/ppermute | solution.py:20
  31.0 7.7 %collective-permute-start.13 = (bf16[2,512,128]{2,1,0:T(8,128)(2,1)S(1)}, bf16[2,512,128]{2,1,0:T(8,128)(2,1)S(1)}, u32[]{:S(2)}, u32[]{:S(2)}) collective-permute-start(bf16[2,512,128]{2,1,0:T(8,128)(2,1)S(1)} %slice.35), channel_id=1, source_target_pairs={{24,0},{16,8},{8,16},{0,24},{56,32},{48,40},{40,48},{32,56},{88,64... | collective-permute-start | bytes 786440 | tf_op jit(solution)/shard_map/ppermute | solution.py:20
  33.6 10.2 %collective-permute-start.5 = (bf16[2,512,128]{2,1,0:T(8,128)(2,1)S(1)}, bf16[2,512,128]{2,1,0:T(8,128)(2,1)S(1)}, u32[]{:S(2)}, u32[]{:S(2)}) collective-permute-start(bf16[2,512,128]{2,1,0:T(8,128)(2,1)S(1)} %slice.40), channel_id=1, source_target_pairs={{32,0},{40,8},{48,16},{56,24},{0,32},{8,40},{16,48},{24,56},{96,64... | collective-permute-start | bytes 786440 | tf_op jit(solution)/shard_map/ppermute | solution.py:20
  33.7 10.1 %collective-permute-start.6 = (bf16[2,512,128]{2,1,0:T(8,128)(2,1)S(1)}, bf16[2,512,128]{2,1,0:T(8,128)(2,1)S(1)}, u32[]{:S(2)}, u32[]{:S(2)}) collective-permute-start(bf16[2,512,128]{2,1,0:T(8,128)(2,1)S(1)} %slice.41), channel_id=1, source_target_pairs={{96,0},{104,8},{112,16},{120,24},{64,32},{72,40},{80,48},{88,56},{... | collective-permute-start | bytes 786440 | tf_op jit(solution)/shard_map/ppermute | solution.py:20
  43.7 6.1 %collective-permute-start.14 = (f32[256,3328]{1,0:T(8,128)S(1)}, f32[256,3328]{1,0:T(8,128)S(1)}, u32[]{:S(2)}, u32[]{:S(2)}) collective-permute-start(f32[256,3328]{1,0:T(8,128)S(1)} %project_other.2), channel_id=1, source_target_pairs={{1,0},{0,1},{3,2},{2,3},{5,4},{4,5},{7,6},{6,7},{9,8},{8,9},{11,10... | collective-permute-start | bytes 10223624 | tf_op jit(solution)/shard_map/ppermute | solution.py:28
  48.9 8.7 %collective-permute-start.15 = (f32[256,3328]{1,0:T(8,128)S(1)}, f32[256,3328]{1,0:T(8,128)S(1)}, u32[]{:S(2)}, u32[]{:S(2)}) collective-permute-start(f32[256,3328]{1,0:T(8,128)S(1)} %project_other.3), channel_id=1, source_target_pairs={{1,0},{0,1},{3,2},{2,3},{5,4},{4,5},{7,6},{6,7},{9,8},{8,9},{11,10... | collective-permute-start | bytes 10223624 | tf_op jit(solution)/shard_map/ppermute | solution.py:28
  53.8 12.7 %collective-permute-start.18 = (bf16[64,3328]{1,0:T(8,128)(2,1)S(1)}, bf16[64,3328]{1,0:T(8,128)(2,1)S(1)}, u32[]{:S(2)}, u32[]{:S(2)}) collective-permute-start(bf16[64,3328]{1,0:T(8,128)(2,1)S(1)} %get-tuple-element.107), channel_id=1, source_target_pairs={{2,0},{3,1},{0,2},{1,3},{6,4},{7,5},{4,6},{5,7},{10,8},{11,9},{8,1... | collective-permute-start | bytes 1277960 | tf_op jit(solution)/shard_map/ppermute | solution.py:24
  55.4 13.9 %collective-permute-start.19 = (bf16[64,3328]{1,0:T(8,128)(2,1)S(1)}, bf16[64,3328]{1,0:T(8,128)(2,1)S(1)}, u32[]{:S(2)}, u32[]{:S(2)}) collective-permute-start(bf16[64,3328]{1,0:T(8,128)(2,1)S(1)} %get-tuple-element.108), channel_id=1, source_target_pairs={{6,0},{7,1},{4,2},{5,3},{2,4},{3,5},{0,6},{1,7},{14,8},{15,9},{12,... | collective-permute-start | bytes 1277960 | tf_op jit(solution)/shard_map/ppermute | solution.py:24
  61.5 14.1 %collective-permute-start.16 = (bf16[64,3328]{1,0:T(8,128)(2,1)S(1)}, bf16[64,3328]{1,0:T(8,128)(2,1)S(1)}, u32[]{:S(2)}, u32[]{:S(2)}) collective-permute-start(bf16[64,3328]{1,0:T(8,128)(2,1)S(1)} %get-tuple-element.103), channel_id=1, source_target_pairs={{2,0},{3,1},{0,2},{1,3},{6,4},{7,5},{4,6},{5,7},{10,8},{11,9},{8,1... | collective-permute-start | bytes 1277960 | tf_op jit(solution)/shard_map/ppermute | solution.py:24
  62.3 16.2 %collective-permute-start.17 = (bf16[64,3328]{1,0:T(8,128)(2,1)S(1)}, bf16[64,3328]{1,0:T(8,128)(2,1)S(1)}, u32[]{:S(2)}, u32[]{:S(2)}) collective-permute-start(bf16[64,3328]{1,0:T(8,128)(2,1)S(1)} %get-tuple-element.104), channel_id=1, source_target_pairs={{6,0},{7,1},{4,2},{5,3},{2,4},{3,5},{0,6},{1,7},{14,8},{15,9},{12,... | collective-permute-start | bytes 1277960 | tf_op jit(solution)/shard_map/ppermute | solution.py:24
  69.4 10.0 %collective-permute-start.20 = (bf16[32,3328]{1,0:T(8,128)(2,1)S(1)}, bf16[32,3328]{1,0:T(8,128)(2,1)S(1)}, u32[]{:S(2)}, u32[]{:S(2)}) collective-permute-start(bf16[32,3328]{1,0:T(8,128)(2,1)S(1)} %get-tuple-element.111), channel_id=1, source_target_pairs={{2,0},{3,1},{0,2},{1,3},{6,4},{7,5},{4,6},{5,7},{10,8},{11,9},{8,1... | collective-permute-start | bytes 638984 | tf_op jit(solution)/shard_map/ppermute | solution.py:24
  69.5 12.4 %collective-permute-start.21 = (bf16[32,3328]{1,0:T(8,128)(2,1)S(1)}, bf16[32,3328]{1,0:T(8,128)(2,1)S(1)}, u32[]{:S(2)}, u32[]{:S(2)}) collective-permute-start(bf16[32,3328]{1,0:T(8,128)(2,1)S(1)} %get-tuple-element.112), channel_id=1, source_target_pairs={{6,0},{7,1},{4,2},{5,3},{2,4},{3,5},{0,6},{1,7},{14,8},{15,9},{12,... | collective-permute-start | bytes 638984 | tf_op jit(solution)/shard_map/ppermute | solution.py:24
  82.1 12.1 %collective-permute-start.22 = (bf16[64,1664]{1,0:T(8,128)(2,1)S(1)}, bf16[64,1664]{1,0:T(8,128)(2,1)S(1)}, u32[]{:S(2)}, u32[]{:S(2)}) collective-permute-start(bf16[64,1664]{1,0:T(8,128)(2,1)S(1)} %hidden.2), channel_id=1, source_target_pairs={{2,0},{3,1},{0,2},{1,3},{6,4},{7,5},{4,6},{5,7},{10,8},{11,9},{8,1... | collective-permute-start | bytes 638984 | tf_op jit(solution)/shard_map/ppermute | solution.py:24
  82.2 12.0 %collective-permute-start.23 = (bf16[64,1664]{1,0:T(8,128)(2,1)S(1)}, bf16[64,1664]{1,0:T(8,128)(2,1)S(1)}, u32[]{:S(2)}, u32[]{:S(2)}) collective-permute-start(bf16[64,1664]{1,0:T(8,128)(2,1)S(1)} %hidden.2), channel_id=1, source_target_pairs={{6,0},{7,1},{4,2},{5,3},{2,4},{3,5},{0,6},{1,7},{14,8},{15,9},{12,... | collective-permute-start | bytes 638984 | tf_op jit(solution)/shard_map/ppermute | solution.py:24
  84.6 8.4 %collective-permute-start.24 = (bf16[32,3328]{1,0:T(8,128)(2,1)S(1)}, bf16[32,3328]{1,0:T(8,128)(2,1)S(1)}, u32[]{:S(2)}, u32[]{:S(2)}) collective-permute-start(bf16[32,3328]{1,0:T(8,128)(2,1)S(1)} %get-tuple-element.119), channel_id=1, source_target_pairs={{2,0},{3,1},{0,2},{1,3},{6,4},{7,5},{4,6},{5,7},{10,8},{11,9},{8,1... | collective-permute-start | bytes 638984 | tf_op jit(solution)/shard_map/ppermute | solution.py:24
  86.0 8.3 %collective-permute-start.25 = (bf16[32,3328]{1,0:T(8,128)(2,1)S(1)}, bf16[32,3328]{1,0:T(8,128)(2,1)S(1)}, u32[]{:S(2)}, u32[]{:S(2)}) collective-permute-start(bf16[32,3328]{1,0:T(8,128)(2,1)S(1)} %get-tuple-element.120), channel_id=1, source_target_pairs={{6,0},{7,1},{4,2},{5,3},{2,4},{3,5},{0,6},{1,7},{14,8},{15,9},{12,... | collective-permute-start | bytes 638984 | tf_op jit(solution)/shard_map/ppermute | solution.py:24
  94.5 9.8 %collective-permute-start.26 = (bf16[64,1664]{1,0:T(8,128)(2,1)S(1)}, bf16[64,1664]{1,0:T(8,128)(2,1)S(1)}, u32[]{:S(2)}, u32[]{:S(2)}) collective-permute-start(bf16[64,1664]{1,0:T(8,128)(2,1)S(1)} %hidden.3), channel_id=1, source_target_pairs={{2,0},{3,1},{0,2},{1,3},{6,4},{7,5},{4,6},{5,7},{10,8},{11,9},{8,1... | collective-permute-start | bytes 638984 | tf_op jit(solution)/shard_map/ppermute | solution.py:24
  95.0 9.3 %collective-permute-start.27 = (bf16[64,1664]{1,0:T(8,128)(2,1)S(1)}, bf16[64,1664]{1,0:T(8,128)(2,1)S(1)}, u32[]{:S(2)}, u32[]{:S(2)}) collective-permute-start(bf16[64,1664]{1,0:T(8,128)(2,1)S(1)} %hidden.3), channel_id=1, source_target_pairs={{6,0},{7,1},{4,2},{5,3},{2,4},{3,5},{0,6},{1,7},{14,8},{15,9},{12,... | collective-permute-start | bytes 638984 | tf_op jit(solution)/shard_map/ppermute | solution.py:24
  97.2 5.2 %collective-permute-start.28 = (bf16[32,1664]{1,0:T(8,128)(2,1)S(1)}, bf16[32,1664]{1,0:T(8,128)(2,1)S(1)}, u32[]{:S(2)}, u32[]{:S(2)}) collective-permute-start(bf16[32,1664]{1,0:T(8,128)(2,1)S(1)} %slice.36), channel_id=1, source_target_pairs={{2,0},{3,1},{0,2},{1,3},{6,4},{7,5},{4,6},{5,7},{10,8},{11,9},{8,1... | collective-permute-start | bytes 319496 | tf_op jit(solution)/shard_map/ppermute | solution.py:24
  98.3 6.0 %collective-permute-start.29 = (bf16[32,1664]{1,0:T(8,128)(2,1)S(1)}, bf16[32,1664]{1,0:T(8,128)(2,1)S(1)}, u32[]{:S(2)}, u32[]{:S(2)}) collective-permute-start(bf16[32,1664]{1,0:T(8,128)(2,1)S(1)} %slice.37), channel_id=1, source_target_pairs={{6,0},{7,1},{4,2},{5,3},{2,4},{3,5},{0,6},{1,7},{14,8},{15,9},{12,... | collective-permute-start | bytes 319496 | tf_op jit(solution)/shard_map/ppermute | solution.py:24
  104.4 2.5 %collective-permute-start.32 = (bf16[256,1664]{1,0:T(8,128)(2,1)S(1)}, bf16[256,1664]{1,0:T(8,128)(2,1)S(1)}, u32[]{:S(2)}, u32[]{:S(2)}) collective-permute-start(bf16[256,1664]{1,0:T(8,128)(2,1)S(1)} %get-tuple-element.174), channel_id=1, source_target_pairs={{1,0},{0,1},{3,2},{2,3},{5,4},{4,5},{7,6},{6,7},{9,8},{8,9},{11,10... | collective-permute-start | bytes 2555912 | tf_op jit(solution)/shard_map/ppermute | solution.py:28
  104.5 7.1 %collective-permute-start.30 = (bf16[32,1664]{1,0:T(8,128)(2,1)S(1)}, bf16[32,1664]{1,0:T(8,128)(2,1)S(1)}, u32[]{:S(2)}, u32[]{:S(2)}) collective-permute-start(bf16[32,1664]{1,0:T(8,128)(2,1)S(1)} %slice.38), channel_id=1, source_target_pairs={{2,0},{3,1},{0,2},{1,3},{6,4},{7,5},{4,6},{5,7},{10,8},{11,9},{8,1... | collective-permute-start | bytes 319496 | tf_op jit(solution)/shard_map/ppermute | solution.py:24
  104.6 7.0 %collective-permute-start.31 = (bf16[32,1664]{1,0:T(8,128)(2,1)S(1)}, bf16[32,1664]{1,0:T(8,128)(2,1)S(1)}, u32[]{:S(2)}, u32[]{:S(2)}) collective-permute-start(bf16[32,1664]{1,0:T(8,128)(2,1)S(1)} %slice.39), channel_id=1, source_target_pairs={{6,0},{7,1},{4,2},{5,3},{2,4},{3,5},{0,6},{1,7},{14,8},{15,9},{12,... | collective-permute-start | bytes 319496 | tf_op jit(solution)/shard_map/ppermute | solution.py:24
  111.7 2.5 %collective-permute-start.33 = (bf16[256,1664]{1,0:T(8,128)(2,1)S(1)}, bf16[256,1664]{1,0:T(8,128)(2,1)S(1)}, u32[]{:S(2)}, u32[]{:S(2)}) collective-permute-start(bf16[256,1664]{1,0:T(8,128)(2,1)S(1)} %get-tuple-element.168), channel_id=1, source_target_pairs={{1,0},{0,1},{3,2},{2,3},{5,4},{4,5},{7,6},{6,7},{9,8},{8,9},{11,10... | collective-permute-start | bytes 2555912 | tf_op jit(solution)/shard_map/ppermute | solution.py:28
  111.9 14.2 %collective-permute-start.36 = (bf16[512,512]{1,0:T(8,128)(2,1)S(1)}, bf16[512,512]{1,0:T(8,128)(2,1)S(1)}, u32[]{:S(2)}, u32[]{:S(2)}) collective-permute-start(bf16[512,512]{1,0:T(8,128)(2,1)S(1)} %get-tuple-element.138), channel_id=1, source_target_pairs={{32,0},{40,8},{48,16},{56,24},{0,32},{8,40},{16,48},{24,56},{96,64... | collective-permute-start | bytes 1572872 | tf_op jit(solution)/shard_map/ppermute | solution.py:20
  111.9 15.4 %collective-permute-start.37 = (bf16[512,512]{1,0:T(8,128)(2,1)S(1)}, bf16[512,512]{1,0:T(8,128)(2,1)S(1)}, u32[]{:S(2)}, u32[]{:S(2)}) collective-permute-start(bf16[512,512]{1,0:T(8,128)(2,1)S(1)} %get-tuple-element.139), channel_id=1, source_target_pairs={{96,0},{104,8},{112,16},{120,24},{64,32},{72,40},{80,48},{88,56},{... | collective-permute-start | bytes 1572872 | tf_op jit(solution)/shard_map/ppermute | solution.py:20
  119.0 17.6 %collective-permute-start.34 = (bf16[512,512]{1,0:T(8,128)(2,1)S(1)}, bf16[512,512]{1,0:T(8,128)(2,1)S(1)}, u32[]{:S(2)}, u32[]{:S(2)}) collective-permute-start(bf16[512,512]{1,0:T(8,128)(2,1)S(1)} %get-tuple-element.134), channel_id=1, source_target_pairs={{8,0},{0,8},{24,16},{16,24},{40,32},{32,40},{56,48},{48,56},{72,64... | collective-permute-start | bytes 1572872 | tf_op jit(solution)/shard_map/ppermute | solution.py:20
  119.7 16.9 %collective-permute-start.35 = (bf16[512,512]{1,0:T(8,128)(2,1)S(1)}, bf16[512,512]{1,0:T(8,128)(2,1)S(1)}, u32[]{:S(2)}, u32[]{:S(2)}) collective-permute-start(bf16[512,512]{1,0:T(8,128)(2,1)S(1)} %get-tuple-element.135), channel_id=1, source_target_pairs={{24,0},{16,8},{8,16},{0,24},{56,32},{48,40},{40,48},{32,56},{88,64... | collective-permute-start | bytes 1572872 | tf_op jit(solution)/shard_map/ppermute | solution.py:20
  127.4 7.8 %collective-permute-start.38 = (bf16[256,512]{1,0:T(8,128)(2,1)S(1)}, bf16[256,512]{1,0:T(8,128)(2,1)S(1)}, u32[]{:S(2)}, u32[]{:S(2)}) collective-permute-start(bf16[256,512]{1,0:T(8,128)(2,1)S(1)} %get-tuple-element.143), channel_id=1, source_target_pairs={{32,0},{40,8},{48,16},{56,24},{0,32},{8,40},{16,48},{24,56},{96,64... | collective-permute-start | bytes 786440 | tf_op jit(solution)/shard_map/ppermute | solution.py:20
  128.1 8.5 %collective-permute-start.39 = (bf16[256,512]{1,0:T(8,128)(2,1)S(1)}, bf16[256,512]{1,0:T(8,128)(2,1)S(1)}, u32[]{:S(2)}, u32[]{:S(2)}) collective-permute-start(bf16[256,512]{1,0:T(8,128)(2,1)S(1)} %get-tuple-element.144), channel_id=1, source_target_pairs={{96,0},{104,8},{112,16},{120,24},{64,32},{72,40},{80,48},{88,56},{... | collective-permute-start | bytes 786440 | tf_op jit(solution)/shard_map/ppermute | solution.py:20
  136.7 14.0 %collective-permute-start.40 = (bf16[256,512]{1,0:T(8,128)(2,1)S(1)}, bf16[256,512]{1,0:T(8,128)(2,1)S(1)}, u32[]{:S(2)}, u32[]{:S(2)}) collective-permute-start(bf16[256,512]{1,0:T(8,128)(2,1)S(1)} %get-tuple-element.147), channel_id=1, source_target_pairs={{8,0},{0,8},{24,16},{16,24},{40,32},{32,40},{56,48},{48,56},{72,64... | collective-permute-start | bytes 786440 | tf_op jit(solution)/shard_map/ppermute | solution.py:20
  137.4 13.2 %collective-permute-start.41 = (bf16[256,512]{1,0:T(8,128)(2,1)S(1)}, bf16[256,512]{1,0:T(8,128)(2,1)S(1)}, u32[]{:S(2)}, u32[]{:S(2)}) collective-permute-start(bf16[256,512]{1,0:T(8,128)(2,1)S(1)} %get-tuple-element.148), channel_id=1, source_target_pairs={{24,0},{16,8},{8,16},{0,24},{56,32},{48,40},{40,48},{32,56},{88,64... | collective-permute-start | bytes 786440 | tf_op jit(solution)/shard_map/ppermute | solution.py:20
  140.3 7.1 %collective-permute-start.42 = (bf16[512,128]{1,0:T(8,128)(2,1)S(1)}, bf16[512,128]{1,0:T(8,128)(2,1)S(1)}, u32[]{:S(2)}, u32[]{:S(2)}) collective-permute-start(bf16[512,128]{1,0:T(8,128)(2,1)S(1)} %get-tuple-element.152), channel_id=1, source_target_pairs={{8,0},{0,8},{24,16},{16,24},{40,32},{32,40},{56,48},{48,56},{72,64... | collective-permute-start | bytes 393224 | tf_op jit(solution)/shard_map/ppermute | solution.py:20
  140.9 9.7 %collective-permute-start.43 = (bf16[512,128]{1,0:T(8,128)(2,1)S(1)}, bf16[512,128]{1,0:T(8,128)(2,1)S(1)}, u32[]{:S(2)}, u32[]{:S(2)}) collective-permute-start(bf16[512,128]{1,0:T(8,128)(2,1)S(1)} %get-tuple-element.153), channel_id=1, source_target_pairs={{16,0},{24,8},{0,16},{8,24},{48,32},{56,40},{32,48},{40,56},{80,64... | collective-permute-start | bytes 393224 | tf_op jit(solution)/shard_map/ppermute | solution.py:20
  142.4 8.3 %collective-permute-start.44 = (bf16[512,128]{1,0:T(8,128)(2,1)S(1)}, bf16[512,128]{1,0:T(8,128)(2,1)S(1)}, u32[]{:S(2)}, u32[]{:S(2)}) collective-permute-start(bf16[512,128]{1,0:T(8,128)(2,1)S(1)} %get-tuple-element.154), channel_id=1, source_target_pairs={{24,0},{16,8},{8,16},{0,24},{56,32},{48,40},{40,48},{32,56},{88,64... | collective-permute-start | bytes 393224 | tf_op jit(solution)/shard_map/ppermute | solution.py:20
  150.9 5.0 %collective-permute-start.45 = (bf16[512,128]{1,0:T(8,128)(2,1)S(1)}, bf16[512,128]{1,0:T(8,128)(2,1)S(1)}, u32[]{:S(2)}, u32[]{:S(2)}) collective-permute-start(bf16[512,128]{1,0:T(8,128)(2,1)S(1)} %get-tuple-element.162), channel_id=1, source_target_pairs={{32,0},{40,8},{48,16},{56,24},{0,32},{8,40},{16,48},{24,56},{96,64... | collective-permute-start | bytes 393224 | tf_op jit(solution)/shard_map/ppermute | solution.py:20
  151.6 7.0 %collective-permute-start.46 = (bf16[512,128]{1,0:T(8,128)(2,1)S(1)}, bf16[512,128]{1,0:T(8,128)(2,1)S(1)}, u32[]{:S(2)}, u32[]{:S(2)}) collective-permute-start(bf16[512,128]{1,0:T(8,128)(2,1)S(1)} %get-tuple-element.163), channel_id=1, source_target_pairs={{64,0},{72,8},{80,16},{88,24},{96,32},{104,40},{112,48},{120,56},{... | collective-permute-start | bytes 393224 | tf_op jit(solution)/shard_map/ppermute | solution.py:20
  154.2 6.2 %collective-permute-start.47 = (bf16[512,128]{1,0:T(8,128)(2,1)S(1)}, bf16[512,128]{1,0:T(8,128)(2,1)S(1)}, u32[]{:S(2)}, u32[]{:S(2)}) collective-permute-start(bf16[512,128]{1,0:T(8,128)(2,1)S(1)} %get-tuple-element.164), channel_id=1, source_target_pairs={{96,0},{104,8},{112,16},{120,24},{64,32},{72,40},{80,48},{88,56},{... | collective-permute-start | bytes 393224 | tf_op jit(solution)/shard_map/ppermute | solution.py:20
where the time goes:
time: 162 us
  starting transfers between devices  61.5 us (38%)
  waiting for transfers between devices  61.4 us (38%)
  Pallas kernels  36.7 us (23%)
  local copies, waits for them, and re-layouts  1.65 us (1%)
    ppermute x28, starting transfers between devices, from_wide(): return lax.ppermute(array, 'wide', [(i ^ step, i) for i in range(16)])  40.8 us
    pallas_call x18, Pallas kernels, call(): pl.pallas_call(kernel, out_shape=out_shape, in_specs=in_specs, out_specs=...  36.7 us
    ppermute x28, waiting for transfers between devices, from_wide(): return lax.ppermute(array, 'wide', [(i ^ step, i) for i in range(16)])  32.5 us
    ppermute x16, waiting for transfers between devices, from_y(): return lax.ppermute(array, 'narrow', [(i ^ bits * 2, i) for i in range(8)])  28.4 us
    ppermute x16, starting transfers between devices, from_y(): return lax.ppermute(array, 'narrow', [(i ^ bits * 2, i) for i in range(8)])  19.5 us
  transfers between devices with their start and end apart: 48, of which 28 were waited for; matrix products, arithmetic and copies ran while one was open for 0% of the time, Pallas kernels for 21%

commit v1 on v0

--- a/solution.py
+++ b/solution.py
@@ -32,13 +32,14 @@
     return lax.optimization_barrier((value, *earlier))[0]
 
 
-def call(kernel, name, out_shape, in_specs, operands, scratch=(), micros=0, many=True):
+def call(kernel, name, out_shape, in_specs, operands, scratch=(), micros=0, many=True, aliases={}):
     return pl.pallas_call(
         kernel,
         out_shape=out_shape,
         in_specs=in_specs,
         out_specs=[VMEM] * len(out_shape) if many else VMEM,
         scratch_shapes=scratch,
+        input_output_aliases=aliases,
         compiler_params=pltpu.CompilerParams(vmem_limit_bytes=LIMIT),
         cost_estimate=pl.CostEstimate(flops=micros * 10**9, bytes_accessed=0, transcendentals=0),
         name=name,
@@ -72,20 +73,18 @@
     return [rows, one, two, three]
 
 
-def assemble_kernel(first, place, own, one, two_a, two_b, three, out):
+def assemble_kernel(first, early, place, *refs):
+    parts, out = refs[:3], refs[3]
     z, x, y, c = place[0], place[1], place[2], place[3]
     block = out.shape[0] // 8
-    for outer in range(4):
+    for outer in (0, 1, 3) if early else (2,):
         for inner in range(4):
-            if first == "z":
-                column = (z ^ inner) * 4 + (x ^ outer)
+            dz, dx = (inner, outer) if first == "z" else (outer, inner)
+            columns = pl.ds(pl.multiple_of(((z ^ dz) * 4 + (x ^ dx)) * LANES, LANES), LANES)
+            if early:
+                part, index = parts[(0, 1, None, 2)[outer]], inner
             else:
-                column = (z ^ outer) * 4 + (x ^ inner)
-            columns = pl.ds(pl.multiple_of(column * LANES, LANES), LANES)
-            if outer == 2:
-                part, index = (two_a, inner) if inner < 2 else (two_b, inner - 2)
-            else:
-                part, index = (own, one, None, three)[outer], inner
+                part, index = parts[1 + inner // 2], inner % 2
             for side in range(2):
                 core = 1 - c if side == 0 else c
                 for j in range(4):
@@ -94,14 +93,17 @@
                     out[at : at + block, columns] = part[index, rows, :]
 
 
-def assemble(first, place, parts, rows, depth):
+def assemble(first, place, parts, base=None):
+    rows = parts[0].shape[1]
+    operands = [place, *parts] if base is None else [place, base, *parts]
     return call(
-        functools.partial(assemble_kernel, first),
+        functools.partial(assemble_kernel, first, base is None),
         "assemble_" + first,
-        jax.ShapeDtypeStruct((rows, depth), BF16),
-        [SMEM] + [VMEM] * len(parts),
-        [place, *parts],
+        jax.ShapeDtypeStruct((rows, 16 * LANES), BF16),
+        [SMEM] + [VMEM] * (len(operands) - 1),
+        operands,
         many=False,
+        aliases={} if base is None else {1: 0},
     )
 
 
@@ -275,7 +277,6 @@
 def body(tokens, gate_weight, up_weight, down_weight):
     wide, narrow = lax.axis_index("wide"), lax.axis_index("narrow")
     place = jnp.stack([wide // 4, wide % 4, narrow // 2, narrow % 2]).astype(jnp.int32)
-    depth = gate_weight.shape[0]
     rows = tokens.shape[0] // 2
     both = range(2)
     tokens = after(tokens, place)
@@ -285,11 +286,10 @@
     nexts = [[from_wide(axis, bits, stack) for bits in (1, 3)] for axis, stack in zip("xz", stacks)]
     *weights, down_weight = load(*after((gate_weight, up_weight, down_weight), stacks))
     nexts[0] = after(nexts[0], down_weight)
-    planes = [
-        [stack, one, from_wide(axis, 1, three[:2]), from_wide(axis, 3, one[2:]), three]
-        for axis, stack, (one, three) in zip("xz", stacks, nexts)
-    ]
-    chunks = [assemble(axis, place, plane, rows, depth) for axis, plane in zip("zx", planes)]
+    bases = [assemble(axis, place, [stack, *near]) for axis, stack, near in zip("zx", stacks, nexts)]
+    fars = [(from_wide(axis, 1, three[:2]), from_wide(axis, 3, one[2:])) for axis, (one, three) in zip("xz", nexts)]
+    fars[0] = after(fars[0], bases[1])
+    chunks = [assemble(axis, place, far, base) for axis, far, base in zip("zx", fars, bases)]
     others = []
     for at in both:
         others.append(project_other(after(chunks[at], *others), *weights))
@@ -307,13 +307,14 @@
     half = parts[0][0].shape[0] // 2
     first = [first_round(from_y, p) for p in parts]
     second = [second_round(from_y, relay(parts[0], *after(first[0], parts[1][0]))), None]
-    first[1], second[0] = together((first[1], second[0]))
+    relayed = relay(parts[1], *first[1])
+    second[0] = after(second[0], relayed[0])
     hidden = [hidden_of([parts[0][0], *first[0], *second[0]]), None]
     near = [[from_y(bits, hidden[0]) for bits in (1, 3)], None]
-    second[1] = second_round(from_y, relay(parts[1], *first[1]))
-    near[0], second[1] = together((near[0], second[1]))
+    second[1] = second_round(from_y, relayed)
     hidden[1] = hidden_of([parts[1][0], *first[1], *second[1]])
     near[1] = [from_y(bits, hidden[1]) for bits in (1, 3)]
+    near[0] = after(near[0], hidden[1])
     far = [second_round(from_y, (near[0][1][:half], near[0][0][half:])), None]
     near[1], far[0] = together((near[1], far[0]))
     parts = []
@@ -325,10 +326,11 @@
     along = [functools.partial(from_wide, axis) for axis in "zx"]
     first = [first_round(exchange, p) for exchange, p in zip(along, parts)]
     second[0] = second_round(along[0], relay(parts[0], *after(first[0], parts[1][0])))
-    first[1], second[0] = together((first[1], second[0]))
-    second[1] = second_round(along[1], relay(parts[1], *first[1]))
+    relayed = relay(parts[1], *first[1])
+    second[0] = after(second[0], relayed[0])
+    second[1] = second_round(along[1], relayed)
     final = send("x", add_line([parts[0][0], *first[0], *second[0]]))
-    second[1], final = together((second[1], final))
+    second[1], final[1] = together((second[1], final[1]))
     return last(place, final + send("z", add_line([parts[1][0], *first[1], *second[1]])))
 
 

time: 162 us -> 153 us (0.944)
  waiting for transfers between devices: 61.4 us -> 51.5 us
    ppermute x28, waiting for transfers between devices: 32.5 us -> 27 us  [from_wide(): return lax.ppermute(array, 'wide', [(i ^ step, i) for i in range(16)])]
    ppermute x16, waiting for transfers between devices: 28.4 us -> 23.6 us  [from_y(): return lax.ppermute(array, 'narrow', [(i ^ bits * 2, i) for i in range(8)])]
    pallas_call x18 -> x20, Pallas kernels: 36.7 us -> 37.7 us  [call(): pl.pallas_call(kernel, out_shape=out_shape, in_specs=in_specs, out_specs=...]
  transfers between devices with their start and end apart: 48 -> 48, of which waited for: 28 -> 27; matrix products, arithmetic and copies ran while one was open for 0% -> 0% of each run, Pallas kernels for 21% -> 24%
where the time goes in v1:
time: 153 us
  starting transfers between devices  61.3 us (40%)
  waiting for transfers between devices  51.5 us (34%)
  Pallas kernels  37.7 us (25%)
  local copies, waits for them, and re-layouts  1.65 us (1%)
    ppermute x28, starting transfers between devices, from_wide(): return lax.ppermute(array, 'wide', [(i ^ step, i) for i in range(16)])  40 us
    pallas_call x20, Pallas kernels, call(): pl.pallas_call(kernel, out_shape=out_shape, in_specs=in_specs, out_specs=...  37.7 us
    ppermute x28, waiting for transfers between devices, from_wide(): return lax.ppermute(array, 'wide', [(i ^ step, i) for i in range(16)])  27 us
    ppermute x16, waiting for transfers between devices, from_y(): return lax.ppermute(array, 'narrow', [(i ^ bits * 2, i) for i in range(8)])  23.6 us
    ppermute x16, starting transfers between devices, from_y(): return lax.ppermute(array, 'narrow', [(i ^ bits * 2, i) for i in range(8)])  20.3 us
  transfers between devices with their start and end apart: 48, of which 27 were waited for; matrix products, arithmetic and copies ran while one was open for 0% of the time, Pallas kernels for 24%

profile of v1, /device:TPU:0, one launch (start us, length us, event | category | flops | bytes accessed | tf_op | source)
XLA Modules:
  0.0 152.7 jit_solution(12479795547110784634)
XLA Ops:
  0.1 1.0 slice_bitcast_fusion
  1.1 1.7 %collective-permute-start.3 = (bf16[512,128]{1,0:T(8,128)(2,1)S(1)}, bf16[512,128]{1,0:T(8,128)(2,1)S(1)}, u32[]{:S(2)}, u32[]{:S(2)}) collective-permute-start(bf16[512,128]{1,0:T(8,128)(2,1)S(1)} %get-tuple-element.152), channel_id=1, source_target_pairs={{8,0},{0,8},{24,16},{16,24},{40,32},{32,40},{56,48},{48,56},{72,64... | collective-permute-start | bytes 393224 | tf_op jit(solution)/shard_map/ppermute | solution.py:20
  2.7 1.9 %collective-permute-start = (bf16[512,128]{1,0:T(8,128)(2,1)S(1)}, bf16[512,128]{1,0:T(8,128)(2,1)S(1)}, u32[]{:S(2)}, u32[]{:S(2)}) collective-permute-start(bf16[512,128]{1,0:T(8,128)(2,1)S(1)} %get-tuple-element.79), channel_id=1, source_target_pairs={{32,0},{40,8},{48,16},{56,24},{0,32},{8,40},{16,48},{24,56},{96,64... | collective-permute-start | bytes 393224 | tf_op jit(solution)/shard_map/ppermute | solution.py:20
  4.7 3.6 %collective-permute-start.1 = (bf16[512,128]{1,0:T(8,128)(2,1)S(1)}, bf16[512,128]{1,0:T(8,128)(2,1)S(1)}, u32[]{:S(2)}, u32[]{:S(2)}) collective-permute-start(bf16[512,128]{1,0:T(8,128)(2,1)S(1)} %get-tuple-element.79), channel_id=1, source_target_pairs={{64,0},{72,8},{80,16},{88,24},{96,32},{104,40},{112,48},{120,56},{... | collective-permute-start | bytes 393224 | tf_op jit(solution)/shard_map/ppermute | solution.py:20
  8.3 2.7 %collective-permute-start.6 = (bf16[512,128]{1,0:T(8,128)(2,1)S(1)}, bf16[512,128]{1,0:T(8,128)(2,1)S(1)}, u32[]{:S(2)}, u32[]{:S(2)}) collective-permute-start(bf16[512,128]{1,0:T(8,128)(2,1)S(1)} %get-tuple-element.152), channel_id=1, source_target_pairs={{16,0},{24,8},{0,16},{8,24},{48,32},{56,40},{32,48},{40,56},{80,64... | collective-permute-start | bytes 393224 | tf_op jit(solution)/shard_map/ppermute | solution.py:20
  11.5 2.6 %collective-permute-done.1 = bf16[512,128]{1,0:T(8,128)(2,1)S(1)} collective-permute-done((bf16[512,128]{1,0:T(8,128)(2,1)S(1)}, bf16[512,128]{1,0:T(8,128)(2,1)S(1)}, u32[]{:S(2)}, u32[]{:S(2)}) %collective-permute-start.1) | collective-permute-done | bytes 131104 | tf_op jit(solution)/shard_map/ppermute | solution.py:20
  14.1 1.9 %collective-permute-done.2 = bf16[512,128]{1,0:T(8,128)(2,1)S(1)} collective-permute-done((bf16[512,128]{1,0:T(8,128)(2,1)S(1)}, bf16[512,128]{1,0:T(8,128)(2,1)S(1)}, u32[]{:S(2)}, u32[]{:S(2)}) %collective-permute-start.2) | collective-permute-done | bytes 131104 | tf_op jit(solution)/shard_map/ppermute | solution.py:20
  16.7 2.8 %collective-permute-start.5 = (bf16[4,512,128]{2,1,0:T(8,128)(2,1)S(1)}, bf16[4,512,128]{2,1,0:T(8,128)(2,1)S(1)}, u32[]{:S(2)}, u32[]{:S(2)}) collective-permute-start(bf16[4,512,128]{2,1,0:T(8,128)(2,1)S(1)} %pad_maximum_fusion.refs_0_), channel_id=1, source_target_pairs={{24,0},{16,8},{8,16},{0,24},{56,32},{48,40},{40,48},{32,56},{88,64... | collective-permute-start | bytes 1572872 | tf_op jit(solution)/shard_map/ppermute | solution.py:20
  19.6 1.8 %collective-permute-start.11 = (bf16[4,512,128]{2,1,0:T(8,128)(2,1)S(1)}, bf16[4,512,128]{2,1,0:T(8,128)(2,1)S(1)}, u32[]{:S(2)}, u32[]{:S(2)}) collective-permute-start(bf16[4,512,128]{2,1,0:T(8,128)(2,1)S(1)} %pad_maximum_fusion.1.refs_0_), channel_id=1, source_target_pairs={{96,0},{104,8},{112,16},{120,24},{64,32},{72,40},{80,48},{88,56},{... | collective-permute-start | bytes 1572872 | tf_op jit(solution)/shard_map/ppermute | solution.py:20
  21.4 6.8 %load.1 = (bf16[2048,1664]{1,0:T(8,128)(2,1)S(1)}, bf16[2048,1664]{1,0:T(8,128)(2,1)S(1)}, bf16[1664,2048]{1,0:T(8,128)(2,1)S(1)}) custom-call(bf16[2048,1664]{1,0:T(8,128)(2,1)} %refs_0_, bf16[2048,1664]{1,0:T(8,128)(2,1)} %refs_1_, bf16[1664,2048]{1,0:T(8,128)(2,1)} %refs_2_), custom_call_target="tpu_custom_call" | custom-call | flops 5000000000 | tf_op jit(solution)/shard_map/load/pallas_call | solution.py:36
  28.2 0.9 collective-permute-done.4.refs_1_
  29.1 1.5 collective-permute-done.5.refs_2_
  31.0 2.6 %collective-permute-start.9 = (bf16[2,512,128]{2,1,0:T(8,128)(2,1)S(1)}, bf16[2,512,128]{2,1,0:T(8,128)(2,1)S(1)}, u32[]{:S(2)}, u32[]{:S(2)}) collective-permute-start(bf16[2,512,128]{2,1,0:T(8,128)(2,1)S(1)} %slice.33), channel_id=1, source_target_pairs={{24,0},{16,8},{8,16},{0,24},{56,32},{48,40},{40,48},{32,56},{88,64... | collective-permute-start | bytes 786440 | tf_op jit(solution)/shard_map/ppermute | solution.py:20
  33.6 1.0 assemble_z.2.refs_0_
  34.7 0.9 collective-permute-start.13
  35.6 1.0 assemble_x.2.refs_0_
  37.1 1.6 %collective-permute-done.9.refs_2_ = bf16[2,512,128]{2,1,0:T(8,128)(2,1)S(1)} collective-permute-done((bf16[2,512,128]{2,1,0:T(8,128)(2,1)S(1)}, bf16[2,512,128]{2,1,0:T(8,128)(2,1)S(1)}, u32[]{:S(2)}, u32[]{:S(2)}) %collective-permute-start.9) | collective-permute-done | bytes 262176 | tf_op jit(solution)/shard_map/ppermute | solution.py:20
  39.4 3.9 %project_other.2 = f32[256,3328]{1,0:T(8,128)S(1)} custom-call(bf16[512,2048]{1,0:T(8,128)(2,1)S(1)} %assemble_z.3.rows, bf16[2048,1664]{1,0:T(8,128)(2,1)S(1)} %get-tuple-element.91.gate_weight, bf16[2048,1664]{1,0:T(8,128)(2,1)S(1)} %get-tuple-element.92.up_weight), custom_call_target="tpu_custom_call" | custom-call | flops 4000000000 | tf_op jit(solution)/shard_map/project_other/pallas_call | solution.py:36
  43.4 0.7 assemble_x.3.rows
  44.1 3.9 %project_other.3 = f32[256,3328]{1,0:T(8,128)S(1)} custom-call(bf16[512,2048]{1,0:T(8,128)(2,1)S(1)} %assemble_x.3.rows, bf16[2048,1664]{1,0:T(8,128)(2,1)S(1)} %get-tuple-element.91.gate_weight, bf16[2048,1664]{1,0:T(8,128)(2,1)S(1)} %get-tuple-element.92.up_weight), custom_call_target="tpu_custom_call" | custom-call | flops 4000000000 | tf_op jit(solution)/shard_map/project_other/pallas_call | solution.py:36
  48.0 0.7 collective-permute-start.17
  49.4 3.9 %project_own.2 = (f32[64,3328]{1,0:T(8,128)S(1)}, bf16[64,3328]{1,0:T(8,128)(2,1)S(1)}, bf16[64,3328]{1,0:T(8,128)(2,1)S(1)}, f32[32,3328]{1,0:T(8,128)S(1)}, f32[32,3328]{1,0:T(8,128)S(1)}) custom-call(bf16[512,2048]{1,0:T(8,128)(2,1)S(1)} %assemble_z.3.rows, bf16[2048,1664]{1,0:T(8,128)(2,1)S(1)} %get-tuple-element.91.gate_weight, ...), custom_call_target="tpu_custom_call" | custom-call | flops 4000000000 | tf_op jit(solution)/shard_map/project_own/pallas_call | solution.py:36
  53.3 1.7 %collective-permute-start.15 = (bf16[64,3328]{1,0:T(8,128)(2,1)S(1)}, bf16[64,3328]{1,0:T(8,128)(2,1)S(1)}, u32[]{:S(2)}, u32[]{:S(2)}) collective-permute-start(bf16[64,3328]{1,0:T(8,128)(2,1)S(1)} %get-tuple-element.96), channel_id=1, source_target_pairs={{2,0},{3,1},{0,2},{1,3},{6,4},{7,5},{4,6},{5,7},{10,8},{11,9},{8,1... | collective-permute-start | bytes 1277960 | tf_op jit(solution)/shard_map/ppermute | solution.py:24
  55.0 2.2 %collective-permute-start.16 = (bf16[64,3328]{1,0:T(8,128)(2,1)S(1)}, bf16[64,3328]{1,0:T(8,128)(2,1)S(1)}, u32[]{:S(2)}, u32[]{:S(2)}) collective-permute-start(bf16[64,3328]{1,0:T(8,128)(2,1)S(1)} %get-tuple-element.97), channel_id=1, source_target_pairs={{6,0},{7,1},{4,2},{5,3},{2,4},{3,5},{0,6},{1,7},{14,8},{15,9},{12,... | collective-permute-start | bytes 1277960 | tf_op jit(solution)/shard_map/ppermute | solution.py:24
  57.1 3.9 %project_own.3 = (f32[64,3328]{1,0:T(8,128)S(1)}, bf16[64,3328]{1,0:T(8,128)(2,1)S(1)}, bf16[64,3328]{1,0:T(8,128)(2,1)S(1)}, f32[32,3328]{1,0:T(8,128)S(1)}, f32[32,3328]{1,0:T(8,128)S(1)}) custom-call(bf16[512,2048]{1,0:T(8,128)(2,1)S(1)} %assemble_x.3.rows, bf16[2048,1664]{1,0:T(8,128)(2,1)S(1)} %get-tuple-element.91.gate_weight, ...), custom_call_target="tpu_custom_call" | custom-call | flops 4000000000 | tf_op jit(solution)/shard_map/project_own/pallas_call | solution.py:36
  61.0 0.8 collective-permute-start.20
  62.4 3.6 %collective-permute-done.15.from_one.refs_1_ = bf16[64,3328]{1,0:T(8,128)(2,1)S(1)} collective-permute-done((bf16[64,3328]{1,0:T(8,128)(2,1)S(1)}, bf16[64,3328]{1,0:T(8,128)(2,1)S(1)}, u32[]{:S(2)}, u32[]{:S(2)}) %collective-permute-start.15) | collective-permute-done | bytes 426016 | tf_op jit(solution)/shard_map/ppermute | solution.py:24
  66.0 2.8 %collective-permute-done.16.from_three.refs_2_ = bf16[64,3328]{1,0:T(8,128)(2,1)S(1)} collective-permute-done((bf16[64,3328]{1,0:T(8,128)(2,1)S(1)}, bf16[64,3328]{1,0:T(8,128)(2,1)S(1)}, u32[]{:S(2)}, u32[]{:S(2)}) %collective-permute-start.16) | collective-permute-done | bytes 426016 | tf_op jit(solution)/shard_map/ppermute | solution.py:24
  69.0 2.3 %collective-permute-start.19 = (bf16[32,3328]{1,0:T(8,128)(2,1)S(1)}, bf16[32,3328]{1,0:T(8,128)(2,1)S(1)}, u32[]{:S(2)}, u32[]{:S(2)}) collective-permute-start(bf16[32,3328]{1,0:T(8,128)(2,1)S(1)} %get-tuple-element.105), channel_id=1, source_target_pairs={{6,0},{7,1},{4,2},{5,3},{2,4},{3,5},{0,6},{1,7},{14,8},{15,9},{12,... | collective-permute-start | bytes 638984 | tf_op jit(solution)/shard_map/ppermute | solution.py:24
  71.3 3.9 %collective-permute-done.20.from_one.refs_1_ = bf16[64,3328]{1,0:T(8,128)(2,1)S(1)} collective-permute-done((bf16[64,3328]{1,0:T(8,128)(2,1)S(1)}, bf16[64,3328]{1,0:T(8,128)(2,1)S(1)}, u32[]{:S(2)}, u32[]{:S(2)}) %collective-permute-start.20) | collective-permute-done | bytes 426016 | tf_op jit(solution)/shard_map/ppermute | solution.py:24
  75.2 2.8 %collective-permute-done.21.from_three.refs_2_ = bf16[64,3328]{1,0:T(8,128)(2,1)S(1)} collective-permute-done((bf16[64,3328]{1,0:T(8,128)(2,1)S(1)}, bf16[64,3328]{1,0:T(8,128)(2,1)S(1)}, u32[]{:S(2)}, u32[]{:S(2)}) %collective-permute-start.21) | collective-permute-done | bytes 426016 | tf_op jit(solution)/shard_map/ppermute | solution.py:24
  78.2 2.3 %collective-permute-start.25 = (bf16[32,3328]{1,0:T(8,128)(2,1)S(1)}, bf16[32,3328]{1,0:T(8,128)(2,1)S(1)}, u32[]{:S(2)}, u32[]{:S(2)}) collective-permute-start(bf16[32,3328]{1,0:T(8,128)(2,1)S(1)} %get-tuple-element.113), channel_id=1, source_target_pairs={{6,0},{7,1},{4,2},{5,3},{2,4},{3,5},{0,6},{1,7},{14,8},{15,9},{12,... | collective-permute-start | bytes 638984 | tf_op jit(solution)/shard_map/ppermute | solution.py:24
  80.4 2.1 %collective-permute-done.19.refs_4_ = bf16[32,3328]{1,0:T(8,128)(2,1)S(1)} collective-permute-done((bf16[32,3328]{1,0:T(8,128)(2,1)S(1)}, bf16[32,3328]{1,0:T(8,128)(2,1)S(1)}, u32[]{:S(2)}, u32[]{:S(2)}) %collective-permute-start.19) | collective-permute-done | bytes 213024 | tf_op jit(solution)/shard_map/ppermute | solution.py:24
  82.9 2.3 %collective-permute-start.23 = (bf16[64,1664]{1,0:T(8,128)(2,1)S(1)}, bf16[64,1664]{1,0:T(8,128)(2,1)S(1)}, u32[]{:S(2)}, u32[]{:S(2)}) collective-permute-start(bf16[64,1664]{1,0:T(8,128)(2,1)S(1)} %hidden.2), channel_id=1, source_target_pairs={{6,0},{7,1},{4,2},{5,3},{2,4},{3,5},{0,6},{1,7},{14,8},{15,9},{12,... | collective-permute-start | bytes 638984 | tf_op jit(solution)/shard_map/ppermute | solution.py:24
  85.1 2.1 %collective-permute-done.25.refs_4_ = bf16[32,3328]{1,0:T(8,128)(2,1)S(1)} collective-permute-done((bf16[32,3328]{1,0:T(8,128)(2,1)S(1)}, bf16[32,3328]{1,0:T(8,128)(2,1)S(1)}, u32[]{:S(2)}, u32[]{:S(2)}) %collective-permute-start.25) | collective-permute-done | bytes 213024 | tf_op jit(solution)/shard_map/ppermute | solution.py:24
  87.6 2.3 %collective-permute-start.27 = (bf16[64,1664]{1,0:T(8,128)(2,1)S(1)}, bf16[64,1664]{1,0:T(8,128)(2,1)S(1)}, u32[]{:S(2)}, u32[]{:S(2)}) collective-permute-start(bf16[64,1664]{1,0:T(8,128)(2,1)S(1)} %hidden.3), channel_id=1, source_target_pairs={{6,0},{7,1},{4,2},{5,3},{2,4},{3,5},{0,6},{1,7},{14,8},{15,9},{12,... | collective-permute-start | bytes 638984 | tf_op jit(solution)/shard_map/ppermute | solution.py:24
  90.1 2.3 %collective-permute-done.23 = bf16[64,1664]{1,0:T(8,128)(2,1)S(1)} collective-permute-done((bf16[64,1664]{1,0:T(8,128)(2,1)S(1)}, bf16[64,1664]{1,0:T(8,128)(2,1)S(1)}, u32[]{:S(2)}, u32[]{:S(2)}) %collective-permute-start.23) | collective-permute-done | bytes 213024 | tf_op jit(solution)/shard_map/ppermute | solution.py:24
  92.5 2.3 %collective-permute-start.29 = (bf16[32,1664]{1,0:T(8,128)(2,1)S(1)}, bf16[32,1664]{1,0:T(8,128)(2,1)S(1)}, u32[]{:S(2)}, u32[]{:S(2)}) collective-permute-start(bf16[32,1664]{1,0:T(8,128)(2,1)S(1)} %slice.37), channel_id=1, source_target_pairs={{6,0},{7,1},{4,2},{5,3},{2,4},{3,5},{0,6},{1,7},{14,8},{15,9},{12,... | collective-permute-start | bytes 319496 | tf_op jit(solution)/shard_map/ppermute | solution.py:24
  94.8 1.4 collective-permute-done.27
  96.3 0.9 collective-permute-done.28
  97.2 1.4 collective-permute-done.29
  98.8 0.8 collective-permute-start.33
  99.6 2.5 %collective-permute-start.34 = (bf16[32,1664]{1,0:T(8,128)(2,1)S(1)}, bf16[32,1664]{1,0:T(8,128)(2,1)S(1)}, u32[]{:S(2)}, u32[]{:S(2)}) collective-permute-start(bf16[32,1664]{1,0:T(8,128)(2,1)S(1)} %slice.39), channel_id=1, source_target_pairs={{6,0},{7,1},{4,2},{5,3},{2,4},{3,5},{0,6},{1,7},{14,8},{15,9},{12,... | collective-permute-start | bytes 319496 | tf_op jit(solution)/shard_map/ppermute | solution.py:24
  102.3 4.7 %down_z.1 = (f32[512,512]{1,0:T(8,128)S(1)}, bf16[512,512]{1,0:T(8,128)(2,1)S(1)}, bf16[512,512]{1,0:T(8,128)(2,1)S(1)}, f32[256,512]{1,0:T(8,128)S(1)}, f32[256,512]{1,0:T(8,128)S(1)}) custom-call(s32[4]{0:T(128)S(1)} %pad_add_fusion.place, bf16[512,1664]{1,0:T(8,128)(2,1)S(1)} %constant_dynamic-update-slice_fusion.5.rows, ...), custom_call_target="tpu_custom_call" | custom-call | flops 4000000000 | tf_op jit(solution)/shard_map/down_z/pallas_call | solution.py:36
  107.3 2.0 %collective-permute-start.32 = (bf16[512,512]{1,0:T(8,128)(2,1)S(1)}, bf16[512,512]{1,0:T(8,128)(2,1)S(1)}, u32[]{:S(2)}, u32[]{:S(2)}) collective-permute-start(bf16[512,512]{1,0:T(8,128)(2,1)S(1)} %get-tuple-element.120), channel_id=1, source_target_pairs={{96,0},{104,8},{112,16},{120,24},{64,32},{72,40},{80,48},{88,56},{... | collective-permute-start | bytes 1572872 | tf_op jit(solution)/shard_map/ppermute | solution.py:20
  109.6 4.7 %down_x.1 = (f32[512,512]{1,0:T(8,128)S(1)}, bf16[512,512]{1,0:T(8,128)(2,1)S(1)}, bf16[512,512]{1,0:T(8,128)(2,1)S(1)}, f32[256,512]{1,0:T(8,128)S(1)}, f32[256,512]{1,0:T(8,128)S(1)}) custom-call(s32[4]{0:T(128)S(1)} %pad_add_fusion.place, bf16[512,1664]{1,0:T(8,128)(2,1)S(1)} %constant_dynamic-update-slice_fusion.16.rows, ...), custom_call_target="tpu_custom_call" | custom-call | flops 4000000000 | tf_op jit(solution)/shard_map/down_x/pallas_call | solution.py:36
  114.3 1.0 collective-permute-start.38
  115.3 2.4 %collective-permute-start.39 = (bf16[512,512]{1,0:T(8,128)(2,1)S(1)}, bf16[512,512]{1,0:T(8,128)(2,1)S(1)}, u32[]{:S(2)}, u32[]{:S(2)}) collective-permute-start(bf16[512,512]{1,0:T(8,128)(2,1)S(1)} %get-tuple-element.135), channel_id=1, source_target_pairs={{24,0},{16,8},{8,16},{0,24},{56,32},{48,40},{40,48},{32,56},{88,64... | collective-permute-start | bytes 1572872 | tf_op jit(solution)/shard_map/ppermute | solution.py:20
  117.7 3.8 %collective-permute-done.31.from_one = bf16[512,512]{1,0:T(8,128)(2,1)S(1)} collective-permute-done((bf16[512,512]{1,0:T(8,128)(2,1)S(1)}, bf16[512,512]{1,0:T(8,128)(2,1)S(1)}, u32[]{:S(2)}, u32[]{:S(2)}) %collective-permute-start.31) | collective-permute-done | bytes 524320 | tf_op jit(solution)/shard_map/ppermute | solution.py:20
  121.5 1.2 collective-permute-done.32.from_three
  123.4 2.0 %collective-permute-start.37 = (bf16[256,512]{1,0:T(8,128)(2,1)S(1)}, bf16[256,512]{1,0:T(8,128)(2,1)S(1)}, u32[]{:S(2)}, u32[]{:S(2)}) collective-permute-start(bf16[256,512]{1,0:T(8,128)(2,1)S(1)} %get-tuple-element.131), channel_id=1, source_target_pairs={{96,0},{104,8},{112,16},{120,24},{64,32},{72,40},{80,48},{88,56},{... | collective-permute-start | bytes 786440 | tf_op jit(solution)/shard_map/ppermute | solution.py:20
  125.4 3.0 %collective-permute-done.38.from_one = bf16[512,512]{1,0:T(8,128)(2,1)S(1)} collective-permute-done((bf16[512,512]{1,0:T(8,128)(2,1)S(1)}, bf16[512,512]{1,0:T(8,128)(2,1)S(1)}, u32[]{:S(2)}, u32[]{:S(2)}) %collective-permute-start.38) | collective-permute-done | bytes 524320 | tf_op jit(solution)/shard_map/ppermute | solution.py:20
  128.4 1.6 %collective-permute-done.39.from_three = bf16[512,512]{1,0:T(8,128)(2,1)S(1)} collective-permute-done((bf16[512,512]{1,0:T(8,128)(2,1)S(1)}, bf16[512,512]{1,0:T(8,128)(2,1)S(1)}, u32[]{:S(2)}, u32[]{:S(2)}) %collective-permute-start.39) | collective-permute-done | bytes 524320 | tf_op jit(solution)/shard_map/ppermute | solution.py:20
  130.4 2.4 %collective-permute-start.41 = (bf16[256,512]{1,0:T(8,128)(2,1)S(1)}, bf16[256,512]{1,0:T(8,128)(2,1)S(1)}, u32[]{:S(2)}, u32[]{:S(2)}) collective-permute-start(bf16[256,512]{1,0:T(8,128)(2,1)S(1)} %get-tuple-element.140), channel_id=1, source_target_pairs={{24,0},{16,8},{8,16},{0,24},{56,32},{48,40},{40,48},{32,56},{88,64... | collective-permute-start | bytes 786440 | tf_op jit(solution)/shard_map/ppermute | solution.py:20
  133.1 1.4 collective-permute-start.42
  134.5 1.7 %collective-permute-start.43 = (bf16[512,128]{1,0:T(8,128)(2,1)S(1)}, bf16[512,128]{1,0:T(8,128)(2,1)S(1)}, u32[]{:S(2)}, u32[]{:S(2)}) collective-permute-start(bf16[512,128]{1,0:T(8,128)(2,1)S(1)} %get-tuple-element.143), channel_id=1, source_target_pairs={{16,0},{24,8},{0,16},{8,24},{48,32},{56,40},{32,48},{40,56},{80,64... | collective-permute-start | bytes 393224 | tf_op jit(solution)/shard_map/ppermute | solution.py:20
  136.1 1.7 %collective-permute-start.44 = (bf16[512,128]{1,0:T(8,128)(2,1)S(1)}, bf16[512,128]{1,0:T(8,128)(2,1)S(1)}, u32[]{:S(2)}, u32[]{:S(2)}) collective-permute-start(bf16[512,128]{1,0:T(8,128)(2,1)S(1)} %get-tuple-element.144), channel_id=1, source_target_pairs={{24,0},{16,8},{8,16},{0,24},{56,32},{48,40},{40,48},{32,56},{88,64... | collective-permute-start | bytes 393224 | tf_op jit(solution)/shard_map/ppermute | solution.py:20
  137.8 3.4 %collective-permute-done.42.refs_1_ = bf16[512,128]{1,0:T(8,128)(2,1)S(1)} collective-permute-done((bf16[512,128]{1,0:T(8,128)(2,1)S(1)}, bf16[512,128]{1,0:T(8,128)(2,1)S(1)}, u32[]{:S(2)}, u32[]{:S(2)}) %collective-permute-start.42) | collective-permute-done | bytes 131104 | tf_op jit(solution)/shard_map/ppermute | solution.py:20
  141.5 0.8 collective-permute-start.45
  142.3 2.9 %collective-permute-start.46 = (bf16[512,128]{1,0:T(8,128)(2,1)S(1)}, bf16[512,128]{1,0:T(8,128)(2,1)S(1)}, u32[]{:S(2)}, u32[]{:S(2)}) collective-permute-start(bf16[512,128]{1,0:T(8,128)(2,1)S(1)} %get-tuple-element.149), channel_id=1, source_target_pairs={{64,0},{72,8},{80,16},{88,24},{96,32},{104,40},{112,48},{120,56},{... | collective-permute-start | bytes 393224 | tf_op jit(solution)/shard_map/ppermute | solution.py:20
  145.2 1.1 collective-permute-start.47
  146.5 3.0 %collective-permute-done.46.refs_6_ = bf16[512,128]{1,0:T(8,128)(2,1)S(1)} collective-permute-done((bf16[512,128]{1,0:T(8,128)(2,1)S(1)}, bf16[512,128]{1,0:T(8,128)(2,1)S(1)}, u32[]{:S(2)}, u32[]{:S(2)}) %collective-permute-start.46) | collective-permute-done | bytes 131104 | tf_op jit(solution)/shard_map/ppermute | solution.py:20
  149.5 1.8 %collective-permute-done.47.refs_7_ = bf16[512,128]{1,0:T(8,128)(2,1)S(1)} collective-permute-done((bf16[512,128]{1,0:T(8,128)(2,1)S(1)}, bf16[512,128]{1,0:T(8,128)(2,1)S(1)}, u32[]{:S(2)}, u32[]{:S(2)}) %collective-permute-start.47) | collective-permute-done | bytes 131104 | tf_op jit(solution)/shard_map/ppermute | solution.py:20
  151.3 1.4 last.1
  (76 shorter events, 8.7 us)
Async XLA Ops:
  1.1 9.9 %collective-permute-start.3 = (bf16[512,128]{1,0:T(8,128)(2,1)S(1)}, bf16[512,128]{1,0:T(8,128)(2,1)S(1)}, u32[]{:S(2)}, u32[]{:S(2)}) collective-permute-start(bf16[512,128]{1,0:T(8,128)(2,1)S(1)} %get-tuple-element.152), channel_id=1, source_target_pairs={{8,0},{0,8},{24,16},{16,24},{40,32},{32,40},{56,48},{48,56},{72,64... | collective-permute-start | bytes 393224 | tf_op jit(solution)/shard_map/ppermute | solution.py:20
  2.7 8.7 %collective-permute-start = (bf16[512,128]{1,0:T(8,128)(2,1)S(1)}, bf16[512,128]{1,0:T(8,128)(2,1)S(1)}, u32[]{:S(2)}, u32[]{:S(2)}) collective-permute-start(bf16[512,128]{1,0:T(8,128)(2,1)S(1)} %get-tuple-element.79), channel_id=1, source_target_pairs={{32,0},{40,8},{48,16},{56,24},{0,32},{8,40},{16,48},{24,56},{96,64... | collective-permute-start | bytes 393224 | tf_op jit(solution)/shard_map/ppermute | solution.py:20
  4.7 9.4 %collective-permute-start.1 = (bf16[512,128]{1,0:T(8,128)(2,1)S(1)}, bf16[512,128]{1,0:T(8,128)(2,1)S(1)}, u32[]{:S(2)}, u32[]{:S(2)}) collective-permute-start(bf16[512,128]{1,0:T(8,128)(2,1)S(1)} %get-tuple-element.79), channel_id=1, source_target_pairs={{64,0},{72,8},{80,16},{88,24},{96,32},{104,40},{112,48},{120,56},{... | collective-permute-start | bytes 393224 | tf_op jit(solution)/shard_map/ppermute | solution.py:20
  8.2 7.7 %collective-permute-start.2 = (bf16[512,128]{1,0:T(8,128)(2,1)S(1)}, bf16[512,128]{1,0:T(8,128)(2,1)S(1)}, u32[]{:S(2)}, u32[]{:S(2)}) collective-permute-start(bf16[512,128]{1,0:T(8,128)(2,1)S(1)} %get-tuple-element.79), channel_id=1, source_target_pairs={{96,0},{104,8},{112,16},{120,24},{64,32},{72,40},{80,48},{88,56},{... | collective-permute-start | bytes 393224 | tf_op jit(solution)/shard_map/ppermute | solution.py:20
  8.3 11.2 %collective-permute-start.6 = (bf16[512,128]{1,0:T(8,128)(2,1)S(1)}, bf16[512,128]{1,0:T(8,128)(2,1)S(1)}, u32[]{:S(2)}, u32[]{:S(2)}) collective-permute-start(bf16[512,128]{1,0:T(8,128)(2,1)S(1)} %get-tuple-element.152), channel_id=1, source_target_pairs={{16,0},{24,8},{0,16},{8,24},{48,32},{56,40},{32,48},{40,56},{80,64... | collective-permute-start | bytes 393224 | tf_op jit(solution)/shard_map/ppermute | solution.py:20
  11.0 8.5 %collective-permute-start.7 = (bf16[512,128]{1,0:T(8,128)(2,1)S(1)}, bf16[512,128]{1,0:T(8,128)(2,1)S(1)}, u32[]{:S(2)}, u32[]{:S(2)}) collective-permute-start(bf16[512,128]{1,0:T(8,128)(2,1)S(1)} %get-tuple-element.152), channel_id=1, source_target_pairs={{24,0},{16,8},{8,16},{0,24},{56,32},{48,40},{40,48},{32,56},{88,64... | collective-permute-start | bytes 393224 | tf_op jit(solution)/shard_map/ppermute | solution.py:20
  16.1 13.1 %collective-permute-start.4 = (bf16[4,512,128]{2,1,0:T(8,128)(2,1)S(1)}, bf16[4,512,128]{2,1,0:T(8,128)(2,1)S(1)}, u32[]{:S(2)}, u32[]{:S(2)}) collective-permute-start(bf16[4,512,128]{2,1,0:T(8,128)(2,1)S(1)} %pad_maximum_fusion.refs_0_), channel_id=1, source_target_pairs={{8,0},{0,8},{24,16},{16,24},{40,32},{32,40},{56,48},{48,56},{72,64... | collective-permute-start | bytes 1572872 | tf_op jit(solution)/shard_map/ppermute | solution.py:20
  16.7 13.9 %collective-permute-start.5 = (bf16[4,512,128]{2,1,0:T(8,128)(2,1)S(1)}, bf16[4,512,128]{2,1,0:T(8,128)(2,1)S(1)}, u32[]{:S(2)}, u32[]{:S(2)}) collective-permute-start(bf16[4,512,128]{2,1,0:T(8,128)(2,1)S(1)} %pad_maximum_fusion.refs_0_), channel_id=1, source_target_pairs={{24,0},{16,8},{8,16},{0,24},{56,32},{48,40},{40,48},{32,56},{88,64... | collective-permute-start | bytes 1572872 | tf_op jit(solution)/shard_map/ppermute | solution.py:20
  19.5 15.2 %collective-permute-start.10 = (bf16[4,512,128]{2,1,0:T(8,128)(2,1)S(1)}, bf16[4,512,128]{2,1,0:T(8,128)(2,1)S(1)}, u32[]{:S(2)}, u32[]{:S(2)}) collective-permute-start(bf16[4,512,128]{2,1,0:T(8,128)(2,1)S(1)} %pad_maximum_fusion.1.refs_0_), channel_id=1, source_target_pairs={{32,0},{40,8},{48,16},{56,24},{0,32},{8,40},{16,48},{24,56},{96,64... | collective-permute-start | bytes 1572872 | tf_op jit(solution)/shard_map/ppermute | solution.py:20
  19.6 15.0 %collective-permute-start.11 = (bf16[4,512,128]{2,1,0:T(8,128)(2,1)S(1)}, bf16[4,512,128]{2,1,0:T(8,128)(2,1)S(1)}, u32[]{:S(2)}, u32[]{:S(2)}) collective-permute-start(bf16[4,512,128]{2,1,0:T(8,128)(2,1)S(1)} %pad_maximum_fusion.1.refs_0_), channel_id=1, source_target_pairs={{96,0},{104,8},{112,16},{120,24},{64,32},{72,40},{80,48},{88,56},{... | collective-permute-start | bytes 1572872 | tf_op jit(solution)/shard_map/ppermute | solution.py:20
  30.6 6.5 %collective-permute-start.8 = (bf16[2,512,128]{2,1,0:T(8,128)(2,1)S(1)}, bf16[2,512,128]{2,1,0:T(8,128)(2,1)S(1)}, u32[]{:S(2)}, u32[]{:S(2)}) collective-permute-start(bf16[2,512,128]{2,1,0:T(8,128)(2,1)S(1)} %slice.32), channel_id=1, source_target_pairs={{8,0},{0,8},{24,16},{16,24},{40,32},{32,40},{56,48},{48,56},{72,64... | collective-permute-start | bytes 786440 | tf_op jit(solution)/shard_map/ppermute | solution.py:20
  31.0 7.7 %collective-permute-start.9 = (bf16[2,512,128]{2,1,0:T(8,128)(2,1)S(1)}, bf16[2,512,128]{2,1,0:T(8,128)(2,1)S(1)}, u32[]{:S(2)}, u32[]{:S(2)}) collective-permute-start(bf16[2,512,128]{2,1,0:T(8,128)(2,1)S(1)} %slice.33), channel_id=1, source_target_pairs={{24,0},{16,8},{8,16},{0,24},{56,32},{48,40},{40,48},{32,56},{88,64... | collective-permute-start | bytes 786440 | tf_op jit(solution)/shard_map/ppermute | solution.py:20
  34.6 8.7 %collective-permute-start.12 = (bf16[2,512,128]{2,1,0:T(8,128)(2,1)S(1)}, bf16[2,512,128]{2,1,0:T(8,128)(2,1)S(1)}, u32[]{:S(2)}, u32[]{:S(2)}) collective-permute-start(bf16[2,512,128]{2,1,0:T(8,128)(2,1)S(1)} %slice.40), channel_id=1, source_target_pairs={{32,0},{40,8},{48,16},{56,24},{0,32},{8,40},{16,48},{24,56},{96,64... | collective-permute-start | bytes 786440 | tf_op jit(solution)/shard_map/ppermute | solution.py:20
  34.7 8.6 %collective-permute-start.13 = (bf16[2,512,128]{2,1,0:T(8,128)(2,1)S(1)}, bf16[2,512,128]{2,1,0:T(8,128)(2,1)S(1)}, u32[]{:S(2)}, u32[]{:S(2)}) collective-permute-start(bf16[2,512,128]{2,1,0:T(8,128)(2,1)S(1)} %slice.41), channel_id=1, source_target_pairs={{96,0},{104,8},{112,16},{120,24},{64,32},{72,40},{80,48},{88,56},{... | collective-permute-start | bytes 786440 | tf_op jit(solution)/shard_map/ppermute | solution.py:20
  43.2 6.1 %collective-permute-start.14 = (f32[256,3328]{1,0:T(8,128)S(1)}, f32[256,3328]{1,0:T(8,128)S(1)}, u32[]{:S(2)}, u32[]{:S(2)}) collective-permute-start(f32[256,3328]{1,0:T(8,128)S(1)} %project_other.2), channel_id=1, source_target_pairs={{1,0},{0,1},{3,2},{2,3},{5,4},{4,5},{7,6},{6,7},{9,8},{8,9},{11,10... | collective-permute-start | bytes 10223624 | tf_op jit(solution)/shard_map/ppermute | solution.py:28
  48.0 9.2 %collective-permute-start.17 = (f32[256,3328]{1,0:T(8,128)S(1)}, f32[256,3328]{1,0:T(8,128)S(1)}, u32[]{:S(2)}, u32[]{:S(2)}) collective-permute-start(f32[256,3328]{1,0:T(8,128)S(1)} %project_other.3), channel_id=1, source_target_pairs={{1,0},{0,1},{3,2},{2,3},{5,4},{4,5},{7,6},{6,7},{9,8},{8,9},{11,10... | collective-permute-start | bytes 10223624 | tf_op jit(solution)/shard_map/ppermute | solution.py:28
  53.3 12.7 %collective-permute-start.15 = (bf16[64,3328]{1,0:T(8,128)(2,1)S(1)}, bf16[64,3328]{1,0:T(8,128)(2,1)S(1)}, u32[]{:S(2)}, u32[]{:S(2)}) collective-permute-start(bf16[64,3328]{1,0:T(8,128)(2,1)S(1)} %get-tuple-element.96), channel_id=1, source_target_pairs={{2,0},{3,1},{0,2},{1,3},{6,4},{7,5},{4,6},{5,7},{10,8},{11,9},{8,1... | collective-permute-start | bytes 1277960 | tf_op jit(solution)/shard_map/ppermute | solution.py:24
  55.0 13.9 %collective-permute-start.16 = (bf16[64,3328]{1,0:T(8,128)(2,1)S(1)}, bf16[64,3328]{1,0:T(8,128)(2,1)S(1)}, u32[]{:S(2)}, u32[]{:S(2)}) collective-permute-start(bf16[64,3328]{1,0:T(8,128)(2,1)S(1)} %get-tuple-element.97), channel_id=1, source_target_pairs={{6,0},{7,1},{4,2},{5,3},{2,4},{3,5},{0,6},{1,7},{14,8},{15,9},{12,... | collective-permute-start | bytes 1277960 | tf_op jit(solution)/shard_map/ppermute | solution.py:24
  61.0 14.1 %collective-permute-start.20 = (bf16[64,3328]{1,0:T(8,128)(2,1)S(1)}, bf16[64,3328]{1,0:T(8,128)(2,1)S(1)}, u32[]{:S(2)}, u32[]{:S(2)}) collective-permute-start(bf16[64,3328]{1,0:T(8,128)(2,1)S(1)} %get-tuple-element.108), channel_id=1, source_target_pairs={{2,0},{3,1},{0,2},{1,3},{6,4},{7,5},{4,6},{5,7},{10,8},{11,9},{8,1... | collective-permute-start | bytes 1277960 | tf_op jit(solution)/shard_map/ppermute | solution.py:24
  61.8 16.2 %collective-permute-start.21 = (bf16[64,3328]{1,0:T(8,128)(2,1)S(1)}, bf16[64,3328]{1,0:T(8,128)(2,1)S(1)}, u32[]{:S(2)}, u32[]{:S(2)}) collective-permute-start(bf16[64,3328]{1,0:T(8,128)(2,1)S(1)} %get-tuple-element.109), channel_id=1, source_target_pairs={{6,0},{7,1},{4,2},{5,3},{2,4},{3,5},{0,6},{1,7},{14,8},{15,9},{12,... | collective-permute-start | bytes 1277960 | tf_op jit(solution)/shard_map/ppermute | solution.py:24
  69.0 11.5 %collective-permute-start.18 = (bf16[32,3328]{1,0:T(8,128)(2,1)S(1)}, bf16[32,3328]{1,0:T(8,128)(2,1)S(1)}, u32[]{:S(2)}, u32[]{:S(2)}) collective-permute-start(bf16[32,3328]{1,0:T(8,128)(2,1)S(1)} %get-tuple-element.104), channel_id=1, source_target_pairs={{2,0},{3,1},{0,2},{1,3},{6,4},{7,5},{4,6},{5,7},{10,8},{11,9},{8,1... | collective-permute-start | bytes 638984 | tf_op jit(solution)/shard_map/ppermute | solution.py:24
  69.0 13.5 %collective-permute-start.19 = (bf16[32,3328]{1,0:T(8,128)(2,1)S(1)}, bf16[32,3328]{1,0:T(8,128)(2,1)S(1)}, u32[]{:S(2)}, u32[]{:S(2)}) collective-permute-start(bf16[32,3328]{1,0:T(8,128)(2,1)S(1)} %get-tuple-element.105), channel_id=1, source_target_pairs={{6,0},{7,1},{4,2},{5,3},{2,4},{3,5},{0,6},{1,7},{14,8},{15,9},{12,... | collective-permute-start | bytes 638984 | tf_op jit(solution)/shard_map/ppermute | solution.py:24
  78.1 7.1 %collective-permute-start.24 = (bf16[32,3328]{1,0:T(8,128)(2,1)S(1)}, bf16[32,3328]{1,0:T(8,128)(2,1)S(1)}, u32[]{:S(2)}, u32[]{:S(2)}) collective-permute-start(bf16[32,3328]{1,0:T(8,128)(2,1)S(1)} %get-tuple-element.110), channel_id=1, source_target_pairs={{2,0},{3,1},{0,2},{1,3},{6,4},{7,5},{4,6},{5,7},{10,8},{11,9},{8,1... | collective-permute-start | bytes 638984 | tf_op jit(solution)/shard_map/ppermute | solution.py:24
  78.2 9.1 %collective-permute-start.25 = (bf16[32,3328]{1,0:T(8,128)(2,1)S(1)}, bf16[32,3328]{1,0:T(8,128)(2,1)S(1)}, u32[]{:S(2)}, u32[]{:S(2)}) collective-permute-start(bf16[32,3328]{1,0:T(8,128)(2,1)S(1)} %get-tuple-element.113), channel_id=1, source_target_pairs={{6,0},{7,1},{4,2},{5,3},{2,4},{3,5},{0,6},{1,7},{14,8},{15,9},{12,... | collective-permute-start | bytes 638984 | tf_op jit(solution)/shard_map/ppermute | solution.py:24
  82.8 7.3 %collective-permute-start.22 = (bf16[64,1664]{1,0:T(8,128)(2,1)S(1)}, bf16[64,1664]{1,0:T(8,128)(2,1)S(1)}, u32[]{:S(2)}, u32[]{:S(2)}) collective-permute-start(bf16[64,1664]{1,0:T(8,128)(2,1)S(1)} %hidden.2), channel_id=1, source_target_pairs={{2,0},{3,1},{0,2},{1,3},{6,4},{7,5},{4,6},{5,7},{10,8},{11,9},{8,1... | collective-permute-start | bytes 638984 | tf_op jit(solution)/shard_map/ppermute | solution.py:24
  82.9 9.5 %collective-permute-start.23 = (bf16[64,1664]{1,0:T(8,128)(2,1)S(1)}, bf16[64,1664]{1,0:T(8,128)(2,1)S(1)}, u32[]{:S(2)}, u32[]{:S(2)}) collective-permute-start(bf16[64,1664]{1,0:T(8,128)(2,1)S(1)} %hidden.2), channel_id=1, source_target_pairs={{6,0},{7,1},{4,2},{5,3},{2,4},{3,5},{0,6},{1,7},{14,8},{15,9},{12,... | collective-permute-start | bytes 638984 | tf_op jit(solution)/shard_map/ppermute | solution.py:24
  87.5 7.3 %collective-permute-start.26 = (bf16[64,1664]{1,0:T(8,128)(2,1)S(1)}, bf16[64,1664]{1,0:T(8,128)(2,1)S(1)}, u32[]{:S(2)}, u32[]{:S(2)}) collective-permute-start(bf16[64,1664]{1,0:T(8,128)(2,1)S(1)} %hidden.3), channel_id=1, source_target_pairs={{2,0},{3,1},{0,2},{1,3},{6,4},{7,5},{4,6},{5,7},{10,8},{11,9},{8,1... | collective-permute-start | bytes 638984 | tf_op jit(solution)/shard_map/ppermute | solution.py:24
  87.6 8.7 %collective-permute-start.27 = (bf16[64,1664]{1,0:T(8,128)(2,1)S(1)}, bf16[64,1664]{1,0:T(8,128)(2,1)S(1)}, u32[]{:S(2)}, u32[]{:S(2)}) collective-permute-start(bf16[64,1664]{1,0:T(8,128)(2,1)S(1)} %hidden.3), channel_id=1, source_target_pairs={{6,0},{7,1},{4,2},{5,3},{2,4},{3,5},{0,6},{1,7},{14,8},{15,9},{12,... | collective-permute-start | bytes 638984 | tf_op jit(solution)/shard_map/ppermute | solution.py:24
  92.4 4.8 %collective-permute-start.28 = (bf16[32,1664]{1,0:T(8,128)(2,1)S(1)}, bf16[32,1664]{1,0:T(8,128)(2,1)S(1)}, u32[]{:S(2)}, u32[]{:S(2)}) collective-permute-start(bf16[32,1664]{1,0:T(8,128)(2,1)S(1)} %slice.36), channel_id=1, source_target_pairs={{2,0},{3,1},{0,2},{1,3},{6,4},{7,5},{4,6},{5,7},{10,8},{11,9},{8,1... | collective-permute-start | bytes 319496 | tf_op jit(solution)/shard_map/ppermute | solution.py:24
  92.5 6.0 %collective-permute-start.29 = (bf16[32,1664]{1,0:T(8,128)(2,1)S(1)}, bf16[32,1664]{1,0:T(8,128)(2,1)S(1)}, u32[]{:S(2)}, u32[]{:S(2)}) collective-permute-start(bf16[32,1664]{1,0:T(8,128)(2,1)S(1)} %slice.37), channel_id=1, source_target_pairs={{6,0},{7,1},{4,2},{5,3},{2,4},{3,5},{0,6},{1,7},{14,8},{15,9},{12,... | collective-permute-start | bytes 319496 | tf_op jit(solution)/shard_map/ppermute | solution.py:24
  98.6 3.5 %collective-permute-start.30 = (bf16[256,1664]{1,0:T(8,128)(2,1)S(1)}, bf16[256,1664]{1,0:T(8,128)(2,1)S(1)}, u32[]{:S(2)}, u32[]{:S(2)}) collective-permute-start(bf16[256,1664]{1,0:T(8,128)(2,1)S(1)} %get-tuple-element.160), channel_id=1, source_target_pairs={{1,0},{0,1},{3,2},{2,3},{5,4},{4,5},{7,6},{6,7},{9,8},{8,9},{11,10... | collective-permute-start | bytes 2555912 | tf_op jit(solution)/shard_map/ppermute | solution.py:28
  98.8 8.2 %collective-permute-start.33 = (bf16[32,1664]{1,0:T(8,128)(2,1)S(1)}, bf16[32,1664]{1,0:T(8,128)(2,1)S(1)}, u32[]{:S(2)}, u32[]{:S(2)}) collective-permute-start(bf16[32,1664]{1,0:T(8,128)(2,1)S(1)} %slice.38), channel_id=1, source_target_pairs={{2,0},{3,1},{0,2},{1,3},{6,4},{7,5},{4,6},{5,7},{10,8},{11,9},{8,1... | collective-permute-start | bytes 319496 | tf_op jit(solution)/shard_map/ppermute | solution.py:24
  99.6 7.3 %collective-permute-start.34 = (bf16[32,1664]{1,0:T(8,128)(2,1)S(1)}, bf16[32,1664]{1,0:T(8,128)(2,1)S(1)}, u32[]{:S(2)}, u32[]{:S(2)}) collective-permute-start(bf16[32,1664]{1,0:T(8,128)(2,1)S(1)} %slice.39), channel_id=1, source_target_pairs={{6,0},{7,1},{4,2},{5,3},{2,4},{3,5},{0,6},{1,7},{14,8},{15,9},{12,... | collective-permute-start | bytes 319496 | tf_op jit(solution)/shard_map/ppermute | solution.py:24
  107.1 2.5 %collective-permute-start.35 = (bf16[256,1664]{1,0:T(8,128)(2,1)S(1)}, bf16[256,1664]{1,0:T(8,128)(2,1)S(1)}, u32[]{:S(2)}, u32[]{:S(2)}) collective-permute-start(bf16[256,1664]{1,0:T(8,128)(2,1)S(1)} %get-tuple-element.154), channel_id=1, source_target_pairs={{1,0},{0,1},{3,2},{2,3},{5,4},{4,5},{7,6},{6,7},{9,8},{8,9},{11,10... | collective-permute-start | bytes 2555912 | tf_op jit(solution)/shard_map/ppermute | solution.py:28
  107.2 14.3 %collective-permute-start.31 = (bf16[512,512]{1,0:T(8,128)(2,1)S(1)}, bf16[512,512]{1,0:T(8,128)(2,1)S(1)}, u32[]{:S(2)}, u32[]{:S(2)}) collective-permute-start(bf16[512,512]{1,0:T(8,128)(2,1)S(1)} %get-tuple-element.119), channel_id=1, source_target_pairs={{32,0},{40,8},{48,16},{56,24},{0,32},{8,40},{16,48},{24,56},{96,64... | collective-permute-start | bytes 1572872 | tf_op jit(solution)/shard_map/ppermute | solution.py:20
  107.3 15.4 %collective-permute-start.32 = (bf16[512,512]{1,0:T(8,128)(2,1)S(1)}, bf16[512,512]{1,0:T(8,128)(2,1)S(1)}, u32[]{:S(2)}, u32[]{:S(2)}) collective-permute-start(bf16[512,512]{1,0:T(8,128)(2,1)S(1)} %get-tuple-element.120), channel_id=1, source_target_pairs={{96,0},{104,8},{112,16},{120,24},{64,32},{72,40},{80,48},{88,56},{... | collective-permute-start | bytes 1572872 | tf_op jit(solution)/shard_map/ppermute | solution.py:20
  114.3 14.1 %collective-permute-start.38 = (bf16[512,512]{1,0:T(8,128)(2,1)S(1)}, bf16[512,512]{1,0:T(8,128)(2,1)S(1)}, u32[]{:S(2)}, u32[]{:S(2)}) collective-permute-start(bf16[512,512]{1,0:T(8,128)(2,1)S(1)} %get-tuple-element.134), channel_id=1, source_target_pairs={{8,0},{0,8},{24,16},{16,24},{40,32},{32,40},{56,48},{48,56},{72,64... | collective-permute-start | bytes 1572872 | tf_op jit(solution)/shard_map/ppermute | solution.py:20
  115.3 14.6 %collective-permute-start.39 = (bf16[512,512]{1,0:T(8,128)(2,1)S(1)}, bf16[512,512]{1,0:T(8,128)(2,1)S(1)}, u32[]{:S(2)}, u32[]{:S(2)}) collective-permute-start(bf16[512,512]{1,0:T(8,128)(2,1)S(1)} %get-tuple-element.135), channel_id=1, source_target_pairs={{24,0},{16,8},{8,16},{0,24},{56,32},{48,40},{40,48},{32,56},{88,64... | collective-permute-start | bytes 1572872 | tf_op jit(solution)/shard_map/ppermute | solution.py:20
  122.8 10.1 %collective-permute-start.36 = (bf16[256,512]{1,0:T(8,128)(2,1)S(1)}, bf16[256,512]{1,0:T(8,128)(2,1)S(1)}, u32[]{:S(2)}, u32[]{:S(2)}) collective-permute-start(bf16[256,512]{1,0:T(8,128)(2,1)S(1)} %get-tuple-element.130), channel_id=1, source_target_pairs={{32,0},{40,8},{48,16},{56,24},{0,32},{8,40},{16,48},{24,56},{96,64... | collective-permute-start | bytes 786440 | tf_op jit(solution)/shard_map/ppermute | solution.py:20
  123.4 9.4 %collective-permute-start.37 = (bf16[256,512]{1,0:T(8,128)(2,1)S(1)}, bf16[256,512]{1,0:T(8,128)(2,1)S(1)}, u32[]{:S(2)}, u32[]{:S(2)}) collective-permute-start(bf16[256,512]{1,0:T(8,128)(2,1)S(1)} %get-tuple-element.131), channel_id=1, source_target_pairs={{96,0},{104,8},{112,16},{120,24},{64,32},{72,40},{80,48},{88,56},{... | collective-permute-start | bytes 786440 | tf_op jit(solution)/shard_map/ppermute | solution.py:20
  130.1 11.2 %collective-permute-start.40 = (bf16[256,512]{1,0:T(8,128)(2,1)S(1)}, bf16[256,512]{1,0:T(8,128)(2,1)S(1)}, u32[]{:S(2)}, u32[]{:S(2)}) collective-permute-start(bf16[256,512]{1,0:T(8,128)(2,1)S(1)} %get-tuple-element.136), channel_id=1, source_target_pairs={{8,0},{0,8},{24,16},{16,24},{40,32},{32,40},{56,48},{48,56},{72,64... | collective-permute-start | bytes 786440 | tf_op jit(solution)/shard_map/ppermute | solution.py:20
  130.4 10.8 %collective-permute-start.41 = (bf16[256,512]{1,0:T(8,128)(2,1)S(1)}, bf16[256,512]{1,0:T(8,128)(2,1)S(1)}, u32[]{:S(2)}, u32[]{:S(2)}) collective-permute-start(bf16[256,512]{1,0:T(8,128)(2,1)S(1)} %get-tuple-element.140), channel_id=1, source_target_pairs={{24,0},{16,8},{8,16},{0,24},{56,32},{48,40},{40,48},{32,56},{88,64... | collective-permute-start | bytes 786440 | tf_op jit(solution)/shard_map/ppermute | solution.py:20
  133.1 8.2 %collective-permute-start.42 = (bf16[512,128]{1,0:T(8,128)(2,1)S(1)}, bf16[512,128]{1,0:T(8,128)(2,1)S(1)}, u32[]{:S(2)}, u32[]{:S(2)}) collective-permute-start(bf16[512,128]{1,0:T(8,128)(2,1)S(1)} %get-tuple-element.141), channel_id=1, source_target_pairs={{8,0},{0,8},{24,16},{16,24},{40,32},{32,40},{56,48},{48,56},{72,64... | collective-permute-start | bytes 393224 | tf_op jit(solution)/shard_map/ppermute | solution.py:20
  134.5 11.8 %collective-permute-start.43 = (bf16[512,128]{1,0:T(8,128)(2,1)S(1)}, bf16[512,128]{1,0:T(8,128)(2,1)S(1)}, u32[]{:S(2)}, u32[]{:S(2)}) collective-permute-start(bf16[512,128]{1,0:T(8,128)(2,1)S(1)} %get-tuple-element.143), channel_id=1, source_target_pairs={{16,0},{24,8},{0,16},{8,24},{48,32},{56,40},{32,48},{40,56},{80,64... | collective-permute-start | bytes 393224 | tf_op jit(solution)/shard_map/ppermute | solution.py:20
  136.1 10.1 %collective-permute-start.44 = (bf16[512,128]{1,0:T(8,128)(2,1)S(1)}, bf16[512,128]{1,0:T(8,128)(2,1)S(1)}, u32[]{:S(2)}, u32[]{:S(2)}) collective-permute-start(bf16[512,128]{1,0:T(8,128)(2,1)S(1)} %get-tuple-element.144), channel_id=1, source_target_pairs={{24,0},{16,8},{8,16},{0,24},{56,32},{48,40},{40,48},{32,56},{88,64... | collective-permute-start | bytes 393224 | tf_op jit(solution)/shard_map/ppermute | solution.py:20
  141.5 5.0 %collective-permute-start.45 = (bf16[512,128]{1,0:T(8,128)(2,1)S(1)}, bf16[512,128]{1,0:T(8,128)(2,1)S(1)}, u32[]{:S(2)}, u32[]{:S(2)}) collective-permute-start(bf16[512,128]{1,0:T(8,128)(2,1)S(1)} %get-tuple-element.148), channel_id=1, source_target_pairs={{32,0},{40,8},{48,16},{56,24},{0,32},{8,40},{16,48},{24,56},{96,64... | collective-permute-start | bytes 393224 | tf_op jit(solution)/shard_map/ppermute | solution.py:20
  142.3 7.2 %collective-permute-start.46 = (bf16[512,128]{1,0:T(8,128)(2,1)S(1)}, bf16[512,128]{1,0:T(8,128)(2,1)S(1)}, u32[]{:S(2)}, u32[]{:S(2)}) collective-permute-start(bf16[512,128]{1,0:T(8,128)(2,1)S(1)} %get-tuple-element.149), channel_id=1, source_target_pairs={{64,0},{72,8},{80,16},{88,24},{96,32},{104,40},{112,48},{120,56},{... | collective-permute-start | bytes 393224 | tf_op jit(solution)/shard_map/ppermute | solution.py:20
  145.2 6.2 %collective-permute-start.47 = (bf16[512,128]{1,0:T(8,128)(2,1)S(1)}, bf16[512,128]{1,0:T(8,128)(2,1)S(1)}, u32[]{:S(2)}, u32[]{:S(2)}) collective-permute-start(bf16[512,128]{1,0:T(8,128)(2,1)S(1)} %get-tuple-element.150), channel_id=1, source_target_pairs={{96,0},{104,8},{112,16},{120,24},{64,32},{72,40},{80,48},{88,56},{... | collective-permute-start | bytes 393224 | tf_op jit(solution)/shard_map/ppermute | solution.py:20

commit v2 on v1

--- a/solution.py
+++ b/solution.py
@@ -46,26 +46,32 @@
     )(*operands)
 
 
-def load_kernel(*refs):
-    count = len(refs) // 2
-    copies = [pltpu.make_async_copy(refs[i], refs[count + i], refs[-1].at[i]) for i in range(count)]
+def load_kernel(place, gate_hbm, up_hbm, down_hbm, gate, up, down, sem):
+    z, x = place[0], place[1]
+    copies = [pltpu.make_async_copy(gate_hbm, gate, sem.at[0]), pltpu.make_async_copy(up_hbm, up, sem.at[1])]
+    for dz in range(4):
+        for dx in range(4):
+            at = dz * 4 + dx
+            source = pl.ds(pl.multiple_of(((z ^ dz) * 4 + (x ^ dx)) * LANES, LANES), LANES)
+            target = slice(at * LANES, (at + 1) * LANES)
+            copies.append(pltpu.make_async_copy(down_hbm.at[:, source], down.at[:, target], sem.at[2 + at]))
     for copy in copies:
         copy.start()
     for copy in copies:
         copy.wait()
 
 
-def load(*arrays):
+def load(place, *weights):
     out = call(
         load_kernel,
         "load",
-        [pltpu.VMEM(a.shape, a.dtype) for a in arrays],
-        [HBM] * len(arrays),
-        [pltpu.with_memory_space_constraint(a, pltpu.HBM) for a in arrays],
-        scratch=[pltpu.SemaphoreType.DMA((len(arrays),))],
+        [pltpu.VMEM(w.shape, w.dtype) for w in weights],
+        [SMEM] + [HBM] * 3,
+        [place] + [pltpu.with_memory_space_constraint(w, pltpu.HBM) for w in weights],
+        scratch=[pltpu.SemaphoreType.DMA((18,))],
         micros=5,
     )
-    return [pltpu.with_memory_space_constraint(a, pltpu.VMEM) for a in out]
+    return [pltpu.with_memory_space_constraint(w, pltpu.VMEM) for w in out]
 
 
 def line_of(axis, rows):
@@ -192,17 +198,17 @@
     )
 
 
-def down_kernel(first, place, rows, down_weight, own, to_one, to_three, keep_one, keep_three):
-    z, x = place[0], place[1]
+def down_kernel(first, rows, down_weight, own, to_one, to_three, keep_one, keep_three):
     half = rows.shape[0] // 2
     for outer in (2, 1, 3, 0):
         for pair in (0, 2):
-            weights = []
-            for inner in (pair, pair + 1):
-                dz, dx = (outer, inner) if first == "z" else (inner, outer)
-                column = ((z ^ dz) * 4 + (x ^ dx)) * LANES
-                weights.append(down_weight[:, pl.ds(pl.multiple_of(column, LANES), LANES)])
-            term = jnp.dot(rows[...], jnp.concatenate(weights, axis=1), preferred_element_type=F32)
+            if first == "z":
+                at = outer * 4 + pair
+                weights = down_weight[:, at * LANES : (at + 2) * LANES]
+            else:
+                blocks = [pair * 4 + outer, (pair + 1) * 4 + outer]
+                weights = jnp.concatenate([down_weight[:, at * LANES : (at + 1) * LANES] for at in blocks], axis=1)
+            term = jnp.dot(rows[...], weights, preferred_element_type=F32)
             columns = slice(pair * LANES, (pair + 2) * LANES)
             if outer == 0:
                 own[:, columns] = term
@@ -217,7 +223,7 @@
                 to_three[half:, columns] = term[half:].astype(BF16)
 
 
-def down(first, place, rows, down_weight):
+def down(first, rows, down_weight):
     count = rows.shape[0]
     width = down_weight.shape[1] // 4
     shapes = [
@@ -228,8 +234,8 @@
         functools.partial(down_kernel, first),
         "down_" + first,
         shapes,
-        [SMEM, VMEM, VMEM],
-        [place, rows, down_weight],
+        [VMEM, VMEM],
+        [rows, down_weight],
         micros=4,
     )
 
@@ -284,7 +290,7 @@
     lines[0] = after(lines[0], lines[1][1])
     stacks = [jnp.stack(line) for line in lines]
     nexts = [[from_wide(axis, bits, stack) for bits in (1, 3)] for axis, stack in zip("xz", stacks)]
-    *weights, down_weight = load(*after((gate_weight, up_weight, down_weight), stacks))
+    *weights, down_weight = load(place, *after((gate_weight, up_weight, down_weight), stacks))
     nexts[0] = after(nexts[0], down_weight)
     bases = [assemble(axis, place, [stack, *near]) for axis, stack, near in zip("zx", stacks, nexts)]
     fars = [(from_wide(axis, 1, three[:2]), from_wide(axis, 3, one[2:])) for axis, (one, three) in zip("xz", nexts)]
@@ -322,7 +328,7 @@
         if at == 1:
             far[1] = after(second_round(from_y, (near[1][1][:half], near[1][0][half:])), parts[0][0])
         rows_here = jnp.concatenate([hidden[at], near[at][0], *far[at], near[at][1]])
-        parts.append(down(axis, place, jnp.concatenate([rows_here, swap(rows_here)]), down_weight))
+        parts.append(down(axis, jnp.concatenate([rows_here, swap(rows_here)]), down_weight))
     along = [functools.partial(from_wide, axis) for axis in "zx"]
     first = [first_round(exchange, p) for exchange, p in zip(along, parts)]
     second[0] = second_round(along[0], relay(parts[0], *after(first[0], parts[1][0])))
@@ -330,7 +336,7 @@
     second[0] = after(second[0], relayed[0])
     second[1] = second_round(along[1], relayed)
     final = send("x", add_line([parts[0][0], *first[0], *second[0]]))
-    second[1], final[1] = together((second[1], final[1]))
+    second[1] = after(second[1], relayed[0])
     return last(place, final + send("z", add_line([parts[1][0], *first[1], *second[1]])))
 
 

time: 153 us -> 151 us (0.987)
  waiting for transfers between devices: 51.5 us -> 49.5 us
    ppermute x28, waiting for transfers between devices: 27 us -> 25 us  [from_wide(): return lax.ppermute(array, 'wide', [(i ^ step, i) for i in range(16)])]
  transfers between devices with their start and end apart: 48 -> 48, of which waited for: 27 -> 28; matrix products, arithmetic and copies ran while one was open for 0% -> 0% of each run, Pallas kernels for 24% -> 24%
where the time goes in v2:
time: 151 us; the launch traced here: 150 us
  starting transfers between devices  61.3 us (41%)
  waiting for transfers between devices  49.5 us (33%)
  Pallas kernels  37.2 us (25%)
  local copies, waits for them, and re-layouts  1.65 us (1%)
    ppermute x28, starting transfers between devices, from_wide(): return lax.ppermute(array, 'wide', [(i ^ step, i) for i in range(16)])  40 us
    pallas_call x20, Pallas kernels, call(): pl.pallas_call(kernel, out_shape=out_shape, in_specs=in_specs, out_specs=...  37.2 us
    ppermute x28, waiting for transfers between devices, from_wide(): return lax.ppermute(array, 'wide', [(i ^ step, i) for i in range(16)])  25 us
    ppermute x16, waiting for transfers between devices, from_y(): return lax.ppermute(array, 'narrow', [(i ^ bits * 2, i) for i in range(8)])  23.6 us
    ppermute x16, starting transfers between devices, from_y(): return lax.ppermute(array, 'narrow', [(i ^ bits * 2, i) for i in range(8)])  20.3 us
  transfers between devices with their start and end apart: 48, of which 28 were waited for; matrix products, arithmetic and copies ran while one was open for 0% of the time, Pallas kernels for 24%

profile of v2, /device:TPU:0, one launch (start us, length us, event | category | flops | bytes accessed | tf_op | source)
XLA Modules:
  0.0 150.2 jit_solution(15125075730410249411)
XLA Ops:
  0.1 1.0 slice_bitcast_fusion
  1.1 1.7 %collective-permute-start.3 = (bf16[512,128]{1,0:T(8,128)(2,1)S(1)}, bf16[512,128]{1,0:T(8,128)(2,1)S(1)}, u32[]{:S(2)}, u32[]{:S(2)}) collective-permute-start(bf16[512,128]{1,0:T(8,128)(2,1)S(1)} %get-tuple-element.150), channel_id=1, source_target_pairs={{8,0},{0,8},{24,16},{16,24},{40,32},{32,40},{56,48},{48,56},{72,64... | collective-permute-start | bytes 393224 | tf_op jit(solution)/shard_map/ppermute | solution.py:20
  2.7 1.9 %collective-permute-start = (bf16[512,128]{1,0:T(8,128)(2,1)S(1)}, bf16[512,128]{1,0:T(8,128)(2,1)S(1)}, u32[]{:S(2)}, u32[]{:S(2)}) collective-permute-start(bf16[512,128]{1,0:T(8,128)(2,1)S(1)} %get-tuple-element.78), channel_id=1, source_target_pairs={{32,0},{40,8},{48,16},{56,24},{0,32},{8,40},{16,48},{24,56},{96,64... | collective-permute-start | bytes 393224 | tf_op jit(solution)/shard_map/ppermute | solution.py:20
  4.7 3.6 %collective-permute-start.1 = (bf16[512,128]{1,0:T(8,128)(2,1)S(1)}, bf16[512,128]{1,0:T(8,128)(2,1)S(1)}, u32[]{:S(2)}, u32[]{:S(2)}) collective-permute-start(bf16[512,128]{1,0:T(8,128)(2,1)S(1)} %get-tuple-element.78), channel_id=1, source_target_pairs={{64,0},{72,8},{80,16},{88,24},{96,32},{104,40},{112,48},{120,56},{... | collective-permute-start | bytes 393224 | tf_op jit(solution)/shard_map/ppermute | solution.py:20
  8.3 2.7 %collective-permute-start.6 = (bf16[512,128]{1,0:T(8,128)(2,1)S(1)}, bf16[512,128]{1,0:T(8,128)(2,1)S(1)}, u32[]{:S(2)}, u32[]{:S(2)}) collective-permute-start(bf16[512,128]{1,0:T(8,128)(2,1)S(1)} %get-tuple-element.150), channel_id=1, source_target_pairs={{16,0},{24,8},{0,16},{8,24},{48,32},{56,40},{32,48},{40,56},{80,64... | collective-permute-start | bytes 393224 | tf_op jit(solution)/shard_map/ppermute | solution.py:20
  11.5 2.6 %collective-permute-done.1 = bf16[512,128]{1,0:T(8,128)(2,1)S(1)} collective-permute-done((bf16[512,128]{1,0:T(8,128)(2,1)S(1)}, bf16[512,128]{1,0:T(8,128)(2,1)S(1)}, u32[]{:S(2)}, u32[]{:S(2)}) %collective-permute-start.1) | collective-permute-done | bytes 131104 | tf_op jit(solution)/shard_map/ppermute | solution.py:20
  14.1 1.9 %collective-permute-done.2 = bf16[512,128]{1,0:T(8,128)(2,1)S(1)} collective-permute-done((bf16[512,128]{1,0:T(8,128)(2,1)S(1)}, bf16[512,128]{1,0:T(8,128)(2,1)S(1)}, u32[]{:S(2)}, u32[]{:S(2)}) %collective-permute-start.2) | collective-permute-done | bytes 131104 | tf_op jit(solution)/shard_map/ppermute | solution.py:20
  16.7 2.8 %collective-permute-start.5 = (bf16[4,512,128]{2,1,0:T(8,128)(2,1)S(1)}, bf16[4,512,128]{2,1,0:T(8,128)(2,1)S(1)}, u32[]{:S(2)}, u32[]{:S(2)}) collective-permute-start(bf16[4,512,128]{2,1,0:T(8,128)(2,1)S(1)} %pad_maximum_fusion.refs_0_), channel_id=1, source_target_pairs={{24,0},{16,8},{8,16},{0,24},{56,32},{48,40},{40,48},{32,56},{88,64... | collective-permute-start | bytes 1572872 | tf_op jit(solution)/shard_map/ppermute | solution.py:20
  19.6 1.8 %collective-permute-start.11 = (bf16[4,512,128]{2,1,0:T(8,128)(2,1)S(1)}, bf16[4,512,128]{2,1,0:T(8,128)(2,1)S(1)}, u32[]{:S(2)}, u32[]{:S(2)}) collective-permute-start(bf16[4,512,128]{2,1,0:T(8,128)(2,1)S(1)} %pad_maximum_fusion.1.refs_0_), channel_id=1, source_target_pairs={{96,0},{104,8},{112,16},{120,24},{64,32},{72,40},{80,48},{88,56},{... | collective-permute-start | bytes 1572872 | tf_op jit(solution)/shard_map/ppermute | solution.py:20
  21.4 7.6 %load.1 = (bf16[2048,1664]{1,0:T(8,128)(2,1)S(1)}, bf16[2048,1664]{1,0:T(8,128)(2,1)S(1)}, bf16[1664,2048]{1,0:T(8,128)(2,1)S(1)}) custom-call(s32[4]{0:T(128)S(1)} %pad_add_fusion.place, bf16[2048,1664]{1,0:T(8,128)(2,1)} %gate_hbm, bf16[2048,1664]{1,0:T(8,128)(2,1)} %up_hbm, bf16[1664,2048]{1,0:T(8,128)(2,1)} %down_hbm), custom_call_target="tpu_custom_call" | custom-call | flops 5000000000 | tf_op jit(solution)/shard_map/load/pallas_call | solution.py:36
  29.1 1.5 collective-permute-done.5.refs_2_
  31.0 2.6 %collective-permute-start.9 = (bf16[2,512,128]{2,1,0:T(8,128)(2,1)S(1)}, bf16[2,512,128]{2,1,0:T(8,128)(2,1)S(1)}, u32[]{:S(2)}, u32[]{:S(2)}) collective-permute-start(bf16[2,512,128]{2,1,0:T(8,128)(2,1)S(1)} %slice.33), channel_id=1, source_target_pairs={{24,0},{16,8},{8,16},{0,24},{56,32},{48,40},{40,48},{32,56},{88,64... | collective-permute-start | bytes 786440 | tf_op jit(solution)/shard_map/ppermute | solution.py:20
  33.6 1.0 assemble_z.2.refs_0_
  34.7 0.9 collective-permute-start.13
  35.6 1.0 assemble_x.2.refs_0_
  37.1 1.6 %collective-permute-done.9.refs_2_ = bf16[2,512,128]{2,1,0:T(8,128)(2,1)S(1)} collective-permute-done((bf16[2,512,128]{2,1,0:T(8,128)(2,1)S(1)}, bf16[2,512,128]{2,1,0:T(8,128)(2,1)S(1)}, u32[]{:S(2)}, u32[]{:S(2)}) %collective-permute-start.9) | collective-permute-done | bytes 262176 | tf_op jit(solution)/shard_map/ppermute | solution.py:20
  38.7 0.7 assemble_z.3.rows
  39.4 3.9 %project_other.2 = f32[256,3328]{1,0:T(8,128)S(1)} custom-call(bf16[512,2048]{1,0:T(8,128)(2,1)S(1)} %assemble_z.3.rows, bf16[2048,1664]{1,0:T(8,128)(2,1)S(1)} %get-tuple-element.90.gate_weight, bf16[2048,1664]{1,0:T(8,128)(2,1)S(1)} %get-tuple-element.91.up_weight), custom_call_target="tpu_custom_call" | custom-call | flops 4000000000 | tf_op jit(solution)/shard_map/project_other/pallas_call | solution.py:36
  43.4 0.7 assemble_x.3.rows
  44.1 3.9 %project_other.3 = f32[256,3328]{1,0:T(8,128)S(1)} custom-call(bf16[512,2048]{1,0:T(8,128)(2,1)S(1)} %assemble_x.3.rows, bf16[2048,1664]{1,0:T(8,128)(2,1)S(1)} %get-tuple-element.90.gate_weight, bf16[2048,1664]{1,0:T(8,128)(2,1)S(1)} %get-tuple-element.91.up_weight), custom_call_target="tpu_custom_call" | custom-call | flops 4000000000 | tf_op jit(solution)/shard_map/project_other/pallas_call | solution.py:36
  48.0 0.7 collective-permute-start.17
  49.4 3.9 %project_own.2 = (f32[64,3328]{1,0:T(8,128)S(1)}, bf16[64,3328]{1,0:T(8,128)(2,1)S(1)}, bf16[64,3328]{1,0:T(8,128)(2,1)S(1)}, f32[32,3328]{1,0:T(8,128)S(1)}, f32[32,3328]{1,0:T(8,128)S(1)}) custom-call(bf16[512,2048]{1,0:T(8,128)(2,1)S(1)} %assemble_z.3.rows, bf16[2048,1664]{1,0:T(8,128)(2,1)S(1)} %get-tuple-element.90.gate_weight, ...), custom_call_target="tpu_custom_call" | custom-call | flops 4000000000 | tf_op jit(solution)/shard_map/project_own/pallas_call | solution.py:36
  53.3 1.7 %collective-permute-start.15 = (bf16[64,3328]{1,0:T(8,128)(2,1)S(1)}, bf16[64,3328]{1,0:T(8,128)(2,1)S(1)}, u32[]{:S(2)}, u32[]{:S(2)}) collective-permute-start(bf16[64,3328]{1,0:T(8,128)(2,1)S(1)} %get-tuple-element.95), channel_id=1, source_target_pairs={{2,0},{3,1},{0,2},{1,3},{6,4},{7,5},{4,6},{5,7},{10,8},{11,9},{8,1... | collective-permute-start | bytes 1277960 | tf_op jit(solution)/shard_map/ppermute | solution.py:24
  55.0 2.2 %collective-permute-start.16 = (bf16[64,3328]{1,0:T(8,128)(2,1)S(1)}, bf16[64,3328]{1,0:T(8,128)(2,1)S(1)}, u32[]{:S(2)}, u32[]{:S(2)}) collective-permute-start(bf16[64,3328]{1,0:T(8,128)(2,1)S(1)} %get-tuple-element.96), channel_id=1, source_target_pairs={{6,0},{7,1},{4,2},{5,3},{2,4},{3,5},{0,6},{1,7},{14,8},{15,9},{12,... | collective-permute-start | bytes 1277960 | tf_op jit(solution)/shard_map/ppermute | solution.py:24
  57.1 3.9 %project_own.3 = (f32[64,3328]{1,0:T(8,128)S(1)}, bf16[64,3328]{1,0:T(8,128)(2,1)S(1)}, bf16[64,3328]{1,0:T(8,128)(2,1)S(1)}, f32[32,3328]{1,0:T(8,128)S(1)}, f32[32,3328]{1,0:T(8,128)S(1)}) custom-call(bf16[512,2048]{1,0:T(8,128)(2,1)S(1)} %assemble_x.3.rows, bf16[2048,1664]{1,0:T(8,128)(2,1)S(1)} %get-tuple-element.90.gate_weight, ...), custom_call_target="tpu_custom_call" | custom-call | flops 4000000000 | tf_op jit(solution)/shard_map/project_own/pallas_call | solution.py:36
  61.0 0.8 collective-permute-start.20
  62.4 3.6 %collective-permute-done.15.from_one.refs_1_ = bf16[64,3328]{1,0:T(8,128)(2,1)S(1)} collective-permute-done((bf16[64,3328]{1,0:T(8,128)(2,1)S(1)}, bf16[64,3328]{1,0:T(8,128)(2,1)S(1)}, u32[]{:S(2)}, u32[]{:S(2)}) %collective-permute-start.15) | collective-permute-done | bytes 426016 | tf_op jit(solution)/shard_map/ppermute | solution.py:24
  66.0 2.8 %collective-permute-done.16.from_three.refs_2_ = bf16[64,3328]{1,0:T(8,128)(2,1)S(1)} collective-permute-done((bf16[64,3328]{1,0:T(8,128)(2,1)S(1)}, bf16[64,3328]{1,0:T(8,128)(2,1)S(1)}, u32[]{:S(2)}, u32[]{:S(2)}) %collective-permute-start.16) | collective-permute-done | bytes 426016 | tf_op jit(solution)/shard_map/ppermute | solution.py:24
  69.0 2.3 %collective-permute-start.19 = (bf16[32,3328]{1,0:T(8,128)(2,1)S(1)}, bf16[32,3328]{1,0:T(8,128)(2,1)S(1)}, u32[]{:S(2)}, u32[]{:S(2)}) collective-permute-start(bf16[32,3328]{1,0:T(8,128)(2,1)S(1)} %get-tuple-element.104), channel_id=1, source_target_pairs={{6,0},{7,1},{4,2},{5,3},{2,4},{3,5},{0,6},{1,7},{14,8},{15,9},{12,... | collective-permute-start | bytes 638984 | tf_op jit(solution)/shard_map/ppermute | solution.py:24
  71.3 3.9 %collective-permute-done.20.from_one.refs_1_ = bf16[64,3328]{1,0:T(8,128)(2,1)S(1)} collective-permute-done((bf16[64,3328]{1,0:T(8,128)(2,1)S(1)}, bf16[64,3328]{1,0:T(8,128)(2,1)S(1)}, u32[]{:S(2)}, u32[]{:S(2)}) %collective-permute-start.20) | collective-permute-done | bytes 426016 | tf_op jit(solution)/shard_map/ppermute | solution.py:24
  75.2 2.8 %collective-permute-done.21.from_three.refs_2_ = bf16[64,3328]{1,0:T(8,128)(2,1)S(1)} collective-permute-done((bf16[64,3328]{1,0:T(8,128)(2,1)S(1)}, bf16[64,3328]{1,0:T(8,128)(2,1)S(1)}, u32[]{:S(2)}, u32[]{:S(2)}) %collective-permute-start.21) | collective-permute-done | bytes 426016 | tf_op jit(solution)/shard_map/ppermute | solution.py:24
  78.2 2.3 %collective-permute-start.25 = (bf16[32,3328]{1,0:T(8,128)(2,1)S(1)}, bf16[32,3328]{1,0:T(8,128)(2,1)S(1)}, u32[]{:S(2)}, u32[]{:S(2)}) collective-permute-start(bf16[32,3328]{1,0:T(8,128)(2,1)S(1)} %get-tuple-element.112), channel_id=1, source_target_pairs={{6,0},{7,1},{4,2},{5,3},{2,4},{3,5},{0,6},{1,7},{14,8},{15,9},{12,... | collective-permute-start | bytes 638984 | tf_op jit(solution)/shard_map/ppermute | solution.py:24
  80.4 2.1 %collective-permute-done.19.refs_4_ = bf16[32,3328]{1,0:T(8,128)(2,1)S(1)} collective-permute-done((bf16[32,3328]{1,0:T(8,128)(2,1)S(1)}, bf16[32,3328]{1,0:T(8,128)(2,1)S(1)}, u32[]{:S(2)}, u32[]{:S(2)}) %collective-permute-start.19) | collective-permute-done | bytes 213024 | tf_op jit(solution)/shard_map/ppermute | solution.py:24
  82.9 2.3 %collective-permute-start.23 = (bf16[64,1664]{1,0:T(8,128)(2,1)S(1)}, bf16[64,1664]{1,0:T(8,128)(2,1)S(1)}, u32[]{:S(2)}, u32[]{:S(2)}) collective-permute-start(bf16[64,1664]{1,0:T(8,128)(2,1)S(1)} %hidden.2), channel_id=1, source_target_pairs={{6,0},{7,1},{4,2},{5,3},{2,4},{3,5},{0,6},{1,7},{14,8},{15,9},{12,... | collective-permute-start | bytes 638984 | tf_op jit(solution)/shard_map/ppermute | solution.py:24
  85.1 2.1 %collective-permute-done.25.refs_4_ = bf16[32,3328]{1,0:T(8,128)(2,1)S(1)} collective-permute-done((bf16[32,3328]{1,0:T(8,128)(2,1)S(1)}, bf16[32,3328]{1,0:T(8,128)(2,1)S(1)}, u32[]{:S(2)}, u32[]{:S(2)}) %collective-permute-start.25) | collective-permute-done | bytes 213024 | tf_op jit(solution)/shard_map/ppermute | solution.py:24
  87.6 2.3 %collective-permute-start.27 = (bf16[64,1664]{1,0:T(8,128)(2,1)S(1)}, bf16[64,1664]{1,0:T(8,128)(2,1)S(1)}, u32[]{:S(2)}, u32[]{:S(2)}) collective-permute-start(bf16[64,1664]{1,0:T(8,128)(2,1)S(1)} %hidden.3), channel_id=1, source_target_pairs={{6,0},{7,1},{4,2},{5,3},{2,4},{3,5},{0,6},{1,7},{14,8},{15,9},{12,... | collective-permute-start | bytes 638984 | tf_op jit(solution)/shard_map/ppermute | solution.py:24
  90.1 2.3 %collective-permute-done.23 = bf16[64,1664]{1,0:T(8,128)(2,1)S(1)} collective-permute-done((bf16[64,1664]{1,0:T(8,128)(2,1)S(1)}, bf16[64,1664]{1,0:T(8,128)(2,1)S(1)}, u32[]{:S(2)}, u32[]{:S(2)}) %collective-permute-start.23) | collective-permute-done | bytes 213024 | tf_op jit(solution)/shard_map/ppermute | solution.py:24
  92.5 2.3 %collective-permute-start.29 = (bf16[32,1664]{1,0:T(8,128)(2,1)S(1)}, bf16[32,1664]{1,0:T(8,128)(2,1)S(1)}, u32[]{:S(2)}, u32[]{:S(2)}) collective-permute-start(bf16[32,1664]{1,0:T(8,128)(2,1)S(1)} %slice.37), channel_id=1, source_target_pairs={{6,0},{7,1},{4,2},{5,3},{2,4},{3,5},{0,6},{1,7},{14,8},{15,9},{12,... | collective-permute-start | bytes 319496 | tf_op jit(solution)/shard_map/ppermute | solution.py:24
  94.8 1.4 collective-permute-done.27
  96.3 0.9 collective-permute-done.28
  97.2 1.4 collective-permute-done.29
  98.8 0.8 collective-permute-start.33
  99.6 2.5 %collective-permute-start.34 = (bf16[32,1664]{1,0:T(8,128)(2,1)S(1)}, bf16[32,1664]{1,0:T(8,128)(2,1)S(1)}, u32[]{:S(2)}, u32[]{:S(2)}) collective-permute-start(bf16[32,1664]{1,0:T(8,128)(2,1)S(1)} %slice.39), channel_id=1, source_target_pairs={{6,0},{7,1},{4,2},{5,3},{2,4},{3,5},{0,6},{1,7},{14,8},{15,9},{12,... | collective-permute-start | bytes 319496 | tf_op jit(solution)/shard_map/ppermute | solution.py:24
  102.3 4.0 %down_z.1 = (f32[512,512]{1,0:T(8,128)S(1)}, bf16[512,512]{1,0:T(8,128)(2,1)S(1)}, bf16[512,512]{1,0:T(8,128)(2,1)S(1)}, f32[256,512]{1,0:T(8,128)S(1)}, f32[256,512]{1,0:T(8,128)S(1)}) custom-call(bf16[512,1664]{1,0:T(8,128)(2,1)S(1)} %constant_dynamic-update-slice_fusion.5.rows, bf16[1664,2048]{1,0:T(8,128)(2,1)S(1)} %get-tuple-element.85.down_weight), custom_call_target="tpu_custom_call" | custom-call | flops 4000000000 | tf_op jit(solution)/shard_map/down_z/pallas_call | solution.py:36
  106.6 2.1 %collective-permute-start.32 = (bf16[512,512]{1,0:T(8,128)(2,1)S(1)}, bf16[512,512]{1,0:T(8,128)(2,1)S(1)}, u32[]{:S(2)}, u32[]{:S(2)}) collective-permute-start(bf16[512,512]{1,0:T(8,128)(2,1)S(1)} %get-tuple-element.119), channel_id=1, source_target_pairs={{96,0},{104,8},{112,16},{120,24},{64,32},{72,40},{80,48},{88,56},{... | collective-permute-start | bytes 1572872 | tf_op jit(solution)/shard_map/ppermute | solution.py:20
  109.0 4.1 %down_x.1 = (f32[512,512]{1,0:T(8,128)S(1)}, bf16[512,512]{1,0:T(8,128)(2,1)S(1)}, bf16[512,512]{1,0:T(8,128)(2,1)S(1)}, f32[256,512]{1,0:T(8,128)S(1)}, f32[256,512]{1,0:T(8,128)S(1)}) custom-call(bf16[512,1664]{1,0:T(8,128)(2,1)S(1)} %constant_dynamic-update-slice_fusion.16.rows, bf16[1664,2048]{1,0:T(8,128)(2,1)S(1)} %get-tuple-element.85.down_weight), custom_call_target="tpu_custom_call" | custom-call | flops 4000000000 | tf_op jit(solution)/shard_map/down_x/pallas_call | solution.py:36
  113.1 1.0 collective-permute-start.38
  114.1 2.3 %collective-permute-start.39 = (bf16[512,512]{1,0:T(8,128)(2,1)S(1)}, bf16[512,512]{1,0:T(8,128)(2,1)S(1)}, u32[]{:S(2)}, u32[]{:S(2)}) collective-permute-start(bf16[512,512]{1,0:T(8,128)(2,1)S(1)} %get-tuple-element.134), channel_id=1, source_target_pairs={{24,0},{16,8},{8,16},{0,24},{56,32},{48,40},{40,48},{32,56},{88,64... | collective-permute-start | bytes 1572872 | tf_op jit(solution)/shard_map/ppermute | solution.py:20
  116.5 4.4 %collective-permute-done.31.from_one = bf16[512,512]{1,0:T(8,128)(2,1)S(1)} collective-permute-done((bf16[512,512]{1,0:T(8,128)(2,1)S(1)}, bf16[512,512]{1,0:T(8,128)(2,1)S(1)}, u32[]{:S(2)}, u32[]{:S(2)}) %collective-permute-start.31) | collective-permute-done | bytes 524320 | tf_op jit(solution)/shard_map/ppermute | solution.py:20
  120.8 1.2 collective-permute-done.32.from_three
  122.8 2.0 %collective-permute-start.37 = (bf16[256,512]{1,0:T(8,128)(2,1)S(1)}, bf16[256,512]{1,0:T(8,128)(2,1)S(1)}, u32[]{:S(2)}, u32[]{:S(2)}) collective-permute-start(bf16[256,512]{1,0:T(8,128)(2,1)S(1)} %get-tuple-element.130), channel_id=1, source_target_pairs={{96,0},{104,8},{112,16},{120,24},{64,32},{72,40},{80,48},{88,56},{... | collective-permute-start | bytes 786440 | tf_op jit(solution)/shard_map/ppermute | solution.py:20
  124.7 2.4 %collective-permute-done.38.from_one = bf16[512,512]{1,0:T(8,128)(2,1)S(1)} collective-permute-done((bf16[512,512]{1,0:T(8,128)(2,1)S(1)}, bf16[512,512]{1,0:T(8,128)(2,1)S(1)}, u32[]{:S(2)}, u32[]{:S(2)}) %collective-permute-start.38) | collective-permute-done | bytes 524320 | tf_op jit(solution)/shard_map/ppermute | solution.py:20
  127.1 1.6 %collective-permute-done.39.from_three = bf16[512,512]{1,0:T(8,128)(2,1)S(1)} collective-permute-done((bf16[512,512]{1,0:T(8,128)(2,1)S(1)}, bf16[512,512]{1,0:T(8,128)(2,1)S(1)}, u32[]{:S(2)}, u32[]{:S(2)}) %collective-permute-start.39) | collective-permute-done | bytes 524320 | tf_op jit(solution)/shard_map/ppermute | solution.py:20
  129.2 2.4 %collective-permute-start.44 = (bf16[256,512]{1,0:T(8,128)(2,1)S(1)}, bf16[256,512]{1,0:T(8,128)(2,1)S(1)}, u32[]{:S(2)}, u32[]{:S(2)}) collective-permute-start(bf16[256,512]{1,0:T(8,128)(2,1)S(1)} %get-tuple-element.142), channel_id=1, source_target_pairs={{24,0},{16,8},{8,16},{0,24},{56,32},{48,40},{40,48},{32,56},{88,64... | collective-permute-start | bytes 786440 | tf_op jit(solution)/shard_map/ppermute | solution.py:20
  131.8 1.4 collective-permute-start.40
  133.2 2.3 %collective-permute-start.41 = (bf16[512,128]{1,0:T(8,128)(2,1)S(1)}, bf16[512,128]{1,0:T(8,128)(2,1)S(1)}, u32[]{:S(2)}, u32[]{:S(2)}) collective-permute-start(bf16[512,128]{1,0:T(8,128)(2,1)S(1)} %get-tuple-element.140), channel_id=1, source_target_pairs={{16,0},{24,8},{0,16},{8,24},{48,32},{56,40},{32,48},{40,56},{80,64... | collective-permute-start | bytes 393224 | tf_op jit(solution)/shard_map/ppermute | solution.py:20
  135.5 1.1 collective-permute-start.42
  136.6 1.6 %collective-permute-done.43.relay_one = bf16[256,512]{1,0:T(8,128)(2,1)S(1)} collective-permute-done((bf16[256,512]{1,0:T(8,128)(2,1)S(1)}, bf16[256,512]{1,0:T(8,128)(2,1)S(1)}, u32[]{:S(2)}, u32[]{:S(2)}) %collective-permute-start.43) | collective-permute-done | bytes 262176 | tf_op jit(solution)/shard_map/ppermute | solution.py:20
  138.1 0.9 collective-permute-done.44.relay_three
  139.3 3.4 %collective-permute-start.46 = (bf16[512,128]{1,0:T(8,128)(2,1)S(1)}, bf16[512,128]{1,0:T(8,128)(2,1)S(1)}, u32[]{:S(2)}, u32[]{:S(2)}) collective-permute-start(bf16[512,128]{1,0:T(8,128)(2,1)S(1)} %get-tuple-element.147), channel_id=1, source_target_pairs={{64,0},{72,8},{80,16},{88,24},{96,32},{104,40},{112,48},{120,56},{... | collective-permute-start | bytes 393224 | tf_op jit(solution)/shard_map/ppermute | solution.py:20
  142.7 1.3 collective-permute-start.47
  144.2 2.8 %collective-permute-done.46.refs_6_ = bf16[512,128]{1,0:T(8,128)(2,1)S(1)} collective-permute-done((bf16[512,128]{1,0:T(8,128)(2,1)S(1)}, bf16[512,128]{1,0:T(8,128)(2,1)S(1)}, u32[]{:S(2)}, u32[]{:S(2)}) %collective-permute-start.46) | collective-permute-done | bytes 131104 | tf_op jit(solution)/shard_map/ppermute | solution.py:20
  147.0 1.8 %collective-permute-done.47.refs_7_ = bf16[512,128]{1,0:T(8,128)(2,1)S(1)} collective-permute-done((bf16[512,128]{1,0:T(8,128)(2,1)S(1)}, bf16[512,128]{1,0:T(8,128)(2,1)S(1)}, u32[]{:S(2)}, u32[]{:S(2)}) %collective-permute-start.47) | collective-permute-done | bytes 131104 | tf_op jit(solution)/shard_map/ppermute | solution.py:20
  148.8 1.4 last.1
  (76 shorter events, 8.0 us)
Async XLA Ops:
  1.1 9.9 %collective-permute-start.3 = (bf16[512,128]{1,0:T(8,128)(2,1)S(1)}, bf16[512,128]{1,0:T(8,128)(2,1)S(1)}, u32[]{:S(2)}, u32[]{:S(2)}) collective-permute-start(bf16[512,128]{1,0:T(8,128)(2,1)S(1)} %get-tuple-element.150), channel_id=1, source_target_pairs={{8,0},{0,8},{24,16},{16,24},{40,32},{32,40},{56,48},{48,56},{72,64... | collective-permute-start | bytes 393224 | tf_op jit(solution)/shard_map/ppermute | solution.py:20
  2.7 8.7 %collective-permute-start = (bf16[512,128]{1,0:T(8,128)(2,1)S(1)}, bf16[512,128]{1,0:T(8,128)(2,1)S(1)}, u32[]{:S(2)}, u32[]{:S(2)}) collective-permute-start(bf16[512,128]{1,0:T(8,128)(2,1)S(1)} %get-tuple-element.78), channel_id=1, source_target_pairs={{32,0},{40,8},{48,16},{56,24},{0,32},{8,40},{16,48},{24,56},{96,64... | collective-permute-start | bytes 393224 | tf_op jit(solution)/shard_map/ppermute | solution.py:20
  4.7 9.4 %collective-permute-start.1 = (bf16[512,128]{1,0:T(8,128)(2,1)S(1)}, bf16[512,128]{1,0:T(8,128)(2,1)S(1)}, u32[]{:S(2)}, u32[]{:S(2)}) collective-permute-start(bf16[512,128]{1,0:T(8,128)(2,1)S(1)} %get-tuple-element.78), channel_id=1, source_target_pairs={{64,0},{72,8},{80,16},{88,24},{96,32},{104,40},{112,48},{120,56},{... | collective-permute-start | bytes 393224 | tf_op jit(solution)/shard_map/ppermute | solution.py:20
  8.2 7.7 %collective-permute-start.2 = (bf16[512,128]{1,0:T(8,128)(2,1)S(1)}, bf16[512,128]{1,0:T(8,128)(2,1)S(1)}, u32[]{:S(2)}, u32[]{:S(2)}) collective-permute-start(bf16[512,128]{1,0:T(8,128)(2,1)S(1)} %get-tuple-element.78), channel_id=1, source_target_pairs={{96,0},{104,8},{112,16},{120,24},{64,32},{72,40},{80,48},{88,56},{... | collective-permute-start | bytes 393224 | tf_op jit(solution)/shard_map/ppermute | solution.py:20
  8.3 11.2 %collective-permute-start.6 = (bf16[512,128]{1,0:T(8,128)(2,1)S(1)}, bf16[512,128]{1,0:T(8,128)(2,1)S(1)}, u32[]{:S(2)}, u32[]{:S(2)}) collective-permute-start(bf16[512,128]{1,0:T(8,128)(2,1)S(1)} %get-tuple-element.150), channel_id=1, source_target_pairs={{16,0},{24,8},{0,16},{8,24},{48,32},{56,40},{32,48},{40,56},{80,64... | collective-permute-start | bytes 393224 | tf_op jit(solution)/shard_map/ppermute | solution.py:20
  11.0 8.5 %collective-permute-start.7 = (bf16[512,128]{1,0:T(8,128)(2,1)S(1)}, bf16[512,128]{1,0:T(8,128)(2,1)S(1)}, u32[]{:S(2)}, u32[]{:S(2)}) collective-permute-start(bf16[512,128]{1,0:T(8,128)(2,1)S(1)} %get-tuple-element.150), channel_id=1, source_target_pairs={{24,0},{16,8},{8,16},{0,24},{56,32},{48,40},{40,48},{32,56},{88,64... | collective-permute-start | bytes 393224 | tf_op jit(solution)/shard_map/ppermute | solution.py:20
  16.1 13.1 %collective-permute-start.4 = (bf16[4,512,128]{2,1,0:T(8,128)(2,1)S(1)}, bf16[4,512,128]{2,1,0:T(8,128)(2,1)S(1)}, u32[]{:S(2)}, u32[]{:S(2)}) collective-permute-start(bf16[4,512,128]{2,1,0:T(8,128)(2,1)S(1)} %pad_maximum_fusion.refs_0_), channel_id=1, source_target_pairs={{8,0},{0,8},{24,16},{16,24},{40,32},{32,40},{56,48},{48,56},{72,64... | collective-permute-start | bytes 1572872 | tf_op jit(solution)/shard_map/ppermute | solution.py:20
  16.7 13.9 %collective-permute-start.5 = (bf16[4,512,128]{2,1,0:T(8,128)(2,1)S(1)}, bf16[4,512,128]{2,1,0:T(8,128)(2,1)S(1)}, u32[]{:S(2)}, u32[]{:S(2)}) collective-permute-start(bf16[4,512,128]{2,1,0:T(8,128)(2,1)S(1)} %pad_maximum_fusion.refs_0_), channel_id=1, source_target_pairs={{24,0},{16,8},{8,16},{0,24},{56,32},{48,40},{40,48},{32,56},{88,64... | collective-permute-start | bytes 1572872 | tf_op jit(solution)/shard_map/ppermute | solution.py:20
  19.5 15.2 %collective-permute-start.10 = (bf16[4,512,128]{2,1,0:T(8,128)(2,1)S(1)}, bf16[4,512,128]{2,1,0:T(8,128)(2,1)S(1)}, u32[]{:S(2)}, u32[]{:S(2)}) collective-permute-start(bf16[4,512,128]{2,1,0:T(8,128)(2,1)S(1)} %pad_maximum_fusion.1.refs_0_), channel_id=1, source_target_pairs={{32,0},{40,8},{48,16},{56,24},{0,32},{8,40},{16,48},{24,56},{96,64... | collective-permute-start | bytes 1572872 | tf_op jit(solution)/shard_map/ppermute | solution.py:20
  19.6 15.0 %collective-permute-start.11 = (bf16[4,512,128]{2,1,0:T(8,128)(2,1)S(1)}, bf16[4,512,128]{2,1,0:T(8,128)(2,1)S(1)}, u32[]{:S(2)}, u32[]{:S(2)}) collective-permute-start(bf16[4,512,128]{2,1,0:T(8,128)(2,1)S(1)} %pad_maximum_fusion.1.refs_0_), channel_id=1, source_target_pairs={{96,0},{104,8},{112,16},{120,24},{64,32},{72,40},{80,48},{88,56},{... | collective-permute-start | bytes 1572872 | tf_op jit(solution)/shard_map/ppermute | solution.py:20
  30.6 6.5 %collective-permute-start.8 = (bf16[2,512,128]{2,1,0:T(8,128)(2,1)S(1)}, bf16[2,512,128]{2,1,0:T(8,128)(2,1)S(1)}, u32[]{:S(2)}, u32[]{:S(2)}) collective-permute-start(bf16[2,512,128]{2,1,0:T(8,128)(2,1)S(1)} %slice.32), channel_id=1, source_target_pairs={{8,0},{0,8},{24,16},{16,24},{40,32},{32,40},{56,48},{48,56},{72,64... | collective-permute-start | bytes 786440 | tf_op jit(solution)/shard_map/ppermute | solution.py:20
  31.0 7.7 %collective-permute-start.9 = (bf16[2,512,128]{2,1,0:T(8,128)(2,1)S(1)}, bf16[2,512,128]{2,1,0:T(8,128)(2,1)S(1)}, u32[]{:S(2)}, u32[]{:S(2)}) collective-permute-start(bf16[2,512,128]{2,1,0:T(8,128)(2,1)S(1)} %slice.33), channel_id=1, source_target_pairs={{24,0},{16,8},{8,16},{0,24},{56,32},{48,40},{40,48},{32,56},{88,64... | collective-permute-start | bytes 786440 | tf_op jit(solution)/shard_map/ppermute | solution.py:20
  34.6 8.7 %collective-permute-start.12 = (bf16[2,512,128]{2,1,0:T(8,128)(2,1)S(1)}, bf16[2,512,128]{2,1,0:T(8,128)(2,1)S(1)}, u32[]{:S(2)}, u32[]{:S(2)}) collective-permute-start(bf16[2,512,128]{2,1,0:T(8,128)(2,1)S(1)} %slice.40), channel_id=1, source_target_pairs={{32,0},{40,8},{48,16},{56,24},{0,32},{8,40},{16,48},{24,56},{96,64... | collective-permute-start | bytes 786440 | tf_op jit(solution)/shard_map/ppermute | solution.py:20
  34.7 8.6 %collective-permute-start.13 = (bf16[2,512,128]{2,1,0:T(8,128)(2,1)S(1)}, bf16[2,512,128]{2,1,0:T(8,128)(2,1)S(1)}, u32[]{:S(2)}, u32[]{:S(2)}) collective-permute-start(bf16[2,512,128]{2,1,0:T(8,128)(2,1)S(1)} %slice.41), channel_id=1, source_target_pairs={{96,0},{104,8},{112,16},{120,24},{64,32},{72,40},{80,48},{88,56},{... | collective-permute-start | bytes 786440 | tf_op jit(solution)/shard_map/ppermute | solution.py:20
  43.2 6.1 %collective-permute-start.14 = (f32[256,3328]{1,0:T(8,128)S(1)}, f32[256,3328]{1,0:T(8,128)S(1)}, u32[]{:S(2)}, u32[]{:S(2)}) collective-permute-start(f32[256,3328]{1,0:T(8,128)S(1)} %project_other.2), channel_id=1, source_target_pairs={{1,0},{0,1},{3,2},{2,3},{5,4},{4,5},{7,6},{6,7},{9,8},{8,9},{11,10... | collective-permute-start | bytes 10223624 | tf_op jit(solution)/shard_map/ppermute | solution.py:28
  48.0 9.2 %collective-permute-start.17 = (f32[256,3328]{1,0:T(8,128)S(1)}, f32[256,3328]{1,0:T(8,128)S(1)}, u32[]{:S(2)}, u32[]{:S(2)}) collective-permute-start(f32[256,3328]{1,0:T(8,128)S(1)} %project_other.3), channel_id=1, source_target_pairs={{1,0},{0,1},{3,2},{2,3},{5,4},{4,5},{7,6},{6,7},{9,8},{8,9},{11,10... | collective-permute-start | bytes 10223624 | tf_op jit(solution)/shard_map/ppermute | solution.py:28
  53.3 12.7 %collective-permute-start.15 = (bf16[64,3328]{1,0:T(8,128)(2,1)S(1)}, bf16[64,3328]{1,0:T(8,128)(2,1)S(1)}, u32[]{:S(2)}, u32[]{:S(2)}) collective-permute-start(bf16[64,3328]{1,0:T(8,128)(2,1)S(1)} %get-tuple-element.95), channel_id=1, source_target_pairs={{2,0},{3,1},{0,2},{1,3},{6,4},{7,5},{4,6},{5,7},{10,8},{11,9},{8,1... | collective-permute-start | bytes 1277960 | tf_op jit(solution)/shard_map/ppermute | solution.py:24
  55.0 13.9 %collective-permute-start.16 = (bf16[64,3328]{1,0:T(8,128)(2,1)S(1)}, bf16[64,3328]{1,0:T(8,128)(2,1)S(1)}, u32[]{:S(2)}, u32[]{:S(2)}) collective-permute-start(bf16[64,3328]{1,0:T(8,128)(2,1)S(1)} %get-tuple-element.96), channel_id=1, source_target_pairs={{6,0},{7,1},{4,2},{5,3},{2,4},{3,5},{0,6},{1,7},{14,8},{15,9},{12,... | collective-permute-start | bytes 1277960 | tf_op jit(solution)/shard_map/ppermute | solution.py:24
  61.0 14.1 %collective-permute-start.20 = (bf16[64,3328]{1,0:T(8,128)(2,1)S(1)}, bf16[64,3328]{1,0:T(8,128)(2,1)S(1)}, u32[]{:S(2)}, u32[]{:S(2)}) collective-permute-start(bf16[64,3328]{1,0:T(8,128)(2,1)S(1)} %get-tuple-element.107), channel_id=1, source_target_pairs={{2,0},{3,1},{0,2},{1,3},{6,4},{7,5},{4,6},{5,7},{10,8},{11,9},{8,1... | collective-permute-start | bytes 1277960 | tf_op jit(solution)/shard_map/ppermute | solution.py:24
  61.8 16.2 %collective-permute-start.21 = (bf16[64,3328]{1,0:T(8,128)(2,1)S(1)}, bf16[64,3328]{1,0:T(8,128)(2,1)S(1)}, u32[]{:S(2)}, u32[]{:S(2)}) collective-permute-start(bf16[64,3328]{1,0:T(8,128)(2,1)S(1)} %get-tuple-element.108), channel_id=1, source_target_pairs={{6,0},{7,1},{4,2},{5,3},{2,4},{3,5},{0,6},{1,7},{14,8},{15,9},{12,... | collective-permute-start | bytes 1277960 | tf_op jit(solution)/shard_map/ppermute | solution.py:24
  69.0 11.5 %collective-permute-start.18 = (bf16[32,3328]{1,0:T(8,128)(2,1)S(1)}, bf16[32,3328]{1,0:T(8,128)(2,1)S(1)}, u32[]{:S(2)}, u32[]{:S(2)}) collective-permute-start(bf16[32,3328]{1,0:T(8,128)(2,1)S(1)} %get-tuple-element.103), channel_id=1, source_target_pairs={{2,0},{3,1},{0,2},{1,3},{6,4},{7,5},{4,6},{5,7},{10,8},{11,9},{8,1... | collective-permute-start | bytes 638984 | tf_op jit(solution)/shard_map/ppermute | solution.py:24
  69.0 13.5 %collective-permute-start.19 = (bf16[32,3328]{1,0:T(8,128)(2,1)S(1)}, bf16[32,3328]{1,0:T(8,128)(2,1)S(1)}, u32[]{:S(2)}, u32[]{:S(2)}) collective-permute-start(bf16[32,3328]{1,0:T(8,128)(2,1)S(1)} %get-tuple-element.104), channel_id=1, source_target_pairs={{6,0},{7,1},{4,2},{5,3},{2,4},{3,5},{0,6},{1,7},{14,8},{15,9},{12,... | collective-permute-start | bytes 638984 | tf_op jit(solution)/shard_map/ppermute | solution.py:24
  78.1 7.1 %collective-permute-start.24 = (bf16[32,3328]{1,0:T(8,128)(2,1)S(1)}, bf16[32,3328]{1,0:T(8,128)(2,1)S(1)}, u32[]{:S(2)}, u32[]{:S(2)}) collective-permute-start(bf16[32,3328]{1,0:T(8,128)(2,1)S(1)} %get-tuple-element.109), channel_id=1, source_target_pairs={{2,0},{3,1},{0,2},{1,3},{6,4},{7,5},{4,6},{5,7},{10,8},{11,9},{8,1... | collective-permute-start | bytes 638984 | tf_op jit(solution)/shard_map/ppermute | solution.py:24
  78.2 9.1 %collective-permute-start.25 = (bf16[32,3328]{1,0:T(8,128)(2,1)S(1)}, bf16[32,3328]{1,0:T(8,128)(2,1)S(1)}, u32[]{:S(2)}, u32[]{:S(2)}) collective-permute-start(bf16[32,3328]{1,0:T(8,128)(2,1)S(1)} %get-tuple-element.112), channel_id=1, source_target_pairs={{6,0},{7,1},{4,2},{5,3},{2,4},{3,5},{0,6},{1,7},{14,8},{15,9},{12,... | collective-permute-start | bytes 638984 | tf_op jit(solution)/shard_map/ppermute | solution.py:24
  82.8 7.3 %collective-permute-start.22 = (bf16[64,1664]{1,0:T(8,128)(2,1)S(1)}, bf16[64,1664]{1,0:T(8,128)(2,1)S(1)}, u32[]{:S(2)}, u32[]{:S(2)}) collective-permute-start(bf16[64,1664]{1,0:T(8,128)(2,1)S(1)} %hidden.2), channel_id=1, source_target_pairs={{2,0},{3,1},{0,2},{1,3},{6,4},{7,5},{4,6},{5,7},{10,8},{11,9},{8,1... | collective-permute-start | bytes 638984 | tf_op jit(solution)/shard_map/ppermute | solution.py:24
  82.9 9.5 %collective-permute-start.23 = (bf16[64,1664]{1,0:T(8,128)(2,1)S(1)}, bf16[64,1664]{1,0:T(8,128)(2,1)S(1)}, u32[]{:S(2)}, u32[]{:S(2)}) collective-permute-start(bf16[64,1664]{1,0:T(8,128)(2,1)S(1)} %hidden.2), channel_id=1, source_target_pairs={{6,0},{7,1},{4,2},{5,3},{2,4},{3,5},{0,6},{1,7},{14,8},{15,9},{12,... | collective-permute-start | bytes 638984 | tf_op jit(solution)/shard_map/ppermute | solution.py:24
  87.5 7.3 %collective-permute-start.26 = (bf16[64,1664]{1,0:T(8,128)(2,1)S(1)}, bf16[64,1664]{1,0:T(8,128)(2,1)S(1)}, u32[]{:S(2)}, u32[]{:S(2)}) collective-permute-start(bf16[64,1664]{1,0:T(8,128)(2,1)S(1)} %hidden.3), channel_id=1, source_target_pairs={{2,0},{3,1},{0,2},{1,3},{6,4},{7,5},{4,6},{5,7},{10,8},{11,9},{8,1... | collective-permute-start | bytes 638984 | tf_op jit(solution)/shard_map/ppermute | solution.py:24
  87.6 8.7 %collective-permute-start.27 = (bf16[64,1664]{1,0:T(8,128)(2,1)S(1)}, bf16[64,1664]{1,0:T(8,128)(2,1)S(1)}, u32[]{:S(2)}, u32[]{:S(2)}) collective-permute-start(bf16[64,1664]{1,0:T(8,128)(2,1)S(1)} %hidden.3), channel_id=1, source_target_pairs={{6,0},{7,1},{4,2},{5,3},{2,4},{3,5},{0,6},{1,7},{14,8},{15,9},{12,... | collective-permute-start | bytes 638984 | tf_op jit(solution)/shard_map/ppermute | solution.py:24
  92.4 4.8 %collective-permute-start.28 = (bf16[32,1664]{1,0:T(8,128)(2,1)S(1)}, bf16[32,1664]{1,0:T(8,128)(2,1)S(1)}, u32[]{:S(2)}, u32[]{:S(2)}) collective-permute-start(bf16[32,1664]{1,0:T(8,128)(2,1)S(1)} %slice.36), channel_id=1, source_target_pairs={{2,0},{3,1},{0,2},{1,3},{6,4},{7,5},{4,6},{5,7},{10,8},{11,9},{8,1... | collective-permute-start | bytes 319496 | tf_op jit(solution)/shard_map/ppermute | solution.py:24
  92.5 6.0 %collective-permute-start.29 = (bf16[32,1664]{1,0:T(8,128)(2,1)S(1)}, bf16[32,1664]{1,0:T(8,128)(2,1)S(1)}, u32[]{:S(2)}, u32[]{:S(2)}) collective-permute-start(bf16[32,1664]{1,0:T(8,128)(2,1)S(1)} %slice.37), channel_id=1, source_target_pairs={{6,0},{7,1},{4,2},{5,3},{2,4},{3,5},{0,6},{1,7},{14,8},{15,9},{12,... | collective-permute-start | bytes 319496 | tf_op jit(solution)/shard_map/ppermute | solution.py:24
  98.6 3.5 %collective-permute-start.30 = (bf16[256,1664]{1,0:T(8,128)(2,1)S(1)}, bf16[256,1664]{1,0:T(8,128)(2,1)S(1)}, u32[]{:S(2)}, u32[]{:S(2)}) collective-permute-start(bf16[256,1664]{1,0:T(8,128)(2,1)S(1)} %get-tuple-element.158), channel_id=1, source_target_pairs={{1,0},{0,1},{3,2},{2,3},{5,4},{4,5},{7,6},{6,7},{9,8},{8,9},{11,10... | collective-permute-start | bytes 2555912 | tf_op jit(solution)/shard_map/ppermute | solution.py:28
  98.8 7.5 %collective-permute-start.33 = (bf16[32,1664]{1,0:T(8,128)(2,1)S(1)}, bf16[32,1664]{1,0:T(8,128)(2,1)S(1)}, u32[]{:S(2)}, u32[]{:S(2)}) collective-permute-start(bf16[32,1664]{1,0:T(8,128)(2,1)S(1)} %slice.38), channel_id=1, source_target_pairs={{2,0},{3,1},{0,2},{1,3},{6,4},{7,5},{4,6},{5,7},{10,8},{11,9},{8,1... | collective-permute-start | bytes 319496 | tf_op jit(solution)/shard_map/ppermute | solution.py:24
  99.6 6.7 %collective-permute-start.34 = (bf16[32,1664]{1,0:T(8,128)(2,1)S(1)}, bf16[32,1664]{1,0:T(8,128)(2,1)S(1)}, u32[]{:S(2)}, u32[]{:S(2)}) collective-permute-start(bf16[32,1664]{1,0:T(8,128)(2,1)S(1)} %slice.39), channel_id=1, source_target_pairs={{6,0},{7,1},{4,2},{5,3},{2,4},{3,5},{0,6},{1,7},{14,8},{15,9},{12,... | collective-permute-start | bytes 319496 | tf_op jit(solution)/shard_map/ppermute | solution.py:24
  106.4 2.5 %collective-permute-start.35 = (bf16[256,1664]{1,0:T(8,128)(2,1)S(1)}, bf16[256,1664]{1,0:T(8,128)(2,1)S(1)}, u32[]{:S(2)}, u32[]{:S(2)}) collective-permute-start(bf16[256,1664]{1,0:T(8,128)(2,1)S(1)} %get-tuple-element.152), channel_id=1, source_target_pairs={{1,0},{0,1},{3,2},{2,3},{5,4},{4,5},{7,6},{6,7},{9,8},{8,9},{11,10... | collective-permute-start | bytes 2555912 | tf_op jit(solution)/shard_map/ppermute | solution.py:28
  106.5 14.3 %collective-permute-start.31 = (bf16[512,512]{1,0:T(8,128)(2,1)S(1)}, bf16[512,512]{1,0:T(8,128)(2,1)S(1)}, u32[]{:S(2)}, u32[]{:S(2)}) collective-permute-start(bf16[512,512]{1,0:T(8,128)(2,1)S(1)} %get-tuple-element.118), channel_id=1, source_target_pairs={{32,0},{40,8},{48,16},{56,24},{0,32},{8,40},{16,48},{24,56},{96,64... | collective-permute-start | bytes 1572872 | tf_op jit(solution)/shard_map/ppermute | solution.py:20
  106.6 15.4 %collective-permute-start.32 = (bf16[512,512]{1,0:T(8,128)(2,1)S(1)}, bf16[512,512]{1,0:T(8,128)(2,1)S(1)}, u32[]{:S(2)}, u32[]{:S(2)}) collective-permute-start(bf16[512,512]{1,0:T(8,128)(2,1)S(1)} %get-tuple-element.119), channel_id=1, source_target_pairs={{96,0},{104,8},{112,16},{120,24},{64,32},{72,40},{80,48},{88,56},{... | collective-permute-start | bytes 1572872 | tf_op jit(solution)/shard_map/ppermute | solution.py:20
  113.1 14.1 %collective-permute-start.38 = (bf16[512,512]{1,0:T(8,128)(2,1)S(1)}, bf16[512,512]{1,0:T(8,128)(2,1)S(1)}, u32[]{:S(2)}, u32[]{:S(2)}) collective-permute-start(bf16[512,512]{1,0:T(8,128)(2,1)S(1)} %get-tuple-element.133), channel_id=1, source_target_pairs={{8,0},{0,8},{24,16},{16,24},{40,32},{32,40},{56,48},{48,56},{72,64... | collective-permute-start | bytes 1572872 | tf_op jit(solution)/shard_map/ppermute | solution.py:20
  114.1 14.6 %collective-permute-start.39 = (bf16[512,512]{1,0:T(8,128)(2,1)S(1)}, bf16[512,512]{1,0:T(8,128)(2,1)S(1)}, u32[]{:S(2)}, u32[]{:S(2)}) collective-permute-start(bf16[512,512]{1,0:T(8,128)(2,1)S(1)} %get-tuple-element.134), channel_id=1, source_target_pairs={{24,0},{16,8},{8,16},{0,24},{56,32},{48,40},{40,48},{32,56},{88,64... | collective-permute-start | bytes 1572872 | tf_op jit(solution)/shard_map/ppermute | solution.py:20
  122.1 9.5 %collective-permute-start.36 = (bf16[256,512]{1,0:T(8,128)(2,1)S(1)}, bf16[256,512]{1,0:T(8,128)(2,1)S(1)}, u32[]{:S(2)}, u32[]{:S(2)}) collective-permute-start(bf16[256,512]{1,0:T(8,128)(2,1)S(1)} %get-tuple-element.129), channel_id=1, source_target_pairs={{32,0},{40,8},{48,16},{56,24},{0,32},{8,40},{16,48},{24,56},{96,64... | collective-permute-start | bytes 786440 | tf_op jit(solution)/shard_map/ppermute | solution.py:20
  122.8 8.9 %collective-permute-start.37 = (bf16[256,512]{1,0:T(8,128)(2,1)S(1)}, bf16[256,512]{1,0:T(8,128)(2,1)S(1)}, u32[]{:S(2)}, u32[]{:S(2)}) collective-permute-start(bf16[256,512]{1,0:T(8,128)(2,1)S(1)} %get-tuple-element.130), channel_id=1, source_target_pairs={{96,0},{104,8},{112,16},{120,24},{64,32},{72,40},{80,48},{88,56},{... | collective-permute-start | bytes 786440 | tf_op jit(solution)/shard_map/ppermute | solution.py:20
  128.8 9.3 %collective-permute-start.43 = (bf16[256,512]{1,0:T(8,128)(2,1)S(1)}, bf16[256,512]{1,0:T(8,128)(2,1)S(1)}, u32[]{:S(2)}, u32[]{:S(2)}) collective-permute-start(bf16[256,512]{1,0:T(8,128)(2,1)S(1)} %get-tuple-element.135), channel_id=1, source_target_pairs={{8,0},{0,8},{24,16},{16,24},{40,32},{32,40},{56,48},{48,56},{72,64... | collective-permute-start | bytes 786440 | tf_op jit(solution)/shard_map/ppermute | solution.py:20
  129.2 9.8 %collective-permute-start.44 = (bf16[256,512]{1,0:T(8,128)(2,1)S(1)}, bf16[256,512]{1,0:T(8,128)(2,1)S(1)}, u32[]{:S(2)}, u32[]{:S(2)}) collective-permute-start(bf16[256,512]{1,0:T(8,128)(2,1)S(1)} %get-tuple-element.142), channel_id=1, source_target_pairs={{24,0},{16,8},{8,16},{0,24},{56,32},{48,40},{40,48},{32,56},{88,64... | collective-permute-start | bytes 786440 | tf_op jit(solution)/shard_map/ppermute | solution.py:20
  131.8 10.9 %collective-permute-start.40 = (bf16[512,128]{1,0:T(8,128)(2,1)S(1)}, bf16[512,128]{1,0:T(8,128)(2,1)S(1)}, u32[]{:S(2)}, u32[]{:S(2)}) collective-permute-start(bf16[512,128]{1,0:T(8,128)(2,1)S(1)} %get-tuple-element.139), channel_id=1, source_target_pairs={{8,0},{0,8},{24,16},{16,24},{40,32},{32,40},{56,48},{48,56},{72,64... | collective-permute-start | bytes 393224 | tf_op jit(solution)/shard_map/ppermute | solution.py:20
  133.2 10.8 %collective-permute-start.41 = (bf16[512,128]{1,0:T(8,128)(2,1)S(1)}, bf16[512,128]{1,0:T(8,128)(2,1)S(1)}, u32[]{:S(2)}, u32[]{:S(2)}) collective-permute-start(bf16[512,128]{1,0:T(8,128)(2,1)S(1)} %get-tuple-element.140), channel_id=1, source_target_pairs={{16,0},{24,8},{0,16},{8,24},{48,32},{56,40},{32,48},{40,56},{80,64... | collective-permute-start | bytes 393224 | tf_op jit(solution)/shard_map/ppermute | solution.py:20
  135.5 8.5 %collective-permute-start.42 = (bf16[512,128]{1,0:T(8,128)(2,1)S(1)}, bf16[512,128]{1,0:T(8,128)(2,1)S(1)}, u32[]{:S(2)}, u32[]{:S(2)}) collective-permute-start(bf16[512,128]{1,0:T(8,128)(2,1)S(1)} %get-tuple-element.141), channel_id=1, source_target_pairs={{24,0},{16,8},{8,16},{0,24},{56,32},{48,40},{40,48},{32,56},{88,64... | collective-permute-start | bytes 393224 | tf_op jit(solution)/shard_map/ppermute | solution.py:20
  139.2 5.0 %collective-permute-start.45 = (bf16[512,128]{1,0:T(8,128)(2,1)S(1)}, bf16[512,128]{1,0:T(8,128)(2,1)S(1)}, u32[]{:S(2)}, u32[]{:S(2)}) collective-permute-start(bf16[512,128]{1,0:T(8,128)(2,1)S(1)} %get-tuple-element.146), channel_id=1, source_target_pairs={{32,0},{40,8},{48,16},{56,24},{0,32},{8,40},{16,48},{24,56},{96,64... | collective-permute-start | bytes 393224 | tf_op jit(solution)/shard_map/ppermute | solution.py:20
  139.3 7.7 %collective-permute-start.46 = (bf16[512,128]{1,0:T(8,128)(2,1)S(1)}, bf16[512,128]{1,0:T(8,128)(2,1)S(1)}, u32[]{:S(2)}, u32[]{:S(2)}) collective-permute-start(bf16[512,128]{1,0:T(8,128)(2,1)S(1)} %get-tuple-element.147), channel_id=1, source_target_pairs={{64,0},{72,8},{80,16},{88,24},{96,32},{104,40},{112,48},{120,56},{... | collective-permute-start | bytes 393224 | tf_op jit(solution)/shard_map/ppermute | solution.py:20
  142.7 6.2 %collective-permute-start.47 = (bf16[512,128]{1,0:T(8,128)(2,1)S(1)}, bf16[512,128]{1,0:T(8,128)(2,1)S(1)}, u32[]{:S(2)}, u32[]{:S(2)}) collective-permute-start(bf16[512,128]{1,0:T(8,128)(2,1)S(1)} %get-tuple-element.148), channel_id=1, source_target_pairs={{96,0},{104,8},{112,16},{120,24},{64,32},{72,40},{80,48},{88,56},{... | collective-permute-start | bytes 393224 | tf_op jit(solution)/shard_map/ppermute | solution.py:20

commit v3 on v2

--- a/solution.py
+++ b/solution.py
@@ -113,14 +113,18 @@
     )
 
 
+def pairs_of(units):
+    return [(t, min(2 * LANES, units - t)) for t in range(0, units, 2 * LANES)]
+
+
 def project_other_kernel(rows, gate_weight, up_weight, out):
     units = gate_weight.shape[1]
     half = rows.shape[0] // 2
-    for t in range(0, units, LANES):
-        weights = jnp.concatenate([gate_weight[:, t : t + LANES], up_weight[:, t : t + LANES]], axis=1)
+    for t, width in pairs_of(units):
+        weights = jnp.concatenate([gate_weight[:, t : t + width], up_weight[:, t : t + width]], axis=1)
         term = jnp.dot(rows[:half, :], weights, preferred_element_type=F32)
-        out[:, t : t + LANES] = term[:, :LANES]
-        out[:, units + t : units + t + LANES] = term[:, LANES:]
+        out[:, t : t + width] = term[:, :width]
+        out[:, units + t : units + t + width] = term[:, width:]
 
 
 def project_other(rows, gate_weight, up_weight):
@@ -137,12 +141,12 @@
     half = rows.shape[0] // 2
     quarter = half // 4
     eighth = quarter // 2
-    for t in range(0, units, LANES):
-        weights = jnp.concatenate([gate_weight[:, t : t + LANES], up_weight[:, t : t + LANES]], axis=1)
+    for t, width in pairs_of(units):
+        weights = jnp.concatenate([gate_weight[:, t : t + width], up_weight[:, t : t + width]], axis=1)
         term = jnp.dot(rows[half:, :], weights, preferred_element_type=F32)
         for part in range(2):
-            columns = slice(t + part * units, t + part * units + LANES)
-            block = term[:, part * LANES : (part + 1) * LANES] + received[:, columns]
+            columns = slice(t + part * units, t + part * units + width)
+            block = term[:, part * width : (part + 1) * width] + received[:, columns]
             at = lambda j, h: block[j * quarter + h * eighth : j * quarter + (h + 1) * eighth]
             own[:, columns] = block[:quarter]
             to_one[:eighth, columns] = at(2, 0).astype(BF16)
@@ -333,10 +337,8 @@
     first = [first_round(exchange, p) for exchange, p in zip(along, parts)]
     second[0] = second_round(along[0], relay(parts[0], *after(first[0], parts[1][0])))
     relayed = relay(parts[1], *first[1])
-    second[0] = after(second[0], relayed[0])
     second[1] = second_round(along[1], relayed)
     final = send("x", add_line([parts[0][0], *first[0], *second[0]]))
-    second[1] = after(second[1], relayed[0])
     return last(place, final + send("z", add_line([parts[1][0], *first[1], *second[1]])))
 
 

time: 151 us -> 151 us (level)
  no operation moved by 1% of the time
where the time goes in v3:
time: 151 us; the launch traced here: 150 us
  starting transfers between devices  61.2 us (41%)
  waiting for transfers between devices  49.5 us (33%)
  Pallas kernels  37.2 us (25%)
  local copies, waits for them, and re-layouts  1.65 us (1%)
    ppermute x28, starting transfers between devices, from_wide(): return lax.ppermute(array, 'wide', [(i ^ step, i) for i in range(16)])  39.9 us
    pallas_call x20, Pallas kernels, call(): pl.pallas_call(kernel, out_shape=out_shape, in_specs=in_specs, out_specs=...  37.2 us
    ppermute x28, waiting for transfers between devices, from_wide(): return lax.ppermute(array, 'wide', [(i ^ step, i) for i in range(16)])  25.1 us
    ppermute x16, waiting for transfers between devices, from_y(): return lax.ppermute(array, 'narrow', [(i ^ bits * 2, i) for i in range(8)])  23.6 us
    ppermute x16, starting transfers between devices, from_y(): return lax.ppermute(array, 'narrow', [(i ^ bits * 2, i) for i in range(8)])  20.3 us
  transfers between devices with their start and end apart: 48, of which 28 were waited for; matrix products, arithmetic and copies ran while one was open for 0% of the time, Pallas kernels for 24%

profile of v3, /device:TPU:0, one launch (start us, length us, event | category | flops | bytes accessed | tf_op | source)
XLA Modules:
  0.0 150.2 jit_solution(10016245946406220220)
XLA Ops:
  0.1 1.0 slice_bitcast_fusion
  1.1 1.7 %collective-permute-start.3 = (bf16[512,128]{1,0:T(8,128)(2,1)S(1)}, bf16[512,128]{1,0:T(8,128)(2,1)S(1)}, u32[]{:S(2)}, u32[]{:S(2)}) collective-permute-start(bf16[512,128]{1,0:T(8,128)(2,1)S(1)} %get-tuple-element.142), channel_id=1, source_target_pairs={{8,0},{0,8},{24,16},{16,24},{40,32},{32,40},{56,48},{48,56},{72,64... | collective-permute-start | bytes 393224 | tf_op jit(solution)/shard_map/ppermute | solution.py:20
  2.7 1.9 %collective-permute-start = (bf16[512,128]{1,0:T(8,128)(2,1)S(1)}, bf16[512,128]{1,0:T(8,128)(2,1)S(1)}, u32[]{:S(2)}, u32[]{:S(2)}) collective-permute-start(bf16[512,128]{1,0:T(8,128)(2,1)S(1)} %get-tuple-element.74), channel_id=1, source_target_pairs={{32,0},{40,8},{48,16},{56,24},{0,32},{8,40},{16,48},{24,56},{96,64... | collective-permute-start | bytes 393224 | tf_op jit(solution)/shard_map/ppermute | solution.py:20
  4.7 3.6 %collective-permute-start.1 = (bf16[512,128]{1,0:T(8,128)(2,1)S(1)}, bf16[512,128]{1,0:T(8,128)(2,1)S(1)}, u32[]{:S(2)}, u32[]{:S(2)}) collective-permute-start(bf16[512,128]{1,0:T(8,128)(2,1)S(1)} %get-tuple-element.74), channel_id=1, source_target_pairs={{64,0},{72,8},{80,16},{88,24},{96,32},{104,40},{112,48},{120,56},{... | collective-permute-start | bytes 393224 | tf_op jit(solution)/shard_map/ppermute | solution.py:20
  8.3 2.7 %collective-permute-start.6 = (bf16[512,128]{1,0:T(8,128)(2,1)S(1)}, bf16[512,128]{1,0:T(8,128)(2,1)S(1)}, u32[]{:S(2)}, u32[]{:S(2)}) collective-permute-start(bf16[512,128]{1,0:T(8,128)(2,1)S(1)} %get-tuple-element.142), channel_id=1, source_target_pairs={{16,0},{24,8},{0,16},{8,24},{48,32},{56,40},{32,48},{40,56},{80,64... | collective-permute-start | bytes 393224 | tf_op jit(solution)/shard_map/ppermute | solution.py:20
  11.5 2.6 %collective-permute-done.1 = bf16[512,128]{1,0:T(8,128)(2,1)S(1)} collective-permute-done((bf16[512,128]{1,0:T(8,128)(2,1)S(1)}, bf16[512,128]{1,0:T(8,128)(2,1)S(1)}, u32[]{:S(2)}, u32[]{:S(2)}) %collective-permute-start.1) | collective-permute-done | bytes 131104 | tf_op jit(solution)/shard_map/ppermute | solution.py:20
  14.1 1.9 %collective-permute-done.2 = bf16[512,128]{1,0:T(8,128)(2,1)S(1)} collective-permute-done((bf16[512,128]{1,0:T(8,128)(2,1)S(1)}, bf16[512,128]{1,0:T(8,128)(2,1)S(1)}, u32[]{:S(2)}, u32[]{:S(2)}) %collective-permute-start.2) | collective-permute-done | bytes 131104 | tf_op jit(solution)/shard_map/ppermute | solution.py:20
  16.7 2.8 %collective-permute-start.5 = (bf16[4,512,128]{2,1,0:T(8,128)(2,1)S(1)}, bf16[4,512,128]{2,1,0:T(8,128)(2,1)S(1)}, u32[]{:S(2)}, u32[]{:S(2)}) collective-permute-start(bf16[4,512,128]{2,1,0:T(8,128)(2,1)S(1)} %pad_maximum_fusion.refs_0_), channel_id=1, source_target_pairs={{24,0},{16,8},{8,16},{0,24},{56,32},{48,40},{40,48},{32,56},{88,64... | collective-permute-start | bytes 1572872 | tf_op jit(solution)/shard_map/ppermute | solution.py:20
  19.6 1.8 %collective-permute-start.11 = (bf16[4,512,128]{2,1,0:T(8,128)(2,1)S(1)}, bf16[4,512,128]{2,1,0:T(8,128)(2,1)S(1)}, u32[]{:S(2)}, u32[]{:S(2)}) collective-permute-start(bf16[4,512,128]{2,1,0:T(8,128)(2,1)S(1)} %pad_maximum_fusion.1.refs_0_), channel_id=1, source_target_pairs={{96,0},{104,8},{112,16},{120,24},{64,32},{72,40},{80,48},{88,56},{... | collective-permute-start | bytes 1572872 | tf_op jit(solution)/shard_map/ppermute | solution.py:20
  21.4 7.6 %load.1 = (bf16[2048,1664]{1,0:T(8,128)(2,1)S(1)}, bf16[2048,1664]{1,0:T(8,128)(2,1)S(1)}, bf16[1664,2048]{1,0:T(8,128)(2,1)S(1)}) custom-call(s32[4]{0:T(128)S(1)} %pad_add_fusion.place, bf16[2048,1664]{1,0:T(8,128)(2,1)} %gate_hbm, bf16[2048,1664]{1,0:T(8,128)(2,1)} %up_hbm, bf16[1664,2048]{1,0:T(8,128)(2,1)} %down_hbm), custom_call_target="tpu_custom_call" | custom-call | flops 5000000000 | tf_op jit(solution)/shard_map/load/pallas_call | solution.py:36
  29.1 1.5 collective-permute-done.5.refs_2_
  31.0 2.6 %collective-permute-start.9 = (bf16[2,512,128]{2,1,0:T(8,128)(2,1)S(1)}, bf16[2,512,128]{2,1,0:T(8,128)(2,1)S(1)}, u32[]{:S(2)}, u32[]{:S(2)}) collective-permute-start(bf16[2,512,128]{2,1,0:T(8,128)(2,1)S(1)} %slice.33), channel_id=1, source_target_pairs={{24,0},{16,8},{8,16},{0,24},{56,32},{48,40},{40,48},{32,56},{88,64... | collective-permute-start | bytes 786440 | tf_op jit(solution)/shard_map/ppermute | solution.py:20
  33.6 1.0 assemble_z.2.refs_0_
  34.7 0.9 collective-permute-start.13
  35.6 1.0 assemble_x.2.refs_0_
  37.1 1.6 %collective-permute-done.9.refs_2_ = bf16[2,512,128]{2,1,0:T(8,128)(2,1)S(1)} collective-permute-done((bf16[2,512,128]{2,1,0:T(8,128)(2,1)S(1)}, bf16[2,512,128]{2,1,0:T(8,128)(2,1)S(1)}, u32[]{:S(2)}, u32[]{:S(2)}) %collective-permute-start.9) | collective-permute-done | bytes 262176 | tf_op jit(solution)/shard_map/ppermute | solution.py:20
  38.7 0.7 assemble_z.3.rows
  39.4 3.9 %project_other.2 = f32[256,3328]{1,0:T(8,128)S(1)} custom-call(bf16[512,2048]{1,0:T(8,128)(2,1)S(1)} %assemble_z.3.rows, bf16[2048,1664]{1,0:T(8,128)(2,1)S(1)} %get-tuple-element.86.gate_weight, bf16[2048,1664]{1,0:T(8,128)(2,1)S(1)} %get-tuple-element.87.up_weight), custom_call_target="tpu_custom_call" | custom-call | flops 4000000000 | tf_op jit(solution)/shard_map/project_other/pallas_call | solution.py:36
  43.4 0.7 assemble_x.3.rows
  44.1 3.9 %project_other.3 = f32[256,3328]{1,0:T(8,128)S(1)} custom-call(bf16[512,2048]{1,0:T(8,128)(2,1)S(1)} %assemble_x.3.rows, bf16[2048,1664]{1,0:T(8,128)(2,1)S(1)} %get-tuple-element.86.gate_weight, bf16[2048,1664]{1,0:T(8,128)(2,1)S(1)} %get-tuple-element.87.up_weight), custom_call_target="tpu_custom_call" | custom-call | flops 4000000000 | tf_op jit(solution)/shard_map/project_other/pallas_call | solution.py:36
  48.0 0.7 collective-permute-start.17
  49.4 3.9 %project_own.2 = (f32[64,3328]{1,0:T(8,128)S(1)}, bf16[64,3328]{1,0:T(8,128)(2,1)S(1)}, bf16[64,3328]{1,0:T(8,128)(2,1)S(1)}, f32[32,3328]{1,0:T(8,128)S(1)}, f32[32,3328]{1,0:T(8,128)S(1)}) custom-call(bf16[512,2048]{1,0:T(8,128)(2,1)S(1)} %assemble_z.3.rows, bf16[2048,1664]{1,0:T(8,128)(2,1)S(1)} %get-tuple-element.86.gate_weight, ...), custom_call_target="tpu_custom_call" | custom-call | flops 4000000000 | tf_op jit(solution)/shard_map/project_own/pallas_call | solution.py:36
  53.3 1.7 %collective-permute-start.15 = (bf16[64,3328]{1,0:T(8,128)(2,1)S(1)}, bf16[64,3328]{1,0:T(8,128)(2,1)S(1)}, u32[]{:S(2)}, u32[]{:S(2)}) collective-permute-start(bf16[64,3328]{1,0:T(8,128)(2,1)S(1)} %get-tuple-element.91), channel_id=1, source_target_pairs={{2,0},{3,1},{0,2},{1,3},{6,4},{7,5},{4,6},{5,7},{10,8},{11,9},{8,1... | collective-permute-start | bytes 1277960 | tf_op jit(solution)/shard_map/ppermute | solution.py:24
  55.0 2.2 %collective-permute-start.16 = (bf16[64,3328]{1,0:T(8,128)(2,1)S(1)}, bf16[64,3328]{1,0:T(8,128)(2,1)S(1)}, u32[]{:S(2)}, u32[]{:S(2)}) collective-permute-start(bf16[64,3328]{1,0:T(8,128)(2,1)S(1)} %get-tuple-element.92), channel_id=1, source_target_pairs={{6,0},{7,1},{4,2},{5,3},{2,4},{3,5},{0,6},{1,7},{14,8},{15,9},{12,... | collective-permute-start | bytes 1277960 | tf_op jit(solution)/shard_map/ppermute | solution.py:24
  57.2 3.9 %project_own.3 = (f32[64,3328]{1,0:T(8,128)S(1)}, bf16[64,3328]{1,0:T(8,128)(2,1)S(1)}, bf16[64,3328]{1,0:T(8,128)(2,1)S(1)}, f32[32,3328]{1,0:T(8,128)S(1)}, f32[32,3328]{1,0:T(8,128)S(1)}) custom-call(bf16[512,2048]{1,0:T(8,128)(2,1)S(1)} %assemble_x.3.rows, bf16[2048,1664]{1,0:T(8,128)(2,1)S(1)} %get-tuple-element.86.gate_weight, ...), custom_call_target="tpu_custom_call" | custom-call | flops 4000000000 | tf_op jit(solution)/shard_map/project_own/pallas_call | solution.py:36
  61.1 0.8 collective-permute-start.20
  62.4 3.6 %collective-permute-done.15.from_one.refs_1_ = bf16[64,3328]{1,0:T(8,128)(2,1)S(1)} collective-permute-done((bf16[64,3328]{1,0:T(8,128)(2,1)S(1)}, bf16[64,3328]{1,0:T(8,128)(2,1)S(1)}, u32[]{:S(2)}, u32[]{:S(2)}) %collective-permute-start.15) | collective-permute-done | bytes 426016 | tf_op jit(solution)/shard_map/ppermute | solution.py:24
  66.0 2.8 %collective-permute-done.16.from_three.refs_2_ = bf16[64,3328]{1,0:T(8,128)(2,1)S(1)} collective-permute-done((bf16[64,3328]{1,0:T(8,128)(2,1)S(1)}, bf16[64,3328]{1,0:T(8,128)(2,1)S(1)}, u32[]{:S(2)}, u32[]{:S(2)}) %collective-permute-start.16) | collective-permute-done | bytes 426016 | tf_op jit(solution)/shard_map/ppermute | solution.py:24
  69.1 2.3 %collective-permute-start.19 = (bf16[32,3328]{1,0:T(8,128)(2,1)S(1)}, bf16[32,3328]{1,0:T(8,128)(2,1)S(1)}, u32[]{:S(2)}, u32[]{:S(2)}) collective-permute-start(bf16[32,3328]{1,0:T(8,128)(2,1)S(1)} %get-tuple-element.100), channel_id=1, source_target_pairs={{6,0},{7,1},{4,2},{5,3},{2,4},{3,5},{0,6},{1,7},{14,8},{15,9},{12,... | collective-permute-start | bytes 638984 | tf_op jit(solution)/shard_map/ppermute | solution.py:24
  71.3 3.9 %collective-permute-done.20.from_one.refs_1_ = bf16[64,3328]{1,0:T(8,128)(2,1)S(1)} collective-permute-done((bf16[64,3328]{1,0:T(8,128)(2,1)S(1)}, bf16[64,3328]{1,0:T(8,128)(2,1)S(1)}, u32[]{:S(2)}, u32[]{:S(2)}) %collective-permute-start.20) | collective-permute-done | bytes 426016 | tf_op jit(solution)/shard_map/ppermute | solution.py:24
  75.2 2.8 %collective-permute-done.21.from_three.refs_2_ = bf16[64,3328]{1,0:T(8,128)(2,1)S(1)} collective-permute-done((bf16[64,3328]{1,0:T(8,128)(2,1)S(1)}, bf16[64,3328]{1,0:T(8,128)(2,1)S(1)}, u32[]{:S(2)}, u32[]{:S(2)}) %collective-permute-start.21) | collective-permute-done | bytes 426016 | tf_op jit(solution)/shard_map/ppermute | solution.py:24
  78.2 2.3 %collective-permute-start.25 = (bf16[32,3328]{1,0:T(8,128)(2,1)S(1)}, bf16[32,3328]{1,0:T(8,128)(2,1)S(1)}, u32[]{:S(2)}, u32[]{:S(2)}) collective-permute-start(bf16[32,3328]{1,0:T(8,128)(2,1)S(1)} %get-tuple-element.108), channel_id=1, source_target_pairs={{6,0},{7,1},{4,2},{5,3},{2,4},{3,5},{0,6},{1,7},{14,8},{15,9},{12,... | collective-permute-start | bytes 638984 | tf_op jit(solution)/shard_map/ppermute | solution.py:24
  80.4 2.1 %collective-permute-done.19.refs_4_ = bf16[32,3328]{1,0:T(8,128)(2,1)S(1)} collective-permute-done((bf16[32,3328]{1,0:T(8,128)(2,1)S(1)}, bf16[32,3328]{1,0:T(8,128)(2,1)S(1)}, u32[]{:S(2)}, u32[]{:S(2)}) %collective-permute-start.19) | collective-permute-done | bytes 213024 | tf_op jit(solution)/shard_map/ppermute | solution.py:24
  82.9 2.3 %collective-permute-start.23 = (bf16[64,1664]{1,0:T(8,128)(2,1)S(1)}, bf16[64,1664]{1,0:T(8,128)(2,1)S(1)}, u32[]{:S(2)}, u32[]{:S(2)}) collective-permute-start(bf16[64,1664]{1,0:T(8,128)(2,1)S(1)} %hidden.2), channel_id=1, source_target_pairs={{6,0},{7,1},{4,2},{5,3},{2,4},{3,5},{0,6},{1,7},{14,8},{15,9},{12,... | collective-permute-start | bytes 638984 | tf_op jit(solution)/shard_map/ppermute | solution.py:24
  85.2 2.1 %collective-permute-done.25.refs_4_ = bf16[32,3328]{1,0:T(8,128)(2,1)S(1)} collective-permute-done((bf16[32,3328]{1,0:T(8,128)(2,1)S(1)}, bf16[32,3328]{1,0:T(8,128)(2,1)S(1)}, u32[]{:S(2)}, u32[]{:S(2)}) %collective-permute-start.25) | collective-permute-done | bytes 213024 | tf_op jit(solution)/shard_map/ppermute | solution.py:24
  87.6 2.3 %collective-permute-start.27 = (bf16[64,1664]{1,0:T(8,128)(2,1)S(1)}, bf16[64,1664]{1,0:T(8,128)(2,1)S(1)}, u32[]{:S(2)}, u32[]{:S(2)}) collective-permute-start(bf16[64,1664]{1,0:T(8,128)(2,1)S(1)} %hidden.3), channel_id=1, source_target_pairs={{6,0},{7,1},{4,2},{5,3},{2,4},{3,5},{0,6},{1,7},{14,8},{15,9},{12,... | collective-permute-start | bytes 638984 | tf_op jit(solution)/shard_map/ppermute | solution.py:24
  90.1 2.3 %collective-permute-done.23 = bf16[64,1664]{1,0:T(8,128)(2,1)S(1)} collective-permute-done((bf16[64,1664]{1,0:T(8,128)(2,1)S(1)}, bf16[64,1664]{1,0:T(8,128)(2,1)S(1)}, u32[]{:S(2)}, u32[]{:S(2)}) %collective-permute-start.23) | collective-permute-done | bytes 213024 | tf_op jit(solution)/shard_map/ppermute | solution.py:24
  92.6 2.3 %collective-permute-start.29 = (bf16[32,1664]{1,0:T(8,128)(2,1)S(1)}, bf16[32,1664]{1,0:T(8,128)(2,1)S(1)}, u32[]{:S(2)}, u32[]{:S(2)}) collective-permute-start(bf16[32,1664]{1,0:T(8,128)(2,1)S(1)} %slice.37), channel_id=1, source_target_pairs={{6,0},{7,1},{4,2},{5,3},{2,4},{3,5},{0,6},{1,7},{14,8},{15,9},{12,... | collective-permute-start | bytes 319496 | tf_op jit(solution)/shard_map/ppermute | solution.py:24
  94.9 1.4 collective-permute-done.27
  96.3 0.9 collective-permute-done.28
  97.2 1.4 collective-permute-done.29
  98.8 0.8 collective-permute-start.33
  99.6 2.5 %collective-permute-start.34 = (bf16[32,1664]{1,0:T(8,128)(2,1)S(1)}, bf16[32,1664]{1,0:T(8,128)(2,1)S(1)}, u32[]{:S(2)}, u32[]{:S(2)}) collective-permute-start(bf16[32,1664]{1,0:T(8,128)(2,1)S(1)} %slice.39), channel_id=1, source_target_pairs={{6,0},{7,1},{4,2},{5,3},{2,4},{3,5},{0,6},{1,7},{14,8},{15,9},{12,... | collective-permute-start | bytes 319496 | tf_op jit(solution)/shard_map/ppermute | solution.py:24
  102.3 4.0 %down_z.1 = (f32[512,512]{1,0:T(8,128)S(1)}, bf16[512,512]{1,0:T(8,128)(2,1)S(1)}, bf16[512,512]{1,0:T(8,128)(2,1)S(1)}, f32[256,512]{1,0:T(8,128)S(1)}, f32[256,512]{1,0:T(8,128)S(1)}) custom-call(bf16[512,1664]{1,0:T(8,128)(2,1)S(1)} %constant_dynamic-update-slice_fusion.5.rows, bf16[1664,2048]{1,0:T(8,128)(2,1)S(1)} %get-tuple-element.81.down_weight), custom_call_target="tpu_custom_call" | custom-call | flops 4000000000 | tf_op jit(solution)/shard_map/down_z/pallas_call | solution.py:36
  106.6 2.0 %collective-permute-start.32 = (bf16[512,512]{1,0:T(8,128)(2,1)S(1)}, bf16[512,512]{1,0:T(8,128)(2,1)S(1)}, u32[]{:S(2)}, u32[]{:S(2)}) collective-permute-start(bf16[512,512]{1,0:T(8,128)(2,1)S(1)} %get-tuple-element.115), channel_id=1, source_target_pairs={{96,0},{104,8},{112,16},{120,24},{64,32},{72,40},{80,48},{88,56},{... | collective-permute-start | bytes 1572872 | tf_op jit(solution)/shard_map/ppermute | solution.py:20
  109.0 4.1 %down_x.1 = (f32[512,512]{1,0:T(8,128)S(1)}, bf16[512,512]{1,0:T(8,128)(2,1)S(1)}, bf16[512,512]{1,0:T(8,128)(2,1)S(1)}, f32[256,512]{1,0:T(8,128)S(1)}, f32[256,512]{1,0:T(8,128)S(1)}) custom-call(bf16[512,1664]{1,0:T(8,128)(2,1)S(1)} %constant_dynamic-update-slice_fusion.16.rows, bf16[1664,2048]{1,0:T(8,128)(2,1)S(1)} %get-tuple-element.81.down_weight), custom_call_target="tpu_custom_call" | custom-call | flops 4000000000 | tf_op jit(solution)/shard_map/down_x/pallas_call | solution.py:36
  113.1 1.0 collective-permute-start.41
  114.1 2.3 %collective-permute-start.42 = (bf16[512,512]{1,0:T(8,128)(2,1)S(1)}, bf16[512,512]{1,0:T(8,128)(2,1)S(1)}, u32[]{:S(2)}, u32[]{:S(2)}) collective-permute-start(bf16[512,512]{1,0:T(8,128)(2,1)S(1)} %get-tuple-element.132), channel_id=1, source_target_pairs={{24,0},{16,8},{8,16},{0,24},{56,32},{48,40},{40,48},{32,56},{88,64... | collective-permute-start | bytes 1572872 | tf_op jit(solution)/shard_map/ppermute | solution.py:20
  116.5 4.4 %collective-permute-done.31.from_one = bf16[512,512]{1,0:T(8,128)(2,1)S(1)} collective-permute-done((bf16[512,512]{1,0:T(8,128)(2,1)S(1)}, bf16[512,512]{1,0:T(8,128)(2,1)S(1)}, u32[]{:S(2)}, u32[]{:S(2)}) %collective-permute-start.31) | collective-permute-done | bytes 524320 | tf_op jit(solution)/shard_map/ppermute | solution.py:20
  120.9 1.2 collective-permute-done.32.from_three
  122.8 2.0 %collective-permute-start.37 = (bf16[256,512]{1,0:T(8,128)(2,1)S(1)}, bf16[256,512]{1,0:T(8,128)(2,1)S(1)}, u32[]{:S(2)}, u32[]{:S(2)}) collective-permute-start(bf16[256,512]{1,0:T(8,128)(2,1)S(1)} %get-tuple-element.126), channel_id=1, source_target_pairs={{96,0},{104,8},{112,16},{120,24},{64,32},{72,40},{80,48},{88,56},{... | collective-permute-start | bytes 786440 | tf_op jit(solution)/shard_map/ppermute | solution.py:20
  124.7 2.4 %collective-permute-done.41.from_one = bf16[512,512]{1,0:T(8,128)(2,1)S(1)} collective-permute-done((bf16[512,512]{1,0:T(8,128)(2,1)S(1)}, bf16[512,512]{1,0:T(8,128)(2,1)S(1)}, u32[]{:S(2)}, u32[]{:S(2)}) %collective-permute-start.41) | collective-permute-done | bytes 524320 | tf_op jit(solution)/shard_map/ppermute | solution.py:20
  127.2 1.6 %collective-permute-done.42.from_three = bf16[512,512]{1,0:T(8,128)(2,1)S(1)} collective-permute-done((bf16[512,512]{1,0:T(8,128)(2,1)S(1)}, bf16[512,512]{1,0:T(8,128)(2,1)S(1)}, u32[]{:S(2)}, u32[]{:S(2)}) %collective-permute-start.42) | collective-permute-done | bytes 524320 | tf_op jit(solution)/shard_map/ppermute | solution.py:20
  129.2 2.4 %collective-permute-start.44 = (bf16[256,512]{1,0:T(8,128)(2,1)S(1)}, bf16[256,512]{1,0:T(8,128)(2,1)S(1)}, u32[]{:S(2)}, u32[]{:S(2)}) collective-permute-start(bf16[256,512]{1,0:T(8,128)(2,1)S(1)} %get-tuple-element.136), channel_id=1, source_target_pairs={{24,0},{16,8},{8,16},{0,24},{56,32},{48,40},{40,48},{32,56},{88,64... | collective-permute-start | bytes 786440 | tf_op jit(solution)/shard_map/ppermute | solution.py:20
  131.8 1.4 collective-permute-start.38
  133.2 2.3 %collective-permute-start.39 = (bf16[512,128]{1,0:T(8,128)(2,1)S(1)}, bf16[512,128]{1,0:T(8,128)(2,1)S(1)}, u32[]{:S(2)}, u32[]{:S(2)}) collective-permute-start(bf16[512,128]{1,0:T(8,128)(2,1)S(1)} %get-tuple-element.129), channel_id=1, source_target_pairs={{16,0},{24,8},{0,16},{8,24},{48,32},{56,40},{32,48},{40,56},{80,64... | collective-permute-start | bytes 393224 | tf_op jit(solution)/shard_map/ppermute | solution.py:20
  135.5 1.1 collective-permute-start.40
  136.6 1.6 %collective-permute-done.43.relay_one = bf16[256,512]{1,0:T(8,128)(2,1)S(1)} collective-permute-done((bf16[256,512]{1,0:T(8,128)(2,1)S(1)}, bf16[256,512]{1,0:T(8,128)(2,1)S(1)}, u32[]{:S(2)}, u32[]{:S(2)}) %collective-permute-start.43) | collective-permute-done | bytes 262176 | tf_op jit(solution)/shard_map/ppermute | solution.py:20
  138.2 0.8 collective-permute-done.44.relay_three
  139.3 3.4 %collective-permute-start.46 = (bf16[512,128]{1,0:T(8,128)(2,1)S(1)}, bf16[512,128]{1,0:T(8,128)(2,1)S(1)}, u32[]{:S(2)}, u32[]{:S(2)}) collective-permute-start(bf16[512,128]{1,0:T(8,128)(2,1)S(1)} %get-tuple-element.139), channel_id=1, source_target_pairs={{64,0},{72,8},{80,16},{88,24},{96,32},{104,40},{112,48},{120,56},{... | collective-permute-start | bytes 393224 | tf_op jit(solution)/shard_map/ppermute | solution.py:20
  142.7 1.3 collective-permute-start.47
  144.3 2.8 %collective-permute-done.46.refs_6_ = bf16[512,128]{1,0:T(8,128)(2,1)S(1)} collective-permute-done((bf16[512,128]{1,0:T(8,128)(2,1)S(1)}, bf16[512,128]{1,0:T(8,128)(2,1)S(1)}, u32[]{:S(2)}, u32[]{:S(2)}) %collective-permute-start.46) | collective-permute-done | bytes 131104 | tf_op jit(solution)/shard_map/ppermute | solution.py:20
  147.0 1.8 %collective-permute-done.47.refs_7_ = bf16[512,128]{1,0:T(8,128)(2,1)S(1)} collective-permute-done((bf16[512,128]{1,0:T(8,128)(2,1)S(1)}, bf16[512,128]{1,0:T(8,128)(2,1)S(1)}, u32[]{:S(2)}, u32[]{:S(2)}) %collective-permute-start.47) | collective-permute-done | bytes 131104 | tf_op jit(solution)/shard_map/ppermute | solution.py:20
  148.9 1.4 last.1
  (76 shorter events, 8.1 us)
Async XLA Ops:
  1.1 9.9 %collective-permute-start.3 = (bf16[512,128]{1,0:T(8,128)(2,1)S(1)}, bf16[512,128]{1,0:T(8,128)(2,1)S(1)}, u32[]{:S(2)}, u32[]{:S(2)}) collective-permute-start(bf16[512,128]{1,0:T(8,128)(2,1)S(1)} %get-tuple-element.142), channel_id=1, source_target_pairs={{8,0},{0,8},{24,16},{16,24},{40,32},{32,40},{56,48},{48,56},{72,64... | collective-permute-start | bytes 393224 | tf_op jit(solution)/shard_map/ppermute | solution.py:20
  2.7 8.7 %collective-permute-start = (bf16[512,128]{1,0:T(8,128)(2,1)S(1)}, bf16[512,128]{1,0:T(8,128)(2,1)S(1)}, u32[]{:S(2)}, u32[]{:S(2)}) collective-permute-start(bf16[512,128]{1,0:T(8,128)(2,1)S(1)} %get-tuple-element.74), channel_id=1, source_target_pairs={{32,0},{40,8},{48,16},{56,24},{0,32},{8,40},{16,48},{24,56},{96,64... | collective-permute-start | bytes 393224 | tf_op jit(solution)/shard_map/ppermute | solution.py:20
  4.7 9.4 %collective-permute-start.1 = (bf16[512,128]{1,0:T(8,128)(2,1)S(1)}, bf16[512,128]{1,0:T(8,128)(2,1)S(1)}, u32[]{:S(2)}, u32[]{:S(2)}) collective-permute-start(bf16[512,128]{1,0:T(8,128)(2,1)S(1)} %get-tuple-element.74), channel_id=1, source_target_pairs={{64,0},{72,8},{80,16},{88,24},{96,32},{104,40},{112,48},{120,56},{... | collective-permute-start | bytes 393224 | tf_op jit(solution)/shard_map/ppermute | solution.py:20
  8.2 7.7 %collective-permute-start.2 = (bf16[512,128]{1,0:T(8,128)(2,1)S(1)}, bf16[512,128]{1,0:T(8,128)(2,1)S(1)}, u32[]{:S(2)}, u32[]{:S(2)}) collective-permute-start(bf16[512,128]{1,0:T(8,128)(2,1)S(1)} %get-tuple-element.74), channel_id=1, source_target_pairs={{96,0},{104,8},{112,16},{120,24},{64,32},{72,40},{80,48},{88,56},{... | collective-permute-start | bytes 393224 | tf_op jit(solution)/shard_map/ppermute | solution.py:20
  8.3 11.2 %collective-permute-start.6 = (bf16[512,128]{1,0:T(8,128)(2,1)S(1)}, bf16[512,128]{1,0:T(8,128)(2,1)S(1)}, u32[]{:S(2)}, u32[]{:S(2)}) collective-permute-start(bf16[512,128]{1,0:T(8,128)(2,1)S(1)} %get-tuple-element.142), channel_id=1, source_target_pairs={{16,0},{24,8},{0,16},{8,24},{48,32},{56,40},{32,48},{40,56},{80,64... | collective-permute-start | bytes 393224 | tf_op jit(solution)/shard_map/ppermute | solution.py:20
  11.0 8.5 %collective-permute-start.7 = (bf16[512,128]{1,0:T(8,128)(2,1)S(1)}, bf16[512,128]{1,0:T(8,128)(2,1)S(1)}, u32[]{:S(2)}, u32[]{:S(2)}) collective-permute-start(bf16[512,128]{1,0:T(8,128)(2,1)S(1)} %get-tuple-element.142), channel_id=1, source_target_pairs={{24,0},{16,8},{8,16},{0,24},{56,32},{48,40},{40,48},{32,56},{88,64... | collective-permute-start | bytes 393224 | tf_op jit(solution)/shard_map/ppermute | solution.py:20
  16.1 13.1 %collective-permute-start.4 = (bf16[4,512,128]{2,1,0:T(8,128)(2,1)S(1)}, bf16[4,512,128]{2,1,0:T(8,128)(2,1)S(1)}, u32[]{:S(2)}, u32[]{:S(2)}) collective-permute-start(bf16[4,512,128]{2,1,0:T(8,128)(2,1)S(1)} %pad_maximum_fusion.refs_0_), channel_id=1, source_target_pairs={{8,0},{0,8},{24,16},{16,24},{40,32},{32,40},{56,48},{48,56},{72,64... | collective-permute-start | bytes 1572872 | tf_op jit(solution)/shard_map/ppermute | solution.py:20
  16.7 13.9 %collective-permute-start.5 = (bf16[4,512,128]{2,1,0:T(8,128)(2,1)S(1)}, bf16[4,512,128]{2,1,0:T(8,128)(2,1)S(1)}, u32[]{:S(2)}, u32[]{:S(2)}) collective-permute-start(bf16[4,512,128]{2,1,0:T(8,128)(2,1)S(1)} %pad_maximum_fusion.refs_0_), channel_id=1, source_target_pairs={{24,0},{16,8},{8,16},{0,24},{56,32},{48,40},{40,48},{32,56},{88,64... | collective-permute-start | bytes 1572872 | tf_op jit(solution)/shard_map/ppermute | solution.py:20
  19.5 15.2 %collective-permute-start.10 = (bf16[4,512,128]{2,1,0:T(8,128)(2,1)S(1)}, bf16[4,512,128]{2,1,0:T(8,128)(2,1)S(1)}, u32[]{:S(2)}, u32[]{:S(2)}) collective-permute-start(bf16[4,512,128]{2,1,0:T(8,128)(2,1)S(1)} %pad_maximum_fusion.1.refs_0_), channel_id=1, source_target_pairs={{32,0},{40,8},{48,16},{56,24},{0,32},{8,40},{16,48},{24,56},{96,64... | collective-permute-start | bytes 1572872 | tf_op jit(solution)/shard_map/ppermute | solution.py:20
  19.6 15.0 %collective-permute-start.11 = (bf16[4,512,128]{2,1,0:T(8,128)(2,1)S(1)}, bf16[4,512,128]{2,1,0:T(8,128)(2,1)S(1)}, u32[]{:S(2)}, u32[]{:S(2)}) collective-permute-start(bf16[4,512,128]{2,1,0:T(8,128)(2,1)S(1)} %pad_maximum_fusion.1.refs_0_), channel_id=1, source_target_pairs={{96,0},{104,8},{112,16},{120,24},{64,32},{72,40},{80,48},{88,56},{... | collective-permute-start | bytes 1572872 | tf_op jit(solution)/shard_map/ppermute | solution.py:20
  30.6 6.5 %collective-permute-start.8 = (bf16[2,512,128]{2,1,0:T(8,128)(2,1)S(1)}, bf16[2,512,128]{2,1,0:T(8,128)(2,1)S(1)}, u32[]{:S(2)}, u32[]{:S(2)}) collective-permute-start(bf16[2,512,128]{2,1,0:T(8,128)(2,1)S(1)} %slice.32), channel_id=1, source_target_pairs={{8,0},{0,8},{24,16},{16,24},{40,32},{32,40},{56,48},{48,56},{72,64... | collective-permute-start | bytes 786440 | tf_op jit(solution)/shard_map/ppermute | solution.py:20
  31.0 7.7 %collective-permute-start.9 = (bf16[2,512,128]{2,1,0:T(8,128)(2,1)S(1)}, bf16[2,512,128]{2,1,0:T(8,128)(2,1)S(1)}, u32[]{:S(2)}, u32[]{:S(2)}) collective-permute-start(bf16[2,512,128]{2,1,0:T(8,128)(2,1)S(1)} %slice.33), channel_id=1, source_target_pairs={{24,0},{16,8},{8,16},{0,24},{56,32},{48,40},{40,48},{32,56},{88,64... | collective-permute-start | bytes 786440 | tf_op jit(solution)/shard_map/ppermute | solution.py:20
  34.6 8.7 %collective-permute-start.12 = (bf16[2,512,128]{2,1,0:T(8,128)(2,1)S(1)}, bf16[2,512,128]{2,1,0:T(8,128)(2,1)S(1)}, u32[]{:S(2)}, u32[]{:S(2)}) collective-permute-start(bf16[2,512,128]{2,1,0:T(8,128)(2,1)S(1)} %slice.40), channel_id=1, source_target_pairs={{32,0},{40,8},{48,16},{56,24},{0,32},{8,40},{16,48},{24,56},{96,64... | collective-permute-start | bytes 786440 | tf_op jit(solution)/shard_map/ppermute | solution.py:20
  34.7 8.6 %collective-permute-start.13 = (bf16[2,512,128]{2,1,0:T(8,128)(2,1)S(1)}, bf16[2,512,128]{2,1,0:T(8,128)(2,1)S(1)}, u32[]{:S(2)}, u32[]{:S(2)}) collective-permute-start(bf16[2,512,128]{2,1,0:T(8,128)(2,1)S(1)} %slice.41), channel_id=1, source_target_pairs={{96,0},{104,8},{112,16},{120,24},{64,32},{72,40},{80,48},{88,56},{... | collective-permute-start | bytes 786440 | tf_op jit(solution)/shard_map/ppermute | solution.py:20
  43.3 6.1 %collective-permute-start.14 = (f32[256,3328]{1,0:T(8,128)S(1)}, f32[256,3328]{1,0:T(8,128)S(1)}, u32[]{:S(2)}, u32[]{:S(2)}) collective-permute-start(f32[256,3328]{1,0:T(8,128)S(1)} %project_other.2), channel_id=1, source_target_pairs={{1,0},{0,1},{3,2},{2,3},{5,4},{4,5},{7,6},{6,7},{9,8},{8,9},{11,10... | collective-permute-start | bytes 10223624 | tf_op jit(solution)/shard_map/ppermute | solution.py:28
  48.0 9.2 %collective-permute-start.17 = (f32[256,3328]{1,0:T(8,128)S(1)}, f32[256,3328]{1,0:T(8,128)S(1)}, u32[]{:S(2)}, u32[]{:S(2)}) collective-permute-start(f32[256,3328]{1,0:T(8,128)S(1)} %project_other.3), channel_id=1, source_target_pairs={{1,0},{0,1},{3,2},{2,3},{5,4},{4,5},{7,6},{6,7},{9,8},{8,9},{11,10... | collective-permute-start | bytes 10223624 | tf_op jit(solution)/shard_map/ppermute | solution.py:28
  53.3 12.7 %collective-permute-start.15 = (bf16[64,3328]{1,0:T(8,128)(2,1)S(1)}, bf16[64,3328]{1,0:T(8,128)(2,1)S(1)}, u32[]{:S(2)}, u32[]{:S(2)}) collective-permute-start(bf16[64,3328]{1,0:T(8,128)(2,1)S(1)} %get-tuple-element.91), channel_id=1, source_target_pairs={{2,0},{3,1},{0,2},{1,3},{6,4},{7,5},{4,6},{5,7},{10,8},{11,9},{8,1... | collective-permute-start | bytes 1277960 | tf_op jit(solution)/shard_map/ppermute | solution.py:24
  55.0 13.9 %collective-permute-start.16 = (bf16[64,3328]{1,0:T(8,128)(2,1)S(1)}, bf16[64,3328]{1,0:T(8,128)(2,1)S(1)}, u32[]{:S(2)}, u32[]{:S(2)}) collective-permute-start(bf16[64,3328]{1,0:T(8,128)(2,1)S(1)} %get-tuple-element.92), channel_id=1, source_target_pairs={{6,0},{7,1},{4,2},{5,3},{2,4},{3,5},{0,6},{1,7},{14,8},{15,9},{12,... | collective-permute-start | bytes 1277960 | tf_op jit(solution)/shard_map/ppermute | solution.py:24
  61.1 14.1 %collective-permute-start.20 = (bf16[64,3328]{1,0:T(8,128)(2,1)S(1)}, bf16[64,3328]{1,0:T(8,128)(2,1)S(1)}, u32[]{:S(2)}, u32[]{:S(2)}) collective-permute-start(bf16[64,3328]{1,0:T(8,128)(2,1)S(1)} %get-tuple-element.103), channel_id=1, source_target_pairs={{2,0},{3,1},{0,2},{1,3},{6,4},{7,5},{4,6},{5,7},{10,8},{11,9},{8,1... | collective-permute-start | bytes 1277960 | tf_op jit(solution)/shard_map/ppermute | solution.py:24
  61.8 16.2 %collective-permute-start.21 = (bf16[64,3328]{1,0:T(8,128)(2,1)S(1)}, bf16[64,3328]{1,0:T(8,128)(2,1)S(1)}, u32[]{:S(2)}, u32[]{:S(2)}) collective-permute-start(bf16[64,3328]{1,0:T(8,128)(2,1)S(1)} %get-tuple-element.104), channel_id=1, source_target_pairs={{6,0},{7,1},{4,2},{5,3},{2,4},{3,5},{0,6},{1,7},{14,8},{15,9},{12,... | collective-permute-start | bytes 1277960 | tf_op jit(solution)/shard_map/ppermute | solution.py:24
  69.0 11.5 %collective-permute-start.18 = (bf16[32,3328]{1,0:T(8,128)(2,1)S(1)}, bf16[32,3328]{1,0:T(8,128)(2,1)S(1)}, u32[]{:S(2)}, u32[]{:S(2)}) collective-permute-start(bf16[32,3328]{1,0:T(8,128)(2,1)S(1)} %get-tuple-element.99), channel_id=1, source_target_pairs={{2,0},{3,1},{0,2},{1,3},{6,4},{7,5},{4,6},{5,7},{10,8},{11,9},{8,1... | collective-permute-start | bytes 638984 | tf_op jit(solution)/shard_map/ppermute | solution.py:24
  69.1 13.5 %collective-permute-start.19 = (bf16[32,3328]{1,0:T(8,128)(2,1)S(1)}, bf16[32,3328]{1,0:T(8,128)(2,1)S(1)}, u32[]{:S(2)}, u32[]{:S(2)}) collective-permute-start(bf16[32,3328]{1,0:T(8,128)(2,1)S(1)} %get-tuple-element.100), channel_id=1, source_target_pairs={{6,0},{7,1},{4,2},{5,3},{2,4},{3,5},{0,6},{1,7},{14,8},{15,9},{12,... | collective-permute-start | bytes 638984 | tf_op jit(solution)/shard_map/ppermute | solution.py:24
  78.1 7.1 %collective-permute-start.24 = (bf16[32,3328]{1,0:T(8,128)(2,1)S(1)}, bf16[32,3328]{1,0:T(8,128)(2,1)S(1)}, u32[]{:S(2)}, u32[]{:S(2)}) collective-permute-start(bf16[32,3328]{1,0:T(8,128)(2,1)S(1)} %get-tuple-element.105), channel_id=1, source_target_pairs={{2,0},{3,1},{0,2},{1,3},{6,4},{7,5},{4,6},{5,7},{10,8},{11,9},{8,1... | collective-permute-start | bytes 638984 | tf_op jit(solution)/shard_map/ppermute | solution.py:24
  78.2 9.1 %collective-permute-start.25 = (bf16[32,3328]{1,0:T(8,128)(2,1)S(1)}, bf16[32,3328]{1,0:T(8,128)(2,1)S(1)}, u32[]{:S(2)}, u32[]{:S(2)}) collective-permute-start(bf16[32,3328]{1,0:T(8,128)(2,1)S(1)} %get-tuple-element.108), channel_id=1, source_target_pairs={{6,0},{7,1},{4,2},{5,3},{2,4},{3,5},{0,6},{1,7},{14,8},{15,9},{12,... | collective-permute-start | bytes 638984 | tf_op jit(solution)/shard_map/ppermute | solution.py:24
  82.8 7.3 %collective-permute-start.22 = (bf16[64,1664]{1,0:T(8,128)(2,1)S(1)}, bf16[64,1664]{1,0:T(8,128)(2,1)S(1)}, u32[]{:S(2)}, u32[]{:S(2)}) collective-permute-start(bf16[64,1664]{1,0:T(8,128)(2,1)S(1)} %hidden.2), channel_id=1, source_target_pairs={{2,0},{3,1},{0,2},{1,3},{6,4},{7,5},{4,6},{5,7},{10,8},{11,9},{8,1... | collective-permute-start | bytes 638984 | tf_op jit(solution)/shard_map/ppermute | solution.py:24
  82.9 9.5 %collective-permute-start.23 = (bf16[64,1664]{1,0:T(8,128)(2,1)S(1)}, bf16[64,1664]{1,0:T(8,128)(2,1)S(1)}, u32[]{:S(2)}, u32[]{:S(2)}) collective-permute-start(bf16[64,1664]{1,0:T(8,128)(2,1)S(1)} %hidden.2), channel_id=1, source_target_pairs={{6,0},{7,1},{4,2},{5,3},{2,4},{3,5},{0,6},{1,7},{14,8},{15,9},{12,... | collective-permute-start | bytes 638984 | tf_op jit(solution)/shard_map/ppermute | solution.py:24
  87.5 7.3 %collective-permute-start.26 = (bf16[64,1664]{1,0:T(8,128)(2,1)S(1)}, bf16[64,1664]{1,0:T(8,128)(2,1)S(1)}, u32[]{:S(2)}, u32[]{:S(2)}) collective-permute-start(bf16[64,1664]{1,0:T(8,128)(2,1)S(1)} %hidden.3), channel_id=1, source_target_pairs={{2,0},{3,1},{0,2},{1,3},{6,4},{7,5},{4,6},{5,7},{10,8},{11,9},{8,1... | collective-permute-start | bytes 638984 | tf_op jit(solution)/shard_map/ppermute | solution.py:24
  87.6 8.7 %collective-permute-start.27 = (bf16[64,1664]{1,0:T(8,128)(2,1)S(1)}, bf16[64,1664]{1,0:T(8,128)(2,1)S(1)}, u32[]{:S(2)}, u32[]{:S(2)}) collective-permute-start(bf16[64,1664]{1,0:T(8,128)(2,1)S(1)} %hidden.3), channel_id=1, source_target_pairs={{6,0},{7,1},{4,2},{5,3},{2,4},{3,5},{0,6},{1,7},{14,8},{15,9},{12,... | collective-permute-start | bytes 638984 | tf_op jit(solution)/shard_map/ppermute | solution.py:24
  92.4 4.8 %collective-permute-start.28 = (bf16[32,1664]{1,0:T(8,128)(2,1)S(1)}, bf16[32,1664]{1,0:T(8,128)(2,1)S(1)}, u32[]{:S(2)}, u32[]{:S(2)}) collective-permute-start(bf16[32,1664]{1,0:T(8,128)(2,1)S(1)} %slice.36), channel_id=1, source_target_pairs={{2,0},{3,1},{0,2},{1,3},{6,4},{7,5},{4,6},{5,7},{10,8},{11,9},{8,1... | collective-permute-start | bytes 319496 | tf_op jit(solution)/shard_map/ppermute | solution.py:24
  92.6 6.0 %collective-permute-start.29 = (bf16[32,1664]{1,0:T(8,128)(2,1)S(1)}, bf16[32,1664]{1,0:T(8,128)(2,1)S(1)}, u32[]{:S(2)}, u32[]{:S(2)}) collective-permute-start(bf16[32,1664]{1,0:T(8,128)(2,1)S(1)} %slice.37), channel_id=1, source_target_pairs={{6,0},{7,1},{4,2},{5,3},{2,4},{3,5},{0,6},{1,7},{14,8},{15,9},{12,... | collective-permute-start | bytes 319496 | tf_op jit(solution)/shard_map/ppermute | solution.py:24
  98.7 3.5 %collective-permute-start.30 = (bf16[256,1664]{1,0:T(8,128)(2,1)S(1)}, bf16[256,1664]{1,0:T(8,128)(2,1)S(1)}, u32[]{:S(2)}, u32[]{:S(2)}) collective-permute-start(bf16[256,1664]{1,0:T(8,128)(2,1)S(1)} %get-tuple-element.150), channel_id=1, source_target_pairs={{1,0},{0,1},{3,2},{2,3},{5,4},{4,5},{7,6},{6,7},{9,8},{8,9},{11,10... | collective-permute-start | bytes 2555912 | tf_op jit(solution)/shard_map/ppermute | solution.py:28
  98.8 7.5 %collective-permute-start.33 = (bf16[32,1664]{1,0:T(8,128)(2,1)S(1)}, bf16[32,1664]{1,0:T(8,128)(2,1)S(1)}, u32[]{:S(2)}, u32[]{:S(2)}) collective-permute-start(bf16[32,1664]{1,0:T(8,128)(2,1)S(1)} %slice.38), channel_id=1, source_target_pairs={{2,0},{3,1},{0,2},{1,3},{6,4},{7,5},{4,6},{5,7},{10,8},{11,9},{8,1... | collective-permute-start | bytes 319496 | tf_op jit(solution)/shard_map/ppermute | solution.py:24
  99.6 6.7 %collective-permute-start.34 = (bf16[32,1664]{1,0:T(8,128)(2,1)S(1)}, bf16[32,1664]{1,0:T(8,128)(2,1)S(1)}, u32[]{:S(2)}, u32[]{:S(2)}) collective-permute-start(bf16[32,1664]{1,0:T(8,128)(2,1)S(1)} %slice.39), channel_id=1, source_target_pairs={{6,0},{7,1},{4,2},{5,3},{2,4},{3,5},{0,6},{1,7},{14,8},{15,9},{12,... | collective-permute-start | bytes 319496 | tf_op jit(solution)/shard_map/ppermute | solution.py:24
  106.4 2.5 %collective-permute-start.35 = (bf16[256,1664]{1,0:T(8,128)(2,1)S(1)}, bf16[256,1664]{1,0:T(8,128)(2,1)S(1)}, u32[]{:S(2)}, u32[]{:S(2)}) collective-permute-start(bf16[256,1664]{1,0:T(8,128)(2,1)S(1)} %get-tuple-element.144), channel_id=1, source_target_pairs={{1,0},{0,1},{3,2},{2,3},{5,4},{4,5},{7,6},{6,7},{9,8},{8,9},{11,10... | collective-permute-start | bytes 2555912 | tf_op jit(solution)/shard_map/ppermute | solution.py:28
  106.5 14.3 %collective-permute-start.31 = (bf16[512,512]{1,0:T(8,128)(2,1)S(1)}, bf16[512,512]{1,0:T(8,128)(2,1)S(1)}, u32[]{:S(2)}, u32[]{:S(2)}) collective-permute-start(bf16[512,512]{1,0:T(8,128)(2,1)S(1)} %get-tuple-element.114), channel_id=1, source_target_pairs={{32,0},{40,8},{48,16},{56,24},{0,32},{8,40},{16,48},{24,56},{96,64... | collective-permute-start | bytes 1572872 | tf_op jit(solution)/shard_map/ppermute | solution.py:20
  106.6 15.4 %collective-permute-start.32 = (bf16[512,512]{1,0:T(8,128)(2,1)S(1)}, bf16[512,512]{1,0:T(8,128)(2,1)S(1)}, u32[]{:S(2)}, u32[]{:S(2)}) collective-permute-start(bf16[512,512]{1,0:T(8,128)(2,1)S(1)} %get-tuple-element.115), channel_id=1, source_target_pairs={{96,0},{104,8},{112,16},{120,24},{64,32},{72,40},{80,48},{88,56},{... | collective-permute-start | bytes 1572872 | tf_op jit(solution)/shard_map/ppermute | solution.py:20
  113.1 14.1 %collective-permute-start.41 = (bf16[512,512]{1,0:T(8,128)(2,1)S(1)}, bf16[512,512]{1,0:T(8,128)(2,1)S(1)}, u32[]{:S(2)}, u32[]{:S(2)}) collective-permute-start(bf16[512,512]{1,0:T(8,128)(2,1)S(1)} %get-tuple-element.131), channel_id=1, source_target_pairs={{8,0},{0,8},{24,16},{16,24},{40,32},{32,40},{56,48},{48,56},{72,64... | collective-permute-start | bytes 1572872 | tf_op jit(solution)/shard_map/ppermute | solution.py:20
  114.1 14.6 %collective-permute-start.42 = (bf16[512,512]{1,0:T(8,128)(2,1)S(1)}, bf16[512,512]{1,0:T(8,128)(2,1)S(1)}, u32[]{:S(2)}, u32[]{:S(2)}) collective-permute-start(bf16[512,512]{1,0:T(8,128)(2,1)S(1)} %get-tuple-element.132), channel_id=1, source_target_pairs={{24,0},{16,8},{8,16},{0,24},{56,32},{48,40},{40,48},{32,56},{88,64... | collective-permute-start | bytes 1572872 | tf_op jit(solution)/shard_map/ppermute | solution.py:20
  122.2 9.5 %collective-permute-start.36 = (bf16[256,512]{1,0:T(8,128)(2,1)S(1)}, bf16[256,512]{1,0:T(8,128)(2,1)S(1)}, u32[]{:S(2)}, u32[]{:S(2)}) collective-permute-start(bf16[256,512]{1,0:T(8,128)(2,1)S(1)} %get-tuple-element.125), channel_id=1, source_target_pairs={{32,0},{40,8},{48,16},{56,24},{0,32},{8,40},{16,48},{24,56},{96,64... | collective-permute-start | bytes 786440 | tf_op jit(solution)/shard_map/ppermute | solution.py:20
  122.8 8.9 %collective-permute-start.37 = (bf16[256,512]{1,0:T(8,128)(2,1)S(1)}, bf16[256,512]{1,0:T(8,128)(2,1)S(1)}, u32[]{:S(2)}, u32[]{:S(2)}) collective-permute-start(bf16[256,512]{1,0:T(8,128)(2,1)S(1)} %get-tuple-element.126), channel_id=1, source_target_pairs={{96,0},{104,8},{112,16},{120,24},{64,32},{72,40},{80,48},{88,56},{... | collective-permute-start | bytes 786440 | tf_op jit(solution)/shard_map/ppermute | solution.py:20
  128.9 9.3 %collective-permute-start.43 = (bf16[256,512]{1,0:T(8,128)(2,1)S(1)}, bf16[256,512]{1,0:T(8,128)(2,1)S(1)}, u32[]{:S(2)}, u32[]{:S(2)}) collective-permute-start(bf16[256,512]{1,0:T(8,128)(2,1)S(1)} %get-tuple-element.135), channel_id=1, source_target_pairs={{8,0},{0,8},{24,16},{16,24},{40,32},{32,40},{56,48},{48,56},{72,64... | collective-permute-start | bytes 786440 | tf_op jit(solution)/shard_map/ppermute | solution.py:20
  129.2 9.8 %collective-permute-start.44 = (bf16[256,512]{1,0:T(8,128)(2,1)S(1)}, bf16[256,512]{1,0:T(8,128)(2,1)S(1)}, u32[]{:S(2)}, u32[]{:S(2)}) collective-permute-start(bf16[256,512]{1,0:T(8,128)(2,1)S(1)} %get-tuple-element.136), channel_id=1, source_target_pairs={{24,0},{16,8},{8,16},{0,24},{56,32},{48,40},{40,48},{32,56},{88,64... | collective-permute-start | bytes 786440 | tf_op jit(solution)/shard_map/ppermute | solution.py:20
  131.8 10.9 %collective-permute-start.38 = (bf16[512,128]{1,0:T(8,128)(2,1)S(1)}, bf16[512,128]{1,0:T(8,128)(2,1)S(1)}, u32[]{:S(2)}, u32[]{:S(2)}) collective-permute-start(bf16[512,128]{1,0:T(8,128)(2,1)S(1)} %get-tuple-element.128), channel_id=1, source_target_pairs={{8,0},{0,8},{24,16},{16,24},{40,32},{32,40},{56,48},{48,56},{72,64... | collective-permute-start | bytes 393224 | tf_op jit(solution)/shard_map/ppermute | solution.py:20
  133.2 10.8 %collective-permute-start.39 = (bf16[512,128]{1,0:T(8,128)(2,1)S(1)}, bf16[512,128]{1,0:T(8,128)(2,1)S(1)}, u32[]{:S(2)}, u32[]{:S(2)}) collective-permute-start(bf16[512,128]{1,0:T(8,128)(2,1)S(1)} %get-tuple-element.129), channel_id=1, source_target_pairs={{16,0},{24,8},{0,16},{8,24},{48,32},{56,40},{32,48},{40,56},{80,64... | collective-permute-start | bytes 393224 | tf_op jit(solution)/shard_map/ppermute | solution.py:20
  135.5 8.5 %collective-permute-start.40 = (bf16[512,128]{1,0:T(8,128)(2,1)S(1)}, bf16[512,128]{1,0:T(8,128)(2,1)S(1)}, u32[]{:S(2)}, u32[]{:S(2)}) collective-permute-start(bf16[512,128]{1,0:T(8,128)(2,1)S(1)} %get-tuple-element.130), channel_id=1, source_target_pairs={{24,0},{16,8},{8,16},{0,24},{56,32},{48,40},{40,48},{32,56},{88,64... | collective-permute-start | bytes 393224 | tf_op jit(solution)/shard_map/ppermute | solution.py:20
  139.2 5.0 %collective-permute-start.45 = (bf16[512,128]{1,0:T(8,128)(2,1)S(1)}, bf16[512,128]{1,0:T(8,128)(2,1)S(1)}, u32[]{:S(2)}, u32[]{:S(2)}) collective-permute-start(bf16[512,128]{1,0:T(8,128)(2,1)S(1)} %get-tuple-element.138), channel_id=1, source_target_pairs={{32,0},{40,8},{48,16},{56,24},{0,32},{8,40},{16,48},{24,56},{96,64... | collective-permute-start | bytes 393224 | tf_op jit(solution)/shard_map/ppermute | solution.py:20
  139.3 7.7 %collective-permute-start.46 = (bf16[512,128]{1,0:T(8,128)(2,1)S(1)}, bf16[512,128]{1,0:T(8,128)(2,1)S(1)}, u32[]{:S(2)}, u32[]{:S(2)}) collective-permute-start(bf16[512,128]{1,0:T(8,128)(2,1)S(1)} %get-tuple-element.139), channel_id=1, source_target_pairs={{64,0},{72,8},{80,16},{88,24},{96,32},{104,40},{112,48},{120,56},{... | collective-permute-start | bytes 393224 | tf_op jit(solution)/shard_map/ppermute | solution.py:20
  142.7 6.2 %collective-permute-start.47 = (bf16[512,128]{1,0:T(8,128)(2,1)S(1)}, bf16[512,128]{1,0:T(8,128)(2,1)S(1)}, u32[]{:S(2)}, u32[]{:S(2)}) collective-permute-start(bf16[512,128]{1,0:T(8,128)(2,1)S(1)} %get-tuple-element.140), channel_id=1, source_target_pairs={{96,0},{104,8},{112,16},{120,24},{64,32},{72,40},{80,48},{88,56},{... | collective-permute-start | bytes 393224 | tf_op jit(solution)/shard_map/ppermute | solution.py:20

commit v4 on v3

--- a/solution.py
+++ b/solution.py
@@ -46,30 +46,33 @@
     )(*operands)
 
 
-def load_kernel(place, gate_hbm, up_hbm, down_hbm, gate, up, down, sem):
+def load_kernel(permuted, place, *refs):
+    count = (len(refs) - 1) // 2
+    sem = refs[-1]
     z, x = place[0], place[1]
-    copies = [pltpu.make_async_copy(gate_hbm, gate, sem.at[0]), pltpu.make_async_copy(up_hbm, up, sem.at[1])]
-    for dz in range(4):
-        for dx in range(4):
-            at = dz * 4 + dx
-            source = pl.ds(pl.multiple_of(((z ^ dz) * 4 + (x ^ dx)) * LANES, LANES), LANES)
+    copies = []
+    if permuted:
+        for at in range(16):
+            source = pl.ds(pl.multiple_of(((z ^ (at // 4)) * 4 + (x ^ (at % 4))) * LANES, LANES), LANES)
             target = slice(at * LANES, (at + 1) * LANES)
-            copies.append(pltpu.make_async_copy(down_hbm.at[:, source], down.at[:, target], sem.at[2 + at]))
+            copies.append(pltpu.make_async_copy(refs[0].at[:, source], refs[1].at[:, target], sem.at[at]))
+    else:
+        copies = [pltpu.make_async_copy(refs[i], refs[count + i], sem.at[i]) for i in range(count)]
     for copy in copies:
         copy.start()
     for copy in copies:
         copy.wait()
 
 
-def load(place, *weights):
+def load(permuted, place, *weights):
     out = call(
-        load_kernel,
+        functools.partial(load_kernel, permuted),
         "load",
         [pltpu.VMEM(w.shape, w.dtype) for w in weights],
-        [SMEM] + [HBM] * 3,
+        [SMEM] + [HBM] * len(weights),
         [place] + [pltpu.with_memory_space_constraint(w, pltpu.HBM) for w in weights],
-        scratch=[pltpu.SemaphoreType.DMA((18,))],
-        micros=5,
+        scratch=[pltpu.SemaphoreType.DMA((16,))],
+        micros=4,
     )
     return [pltpu.with_memory_space_constraint(w, pltpu.VMEM) for w in out]
 
@@ -294,8 +297,8 @@
     lines[0] = after(lines[0], lines[1][1])
     stacks = [jnp.stack(line) for line in lines]
     nexts = [[from_wide(axis, bits, stack) for bits in (1, 3)] for axis, stack in zip("xz", stacks)]
-    *weights, down_weight = load(place, *after((gate_weight, up_weight, down_weight), stacks))
-    nexts[0] = after(nexts[0], down_weight)
+    weights = load(False, place, *after((gate_weight, up_weight), stacks))
+    nexts[0] = after(nexts[0], weights)
     bases = [assemble(axis, place, [stack, *near]) for axis, stack, near in zip("zx", stacks, nexts)]
     fars = [(from_wide(axis, 1, three[:2]), from_wide(axis, 3, one[2:])) for axis, (one, three) in zip("xz", nexts)]
     fars[0] = after(fars[0], bases[1])
@@ -316,7 +319,8 @@
     together = lax.optimization_barrier
     half = parts[0][0].shape[0] // 2
     first = [first_round(from_y, p) for p in parts]
-    second = [second_round(from_y, relay(parts[0], *after(first[0], parts[1][0]))), None]
+    (down_weight,) = load(True, place, after(down_weight, parts[1][0]))
+    second = [second_round(from_y, relay(parts[0], *after(first[0], down_weight))), None]
     relayed = relay(parts[1], *first[1])
     second[0] = after(second[0], relayed[0])
     hidden = [hidden_of([parts[0][0], *first[0], *second[0]]), None]

time: 151 us -> 151 us (level)
  waiting for transfers between devices: 49.5 us -> 47.4 us
  Pallas kernels: 37.2 us -> 38.8 us
    ppermute x16, waiting for transfers between devices: 23.6 us -> 19.7 us  [from_y(): return lax.ppermute(array, 'narrow', [(i ^ bits * 2, i) for i in range(8)])]
    ppermute x28, waiting for transfers between devices: 25.1 us -> 26.8 us  [from_wide(): return lax.ppermute(array, 'wide', [(i ^ step, i) for i in range(16)])]
    pallas_call x20 -> x21, Pallas kernels: 37.2 us -> 38.8 us  [call(): pl.pallas_call(kernel, out_shape=out_shape, in_specs=in_specs, out_specs=...]
  transfers between devices with their start and end apart: 48 -> 48, of which waited for: 28 -> 27; matrix products, arithmetic and copies ran while one was open for 0% -> 0% of each run, Pallas kernels for 24% -> 25%
where the time goes in v4:
time: 151 us; the launch traced here: 150 us
  starting transfers between devices  61.2 us (41%)
  waiting for transfers between devices  47.4 us (31%)
  Pallas kernels  38.8 us (26%)
  local copies, waits for them, and re-layouts  1.65 us (1%)
    ppermute x28, starting transfers between devices, from_wide(): return lax.ppermute(array, 'wide', [(i ^ step, i) for i in range(16)])  39.9 us
    pallas_call x21, Pallas kernels, call(): pl.pallas_call(kernel, out_shape=out_shape, in_specs=in_specs, out_specs=...  38.8 us
    ppermute x28, waiting for transfers between devices, from_wide(): return lax.ppermute(array, 'wide', [(i ^ step, i) for i in range(16)])  26.8 us
    ppermute x16, starting transfers between devices, from_y(): return lax.ppermute(array, 'narrow', [(i ^ bits * 2, i) for i in range(8)])  20.3 us
    ppermute x16, waiting for transfers between devices, from_y(): return lax.ppermute(array, 'narrow', [(i ^ bits * 2, i) for i in range(8)])  19.7 us
  transfers between devices with their start and end apart: 48, of which 27 were waited for; matrix products, arithmetic and copies ran while one was open for 0% of the time, Pallas kernels for 25%

profile of v4, /device:TPU:0, one launch (start us, length us, event | category | flops | bytes accessed | tf_op | source)
XLA Modules:
  0.0 149.7 jit_solution(11337637118214743957)
XLA Ops:
  0.1 1.0 slice_bitcast_fusion
  1.1 1.7 %collective-permute-start.3 = (bf16[512,128]{1,0:T(8,128)(2,1)S(1)}, bf16[512,128]{1,0:T(8,128)(2,1)S(1)}, u32[]{:S(2)}, u32[]{:S(2)}) collective-permute-start(bf16[512,128]{1,0:T(8,128)(2,1)S(1)} %get-tuple-element.140), channel_id=1, source_target_pairs={{8,0},{0,8},{24,16},{16,24},{40,32},{32,40},{56,48},{48,56},{72,64... | collective-permute-start | bytes 393224 | tf_op jit(solution)/shard_map/ppermute | solution.py:20
  2.7 1.9 %collective-permute-start = (bf16[512,128]{1,0:T(8,128)(2,1)S(1)}, bf16[512,128]{1,0:T(8,128)(2,1)S(1)}, u32[]{:S(2)}, u32[]{:S(2)}) collective-permute-start(bf16[512,128]{1,0:T(8,128)(2,1)S(1)} %get-tuple-element.73), channel_id=1, source_target_pairs={{32,0},{40,8},{48,16},{56,24},{0,32},{8,40},{16,48},{24,56},{96,64... | collective-permute-start | bytes 393224 | tf_op jit(solution)/shard_map/ppermute | solution.py:20
  4.7 3.6 %collective-permute-start.1 = (bf16[512,128]{1,0:T(8,128)(2,1)S(1)}, bf16[512,128]{1,0:T(8,128)(2,1)S(1)}, u32[]{:S(2)}, u32[]{:S(2)}) collective-permute-start(bf16[512,128]{1,0:T(8,128)(2,1)S(1)} %get-tuple-element.73), channel_id=1, source_target_pairs={{64,0},{72,8},{80,16},{88,24},{96,32},{104,40},{112,48},{120,56},{... | collective-permute-start | bytes 393224 | tf_op jit(solution)/shard_map/ppermute | solution.py:20
  8.3 2.7 %collective-permute-start.6 = (bf16[512,128]{1,0:T(8,128)(2,1)S(1)}, bf16[512,128]{1,0:T(8,128)(2,1)S(1)}, u32[]{:S(2)}, u32[]{:S(2)}) collective-permute-start(bf16[512,128]{1,0:T(8,128)(2,1)S(1)} %get-tuple-element.140), channel_id=1, source_target_pairs={{16,0},{24,8},{0,16},{8,24},{48,32},{56,40},{32,48},{40,56},{80,64... | collective-permute-start | bytes 393224 | tf_op jit(solution)/shard_map/ppermute | solution.py:20
  11.5 2.6 %collective-permute-done.1 = bf16[512,128]{1,0:T(8,128)(2,1)S(1)} collective-permute-done((bf16[512,128]{1,0:T(8,128)(2,1)S(1)}, bf16[512,128]{1,0:T(8,128)(2,1)S(1)}, u32[]{:S(2)}, u32[]{:S(2)}) %collective-permute-start.1) | collective-permute-done | bytes 131104 | tf_op jit(solution)/shard_map/ppermute | solution.py:20
  14.1 1.9 %collective-permute-done.2 = bf16[512,128]{1,0:T(8,128)(2,1)S(1)} collective-permute-done((bf16[512,128]{1,0:T(8,128)(2,1)S(1)}, bf16[512,128]{1,0:T(8,128)(2,1)S(1)}, u32[]{:S(2)}, u32[]{:S(2)}) %collective-permute-start.2) | collective-permute-done | bytes 131104 | tf_op jit(solution)/shard_map/ppermute | solution.py:20
  16.7 2.8 %collective-permute-start.5 = (bf16[4,512,128]{2,1,0:T(8,128)(2,1)S(1)}, bf16[4,512,128]{2,1,0:T(8,128)(2,1)S(1)}, u32[]{:S(2)}, u32[]{:S(2)}) collective-permute-start(bf16[4,512,128]{2,1,0:T(8,128)(2,1)S(1)} %pad_maximum_fusion.refs_0_), channel_id=1, source_target_pairs={{24,0},{16,8},{8,16},{0,24},{56,32},{48,40},{40,48},{32,56},{88,64... | collective-permute-start | bytes 1572872 | tf_op jit(solution)/shard_map/ppermute | solution.py:20
  19.6 1.8 %collective-permute-start.11 = (bf16[4,512,128]{2,1,0:T(8,128)(2,1)S(1)}, bf16[4,512,128]{2,1,0:T(8,128)(2,1)S(1)}, u32[]{:S(2)}, u32[]{:S(2)}) collective-permute-start(bf16[4,512,128]{2,1,0:T(8,128)(2,1)S(1)} %pad_maximum_fusion.1.refs_0_), channel_id=1, source_target_pairs={{96,0},{104,8},{112,16},{120,24},{64,32},{72,40},{80,48},{88,56},{... | collective-permute-start | bytes 1572872 | tf_op jit(solution)/shard_map/ppermute | solution.py:20
  21.4 5.6 %load.2 = (bf16[2048,1664]{1,0:T(8,128)(2,1)S(1)}, bf16[2048,1664]{1,0:T(8,128)(2,1)S(1)}) custom-call(s32[4]{0:T(128)S(1)} %pad_add_fusion.place, bf16[2048,1664]{1,0:T(8,128)(2,1)} %refs_0_, bf16[2048,1664]{1,0:T(8,128)(2,1)} %refs_1_), custom_call_target="tpu_custom_call" | custom-call | flops 4000000000 | tf_op jit(solution)/shard_map/load/pallas_call | solution.py:36
  27.0 2.2 %collective-permute-done.4.refs_1_ = bf16[4,512,128]{2,1,0:T(8,128)(2,1)S(1)} collective-permute-done((bf16[4,512,128]{2,1,0:T(8,128)(2,1)S(1)}, bf16[4,512,128]{2,1,0:T(8,128)(2,1)S(1)}, u32[]{:S(2)}, u32[]{:S(2)}) %collective-permute-start.4) | collective-permute-done | bytes 524320 | tf_op jit(solution)/shard_map/ppermute | solution.py:20
  29.1 1.5 collective-permute-done.5.refs_2_
  31.0 2.6 %collective-permute-start.9 = (bf16[2,512,128]{2,1,0:T(8,128)(2,1)S(1)}, bf16[2,512,128]{2,1,0:T(8,128)(2,1)S(1)}, u32[]{:S(2)}, u32[]{:S(2)}) collective-permute-start(bf16[2,512,128]{2,1,0:T(8,128)(2,1)S(1)} %slice.33), channel_id=1, source_target_pairs={{24,0},{16,8},{8,16},{0,24},{56,32},{48,40},{40,48},{32,56},{88,64... | collective-permute-start | bytes 786440 | tf_op jit(solution)/shard_map/ppermute | solution.py:20
  33.6 1.0 assemble_z.2.refs_0_
  34.7 0.9 collective-permute-start.13
  35.6 1.0 assemble_x.2.refs_0_
  37.1 1.6 %collective-permute-done.9.refs_2_ = bf16[2,512,128]{2,1,0:T(8,128)(2,1)S(1)} collective-permute-done((bf16[2,512,128]{2,1,0:T(8,128)(2,1)S(1)}, bf16[2,512,128]{2,1,0:T(8,128)(2,1)S(1)}, u32[]{:S(2)}, u32[]{:S(2)}) %collective-permute-start.9) | collective-permute-done | bytes 262176 | tf_op jit(solution)/shard_map/ppermute | solution.py:20
  39.4 3.9 %project_other.2 = f32[256,3328]{1,0:T(8,128)S(1)} custom-call(bf16[512,2048]{1,0:T(8,128)(2,1)S(1)} %assemble_z.3.rows, bf16[2048,1664]{1,0:T(8,128)(2,1)S(1)} %get-tuple-element.79.gate_weight, bf16[2048,1664]{1,0:T(8,128)(2,1)S(1)} %get-tuple-element.80.up_weight), custom_call_target="tpu_custom_call" | custom-call | flops 4000000000 | tf_op jit(solution)/shard_map/project_other/pallas_call | solution.py:36
  43.4 0.7 assemble_x.3.rows
  44.1 3.9 %project_other.3 = f32[256,3328]{1,0:T(8,128)S(1)} custom-call(bf16[512,2048]{1,0:T(8,128)(2,1)S(1)} %assemble_x.3.rows, bf16[2048,1664]{1,0:T(8,128)(2,1)S(1)} %get-tuple-element.79.gate_weight, bf16[2048,1664]{1,0:T(8,128)(2,1)S(1)} %get-tuple-element.80.up_weight), custom_call_target="tpu_custom_call" | custom-call | flops 4000000000 | tf_op jit(solution)/shard_map/project_other/pallas_call | solution.py:36
  48.0 0.7 collective-permute-start.17
  49.4 3.9 %project_own.2 = (f32[64,3328]{1,0:T(8,128)S(1)}, bf16[64,3328]{1,0:T(8,128)(2,1)S(1)}, bf16[64,3328]{1,0:T(8,128)(2,1)S(1)}, f32[32,3328]{1,0:T(8,128)S(1)}, f32[32,3328]{1,0:T(8,128)S(1)}) custom-call(bf16[512,2048]{1,0:T(8,128)(2,1)S(1)} %assemble_z.3.rows, bf16[2048,1664]{1,0:T(8,128)(2,1)S(1)} %get-tuple-element.79.gate_weight, ...), custom_call_target="tpu_custom_call" | custom-call | flops 4000000000 | tf_op jit(solution)/shard_map/project_own/pallas_call | solution.py:36
  53.3 1.7 %collective-permute-start.15 = (bf16[64,3328]{1,0:T(8,128)(2,1)S(1)}, bf16[64,3328]{1,0:T(8,128)(2,1)S(1)}, u32[]{:S(2)}, u32[]{:S(2)}) collective-permute-start(bf16[64,3328]{1,0:T(8,128)(2,1)S(1)} %get-tuple-element.88), channel_id=1, source_target_pairs={{2,0},{3,1},{0,2},{1,3},{6,4},{7,5},{4,6},{5,7},{10,8},{11,9},{8,1... | collective-permute-start | bytes 1277960 | tf_op jit(solution)/shard_map/ppermute | solution.py:24
  55.0 2.2 %collective-permute-start.16 = (bf16[64,3328]{1,0:T(8,128)(2,1)S(1)}, bf16[64,3328]{1,0:T(8,128)(2,1)S(1)}, u32[]{:S(2)}, u32[]{:S(2)}) collective-permute-start(bf16[64,3328]{1,0:T(8,128)(2,1)S(1)} %get-tuple-element.89), channel_id=1, source_target_pairs={{6,0},{7,1},{4,2},{5,3},{2,4},{3,5},{0,6},{1,7},{14,8},{15,9},{12,... | collective-permute-start | bytes 1277960 | tf_op jit(solution)/shard_map/ppermute | solution.py:24
  57.2 3.9 %project_own.3 = (f32[64,3328]{1,0:T(8,128)S(1)}, bf16[64,3328]{1,0:T(8,128)(2,1)S(1)}, bf16[64,3328]{1,0:T(8,128)(2,1)S(1)}, f32[32,3328]{1,0:T(8,128)S(1)}, f32[32,3328]{1,0:T(8,128)S(1)}) custom-call(bf16[512,2048]{1,0:T(8,128)(2,1)S(1)} %assemble_x.3.rows, bf16[2048,1664]{1,0:T(8,128)(2,1)S(1)} %get-tuple-element.79.gate_weight, ...), custom_call_target="tpu_custom_call" | custom-call | flops 4000000000 | tf_op jit(solution)/shard_map/project_own/pallas_call | solution.py:36
  61.1 0.8 collective-permute-start.20
  62.4 3.8 %load.3.down_weight = bf16[1664,2048]{1,0:T(8,128)(2,1)S(1)} custom-call(s32[4]{0:T(128)S(1)} %pad_add_fusion.place, bf16[1664,2048]{1,0:T(8,128)(2,1)} %refs_0_.1), custom_call_target="tpu_custom_call" | custom-call | flops 4000000000 | tf_op jit(solution)/shard_map/load/pallas_call | solution.py:36
  66.3 2.6 %collective-permute-done.16.from_three.refs_2_ = bf16[64,3328]{1,0:T(8,128)(2,1)S(1)} collective-permute-done((bf16[64,3328]{1,0:T(8,128)(2,1)S(1)}, bf16[64,3328]{1,0:T(8,128)(2,1)S(1)}, u32[]{:S(2)}, u32[]{:S(2)}) %collective-permute-start.16) | collective-permute-done | bytes 426016 | tf_op jit(solution)/shard_map/ppermute | solution.py:24
  69.1 2.3 %collective-permute-start.19 = (bf16[32,3328]{1,0:T(8,128)(2,1)S(1)}, bf16[32,3328]{1,0:T(8,128)(2,1)S(1)}, u32[]{:S(2)}, u32[]{:S(2)}) collective-permute-start(bf16[32,3328]{1,0:T(8,128)(2,1)S(1)} %get-tuple-element.98), channel_id=1, source_target_pairs={{6,0},{7,1},{4,2},{5,3},{2,4},{3,5},{0,6},{1,7},{14,8},{15,9},{12,... | collective-permute-start | bytes 638984 | tf_op jit(solution)/shard_map/ppermute | solution.py:24
  71.3 3.9 %collective-permute-done.20.from_one.refs_1_ = bf16[64,3328]{1,0:T(8,128)(2,1)S(1)} collective-permute-done((bf16[64,3328]{1,0:T(8,128)(2,1)S(1)}, bf16[64,3328]{1,0:T(8,128)(2,1)S(1)}, u32[]{:S(2)}, u32[]{:S(2)}) %collective-permute-start.20) | collective-permute-done | bytes 426016 | tf_op jit(solution)/shard_map/ppermute | solution.py:24
  75.2 2.8 %collective-permute-done.21.from_three.refs_2_ = bf16[64,3328]{1,0:T(8,128)(2,1)S(1)} collective-permute-done((bf16[64,3328]{1,0:T(8,128)(2,1)S(1)}, bf16[64,3328]{1,0:T(8,128)(2,1)S(1)}, u32[]{:S(2)}, u32[]{:S(2)}) %collective-permute-start.21) | collective-permute-done | bytes 426016 | tf_op jit(solution)/shard_map/ppermute | solution.py:24
  78.2 2.3 %collective-permute-start.25 = (bf16[32,3328]{1,0:T(8,128)(2,1)S(1)}, bf16[32,3328]{1,0:T(8,128)(2,1)S(1)}, u32[]{:S(2)}, u32[]{:S(2)}) collective-permute-start(bf16[32,3328]{1,0:T(8,128)(2,1)S(1)} %get-tuple-element.106), channel_id=1, source_target_pairs={{6,0},{7,1},{4,2},{5,3},{2,4},{3,5},{0,6},{1,7},{14,8},{15,9},{12,... | collective-permute-start | bytes 638984 | tf_op jit(solution)/shard_map/ppermute | solution.py:24
  80.5 2.1 %collective-permute-done.19.refs_4_ = bf16[32,3328]{1,0:T(8,128)(2,1)S(1)} collective-permute-done((bf16[32,3328]{1,0:T(8,128)(2,1)S(1)}, bf16[32,3328]{1,0:T(8,128)(2,1)S(1)}, u32[]{:S(2)}, u32[]{:S(2)}) %collective-permute-start.19) | collective-permute-done | bytes 213024 | tf_op jit(solution)/shard_map/ppermute | solution.py:24
  82.9 2.3 %collective-permute-start.23 = (bf16[64,1664]{1,0:T(8,128)(2,1)S(1)}, bf16[64,1664]{1,0:T(8,128)(2,1)S(1)}, u32[]{:S(2)}, u32[]{:S(2)}) collective-permute-start(bf16[64,1664]{1,0:T(8,128)(2,1)S(1)} %hidden.2), channel_id=1, source_target_pairs={{6,0},{7,1},{4,2},{5,3},{2,4},{3,5},{0,6},{1,7},{14,8},{15,9},{12,... | collective-permute-start | bytes 638984 | tf_op jit(solution)/shard_map/ppermute | solution.py:24
  85.2 2.1 %collective-permute-done.25.refs_4_ = bf16[32,3328]{1,0:T(8,128)(2,1)S(1)} collective-permute-done((bf16[32,3328]{1,0:T(8,128)(2,1)S(1)}, bf16[32,3328]{1,0:T(8,128)(2,1)S(1)}, u32[]{:S(2)}, u32[]{:S(2)}) %collective-permute-start.25) | collective-permute-done | bytes 213024 | tf_op jit(solution)/shard_map/ppermute | solution.py:24
  87.6 2.3 %collective-permute-start.27 = (bf16[64,1664]{1,0:T(8,128)(2,1)S(1)}, bf16[64,1664]{1,0:T(8,128)(2,1)S(1)}, u32[]{:S(2)}, u32[]{:S(2)}) collective-permute-start(bf16[64,1664]{1,0:T(8,128)(2,1)S(1)} %hidden.3), channel_id=1, source_target_pairs={{6,0},{7,1},{4,2},{5,3},{2,4},{3,5},{0,6},{1,7},{14,8},{15,9},{12,... | collective-permute-start | bytes 638984 | tf_op jit(solution)/shard_map/ppermute | solution.py:24
  90.1 2.2 %collective-permute-done.23 = bf16[64,1664]{1,0:T(8,128)(2,1)S(1)} collective-permute-done((bf16[64,1664]{1,0:T(8,128)(2,1)S(1)}, bf16[64,1664]{1,0:T(8,128)(2,1)S(1)}, u32[]{:S(2)}, u32[]{:S(2)}) %collective-permute-start.23) | collective-permute-done | bytes 213024 | tf_op jit(solution)/shard_map/ppermute | solution.py:24
  92.6 2.3 %collective-permute-start.29 = (bf16[32,1664]{1,0:T(8,128)(2,1)S(1)}, bf16[32,1664]{1,0:T(8,128)(2,1)S(1)}, u32[]{:S(2)}, u32[]{:S(2)}) collective-permute-start(bf16[32,1664]{1,0:T(8,128)(2,1)S(1)} %slice.37), channel_id=1, source_target_pairs={{6,0},{7,1},{4,2},{5,3},{2,4},{3,5},{0,6},{1,7},{14,8},{15,9},{12,... | collective-permute-start | bytes 319496 | tf_op jit(solution)/shard_map/ppermute | solution.py:24
  94.9 1.4 collective-permute-done.27
  96.3 0.9 collective-permute-done.28
  97.2 1.4 collective-permute-done.29
  98.8 0.8 collective-permute-start.33
  99.6 2.5 %collective-permute-start.34 = (bf16[32,1664]{1,0:T(8,128)(2,1)S(1)}, bf16[32,1664]{1,0:T(8,128)(2,1)S(1)}, u32[]{:S(2)}, u32[]{:S(2)}) collective-permute-start(bf16[32,1664]{1,0:T(8,128)(2,1)S(1)} %slice.39), channel_id=1, source_target_pairs={{6,0},{7,1},{4,2},{5,3},{2,4},{3,5},{0,6},{1,7},{14,8},{15,9},{12,... | collective-permute-start | bytes 319496 | tf_op jit(solution)/shard_map/ppermute | solution.py:24
  102.3 4.0 %down_z.1 = (f32[512,512]{1,0:T(8,128)S(1)}, bf16[512,512]{1,0:T(8,128)(2,1)S(1)}, bf16[512,512]{1,0:T(8,128)(2,1)S(1)}, f32[256,512]{1,0:T(8,128)S(1)}, f32[256,512]{1,0:T(8,128)S(1)}) custom-call(bf16[512,1664]{1,0:T(8,128)(2,1)S(1)} %constant_dynamic-update-slice_fusion.5.rows, bf16[1664,2048]{1,0:T(8,128)(2,1)S(1)} %load.3.down_weight), custom_call_target="tpu_custom_call" | custom-call | flops 4000000000 | tf_op jit(solution)/shard_map/down_z/pallas_call | solution.py:36
  106.6 2.0 %collective-permute-start.32 = (bf16[512,512]{1,0:T(8,128)(2,1)S(1)}, bf16[512,512]{1,0:T(8,128)(2,1)S(1)}, u32[]{:S(2)}, u32[]{:S(2)}) collective-permute-start(bf16[512,512]{1,0:T(8,128)(2,1)S(1)} %get-tuple-element.113), channel_id=1, source_target_pairs={{96,0},{104,8},{112,16},{120,24},{64,32},{72,40},{80,48},{88,56},{... | collective-permute-start | bytes 1572872 | tf_op jit(solution)/shard_map/ppermute | solution.py:20
  108.9 4.0 %down_x.1 = (f32[512,512]{1,0:T(8,128)S(1)}, bf16[512,512]{1,0:T(8,128)(2,1)S(1)}, bf16[512,512]{1,0:T(8,128)(2,1)S(1)}, f32[256,512]{1,0:T(8,128)S(1)}, f32[256,512]{1,0:T(8,128)S(1)}) custom-call(bf16[512,1664]{1,0:T(8,128)(2,1)S(1)} %constant_dynamic-update-slice_fusion.16.rows, bf16[1664,2048]{1,0:T(8,128)(2,1)S(1)} %load.3.down_weight), custom_call_target="tpu_custom_call" | custom-call | flops 4000000000 | tf_op jit(solution)/shard_map/down_x/pallas_call | solution.py:36
  112.9 1.0 collective-permute-start.41
  113.9 2.3 %collective-permute-start.42 = (bf16[512,512]{1,0:T(8,128)(2,1)S(1)}, bf16[512,512]{1,0:T(8,128)(2,1)S(1)}, u32[]{:S(2)}, u32[]{:S(2)}) collective-permute-start(bf16[512,512]{1,0:T(8,128)(2,1)S(1)} %get-tuple-element.130), channel_id=1, source_target_pairs={{24,0},{16,8},{8,16},{0,24},{56,32},{48,40},{40,48},{32,56},{88,64... | collective-permute-start | bytes 1572872 | tf_op jit(solution)/shard_map/ppermute | solution.py:20
  116.3 4.5 %collective-permute-done.31.from_one = bf16[512,512]{1,0:T(8,128)(2,1)S(1)} collective-permute-done((bf16[512,512]{1,0:T(8,128)(2,1)S(1)}, bf16[512,512]{1,0:T(8,128)(2,1)S(1)}, u32[]{:S(2)}, u32[]{:S(2)}) %collective-permute-start.31) | collective-permute-done | bytes 524320 | tf_op jit(solution)/shard_map/ppermute | solution.py:20
  120.8 1.2 collective-permute-done.32.from_three
  122.7 2.0 %collective-permute-start.37 = (bf16[256,512]{1,0:T(8,128)(2,1)S(1)}, bf16[256,512]{1,0:T(8,128)(2,1)S(1)}, u32[]{:S(2)}, u32[]{:S(2)}) collective-permute-start(bf16[256,512]{1,0:T(8,128)(2,1)S(1)} %get-tuple-element.124), channel_id=1, source_target_pairs={{96,0},{104,8},{112,16},{120,24},{64,32},{72,40},{80,48},{88,56},{... | collective-permute-start | bytes 786440 | tf_op jit(solution)/shard_map/ppermute | solution.py:20
  124.7 2.3 %collective-permute-done.41.from_one = bf16[512,512]{1,0:T(8,128)(2,1)S(1)} collective-permute-done((bf16[512,512]{1,0:T(8,128)(2,1)S(1)}, bf16[512,512]{1,0:T(8,128)(2,1)S(1)}, u32[]{:S(2)}, u32[]{:S(2)}) %collective-permute-start.41) | collective-permute-done | bytes 524320 | tf_op jit(solution)/shard_map/ppermute | solution.py:20
  126.9 1.6 %collective-permute-done.42.from_three = bf16[512,512]{1,0:T(8,128)(2,1)S(1)} collective-permute-done((bf16[512,512]{1,0:T(8,128)(2,1)S(1)}, bf16[512,512]{1,0:T(8,128)(2,1)S(1)}, u32[]{:S(2)}, u32[]{:S(2)}) %collective-permute-start.42) | collective-permute-done | bytes 524320 | tf_op jit(solution)/shard_map/ppermute | solution.py:20
  129.0 2.4 %collective-permute-start.44 = (bf16[256,512]{1,0:T(8,128)(2,1)S(1)}, bf16[256,512]{1,0:T(8,128)(2,1)S(1)}, u32[]{:S(2)}, u32[]{:S(2)}) collective-permute-start(bf16[256,512]{1,0:T(8,128)(2,1)S(1)} %get-tuple-element.134), channel_id=1, source_target_pairs={{24,0},{16,8},{8,16},{0,24},{56,32},{48,40},{40,48},{32,56},{88,64... | collective-permute-start | bytes 786440 | tf_op jit(solution)/shard_map/ppermute | solution.py:20
  131.6 1.4 collective-permute-start.38
  133.0 2.4 %collective-permute-start.39 = (bf16[512,128]{1,0:T(8,128)(2,1)S(1)}, bf16[512,128]{1,0:T(8,128)(2,1)S(1)}, u32[]{:S(2)}, u32[]{:S(2)}) collective-permute-start(bf16[512,128]{1,0:T(8,128)(2,1)S(1)} %get-tuple-element.127), channel_id=1, source_target_pairs={{16,0},{24,8},{0,16},{8,24},{48,32},{56,40},{32,48},{40,56},{80,64... | collective-permute-start | bytes 393224 | tf_op jit(solution)/shard_map/ppermute | solution.py:20
  135.4 1.0 collective-permute-start.40
  136.4 1.6 %collective-permute-done.43.relay_one = bf16[256,512]{1,0:T(8,128)(2,1)S(1)} collective-permute-done((bf16[256,512]{1,0:T(8,128)(2,1)S(1)}, bf16[256,512]{1,0:T(8,128)(2,1)S(1)}, u32[]{:S(2)}, u32[]{:S(2)}) %collective-permute-start.43) | collective-permute-done | bytes 262176 | tf_op jit(solution)/shard_map/ppermute | solution.py:20
  138.0 0.8 collective-permute-done.44.relay_three
  139.1 3.1 %collective-permute-start.46 = (bf16[512,128]{1,0:T(8,128)(2,1)S(1)}, bf16[512,128]{1,0:T(8,128)(2,1)S(1)}, u32[]{:S(2)}, u32[]{:S(2)}) collective-permute-start(bf16[512,128]{1,0:T(8,128)(2,1)S(1)} %get-tuple-element.137), channel_id=1, source_target_pairs={{64,0},{72,8},{80,16},{88,24},{96,32},{104,40},{112,48},{120,56},{... | collective-permute-start | bytes 393224 | tf_op jit(solution)/shard_map/ppermute | solution.py:20
  142.2 1.6 %collective-permute-start.47 = (bf16[512,128]{1,0:T(8,128)(2,1)S(1)}, bf16[512,128]{1,0:T(8,128)(2,1)S(1)}, u32[]{:S(2)}, u32[]{:S(2)}) collective-permute-start(bf16[512,128]{1,0:T(8,128)(2,1)S(1)} %get-tuple-element.138), channel_id=1, source_target_pairs={{96,0},{104,8},{112,16},{120,24},{64,32},{72,40},{80,48},{88,56},{... | collective-permute-start | bytes 393224 | tf_op jit(solution)/shard_map/ppermute | solution.py:20
  144.0 2.5 %collective-permute-done.46.refs_6_ = bf16[512,128]{1,0:T(8,128)(2,1)S(1)} collective-permute-done((bf16[512,128]{1,0:T(8,128)(2,1)S(1)}, bf16[512,128]{1,0:T(8,128)(2,1)S(1)}, u32[]{:S(2)}, u32[]{:S(2)}) %collective-permute-start.46) | collective-permute-done | bytes 131104 | tf_op jit(solution)/shard_map/ppermute | solution.py:20
  146.5 1.8 %collective-permute-done.47.refs_7_ = bf16[512,128]{1,0:T(8,128)(2,1)S(1)} collective-permute-done((bf16[512,128]{1,0:T(8,128)(2,1)S(1)}, bf16[512,128]{1,0:T(8,128)(2,1)S(1)}, u32[]{:S(2)}, u32[]{:S(2)}) %collective-permute-start.47) | collective-permute-done | bytes 131104 | tf_op jit(solution)/shard_map/ppermute | solution.py:20
  148.4 1.4 last.1
  (77 shorter events, 8.8 us)
Async XLA Ops:
  1.1 9.9 %collective-permute-start.3 = (bf16[512,128]{1,0:T(8,128)(2,1)S(1)}, bf16[512,128]{1,0:T(8,128)(2,1)S(1)}, u32[]{:S(2)}, u32[]{:S(2)}) collective-permute-start(bf16[512,128]{1,0:T(8,128)(2,1)S(1)} %get-tuple-element.140), channel_id=1, source_target_pairs={{8,0},{0,8},{24,16},{16,24},{40,32},{32,40},{56,48},{48,56},{72,64... | collective-permute-start | bytes 393224 | tf_op jit(solution)/shard_map/ppermute | solution.py:20
  2.7 8.7 %collective-permute-start = (bf16[512,128]{1,0:T(8,128)(2,1)S(1)}, bf16[512,128]{1,0:T(8,128)(2,1)S(1)}, u32[]{:S(2)}, u32[]{:S(2)}) collective-permute-start(bf16[512,128]{1,0:T(8,128)(2,1)S(1)} %get-tuple-element.73), channel_id=1, source_target_pairs={{32,0},{40,8},{48,16},{56,24},{0,32},{8,40},{16,48},{24,56},{96,64... | collective-permute-start | bytes 393224 | tf_op jit(solution)/shard_map/ppermute | solution.py:20
  4.7 9.4 %collective-permute-start.1 = (bf16[512,128]{1,0:T(8,128)(2,1)S(1)}, bf16[512,128]{1,0:T(8,128)(2,1)S(1)}, u32[]{:S(2)}, u32[]{:S(2)}) collective-permute-start(bf16[512,128]{1,0:T(8,128)(2,1)S(1)} %get-tuple-element.73), channel_id=1, source_target_pairs={{64,0},{72,8},{80,16},{88,24},{96,32},{104,40},{112,48},{120,56},{... | collective-permute-start | bytes 393224 | tf_op jit(solution)/shard_map/ppermute | solution.py:20
  8.2 7.7 %collective-permute-start.2 = (bf16[512,128]{1,0:T(8,128)(2,1)S(1)}, bf16[512,128]{1,0:T(8,128)(2,1)S(1)}, u32[]{:S(2)}, u32[]{:S(2)}) collective-permute-start(bf16[512,128]{1,0:T(8,128)(2,1)S(1)} %get-tuple-element.73), channel_id=1, source_target_pairs={{96,0},{104,8},{112,16},{120,24},{64,32},{72,40},{80,48},{88,56},{... | collective-permute-start | bytes 393224 | tf_op jit(solution)/shard_map/ppermute | solution.py:20
  8.3 11.2 %collective-permute-start.6 = (bf16[512,128]{1,0:T(8,128)(2,1)S(1)}, bf16[512,128]{1,0:T(8,128)(2,1)S(1)}, u32[]{:S(2)}, u32[]{:S(2)}) collective-permute-start(bf16[512,128]{1,0:T(8,128)(2,1)S(1)} %get-tuple-element.140), channel_id=1, source_target_pairs={{16,0},{24,8},{0,16},{8,24},{48,32},{56,40},{32,48},{40,56},{80,64... | collective-permute-start | bytes 393224 | tf_op jit(solution)/shard_map/ppermute | solution.py:20
  11.0 8.5 %collective-permute-start.7 = (bf16[512,128]{1,0:T(8,128)(2,1)S(1)}, bf16[512,128]{1,0:T(8,128)(2,1)S(1)}, u32[]{:S(2)}, u32[]{:S(2)}) collective-permute-start(bf16[512,128]{1,0:T(8,128)(2,1)S(1)} %get-tuple-element.140), channel_id=1, source_target_pairs={{24,0},{16,8},{8,16},{0,24},{56,32},{48,40},{40,48},{32,56},{88,64... | collective-permute-start | bytes 393224 | tf_op jit(solution)/shard_map/ppermute | solution.py:20
  16.1 13.1 %collective-permute-start.4 = (bf16[4,512,128]{2,1,0:T(8,128)(2,1)S(1)}, bf16[4,512,128]{2,1,0:T(8,128)(2,1)S(1)}, u32[]{:S(2)}, u32[]{:S(2)}) collective-permute-start(bf16[4,512,128]{2,1,0:T(8,128)(2,1)S(1)} %pad_maximum_fusion.refs_0_), channel_id=1, source_target_pairs={{8,0},{0,8},{24,16},{16,24},{40,32},{32,40},{56,48},{48,56},{72,64... | collective-permute-start | bytes 1572872 | tf_op jit(solution)/shard_map/ppermute | solution.py:20
  16.7 13.9 %collective-permute-start.5 = (bf16[4,512,128]{2,1,0:T(8,128)(2,1)S(1)}, bf16[4,512,128]{2,1,0:T(8,128)(2,1)S(1)}, u32[]{:S(2)}, u32[]{:S(2)}) collective-permute-start(bf16[4,512,128]{2,1,0:T(8,128)(2,1)S(1)} %pad_maximum_fusion.refs_0_), channel_id=1, source_target_pairs={{24,0},{16,8},{8,16},{0,24},{56,32},{48,40},{40,48},{32,56},{88,64... | collective-permute-start | bytes 1572872 | tf_op jit(solution)/shard_map/ppermute | solution.py:20
  19.5 15.2 %collective-permute-start.10 = (bf16[4,512,128]{2,1,0:T(8,128)(2,1)S(1)}, bf16[4,512,128]{2,1,0:T(8,128)(2,1)S(1)}, u32[]{:S(2)}, u32[]{:S(2)}) collective-permute-start(bf16[4,512,128]{2,1,0:T(8,128)(2,1)S(1)} %pad_maximum_fusion.1.refs_0_), channel_id=1, source_target_pairs={{32,0},{40,8},{48,16},{56,24},{0,32},{8,40},{16,48},{24,56},{96,64... | collective-permute-start | bytes 1572872 | tf_op jit(solution)/shard_map/ppermute | solution.py:20
  19.6 15.0 %collective-permute-start.11 = (bf16[4,512,128]{2,1,0:T(8,128)(2,1)S(1)}, bf16[4,512,128]{2,1,0:T(8,128)(2,1)S(1)}, u32[]{:S(2)}, u32[]{:S(2)}) collective-permute-start(bf16[4,512,128]{2,1,0:T(8,128)(2,1)S(1)} %pad_maximum_fusion.1.refs_0_), channel_id=1, source_target_pairs={{96,0},{104,8},{112,16},{120,24},{64,32},{72,40},{80,48},{88,56},{... | collective-permute-start | bytes 1572872 | tf_op jit(solution)/shard_map/ppermute | solution.py:20
  30.6 6.5 %collective-permute-start.8 = (bf16[2,512,128]{2,1,0:T(8,128)(2,1)S(1)}, bf16[2,512,128]{2,1,0:T(8,128)(2,1)S(1)}, u32[]{:S(2)}, u32[]{:S(2)}) collective-permute-start(bf16[2,512,128]{2,1,0:T(8,128)(2,1)S(1)} %slice.32), channel_id=1, source_target_pairs={{8,0},{0,8},{24,16},{16,24},{40,32},{32,40},{56,48},{48,56},{72,64... | collective-permute-start | bytes 786440 | tf_op jit(solution)/shard_map/ppermute | solution.py:20
  31.0 7.7 %collective-permute-start.9 = (bf16[2,512,128]{2,1,0:T(8,128)(2,1)S(1)}, bf16[2,512,128]{2,1,0:T(8,128)(2,1)S(1)}, u32[]{:S(2)}, u32[]{:S(2)}) collective-permute-start(bf16[2,512,128]{2,1,0:T(8,128)(2,1)S(1)} %slice.33), channel_id=1, source_target_pairs={{24,0},{16,8},{8,16},{0,24},{56,32},{48,40},{40,48},{32,56},{88,64... | collective-permute-start | bytes 786440 | tf_op jit(solution)/shard_map/ppermute | solution.py:20
  34.6 8.7 %collective-permute-start.12 = (bf16[2,512,128]{2,1,0:T(8,128)(2,1)S(1)}, bf16[2,512,128]{2,1,0:T(8,128)(2,1)S(1)}, u32[]{:S(2)}, u32[]{:S(2)}) collective-permute-start(bf16[2,512,128]{2,1,0:T(8,128)(2,1)S(1)} %slice.40), channel_id=1, source_target_pairs={{32,0},{40,8},{48,16},{56,24},{0,32},{8,40},{16,48},{24,56},{96,64... | collective-permute-start | bytes 786440 | tf_op jit(solution)/shard_map/ppermute | solution.py:20
  34.7 8.6 %collective-permute-start.13 = (bf16[2,512,128]{2,1,0:T(8,128)(2,1)S(1)}, bf16[2,512,128]{2,1,0:T(8,128)(2,1)S(1)}, u32[]{:S(2)}, u32[]{:S(2)}) collective-permute-start(bf16[2,512,128]{2,1,0:T(8,128)(2,1)S(1)} %slice.41), channel_id=1, source_target_pairs={{96,0},{104,8},{112,16},{120,24},{64,32},{72,40},{80,48},{88,56},{... | collective-permute-start | bytes 786440 | tf_op jit(solution)/shard_map/ppermute | solution.py:20
  43.3 6.1 %collective-permute-start.14 = (f32[256,3328]{1,0:T(8,128)S(1)}, f32[256,3328]{1,0:T(8,128)S(1)}, u32[]{:S(2)}, u32[]{:S(2)}) collective-permute-start(f32[256,3328]{1,0:T(8,128)S(1)} %project_other.2), channel_id=1, source_target_pairs={{1,0},{0,1},{3,2},{2,3},{5,4},{4,5},{7,6},{6,7},{9,8},{8,9},{11,10... | collective-permute-start | bytes 10223624 | tf_op jit(solution)/shard_map/ppermute | solution.py:28
  48.0 9.2 %collective-permute-start.17 = (f32[256,3328]{1,0:T(8,128)S(1)}, f32[256,3328]{1,0:T(8,128)S(1)}, u32[]{:S(2)}, u32[]{:S(2)}) collective-permute-start(f32[256,3328]{1,0:T(8,128)S(1)} %project_other.3), channel_id=1, source_target_pairs={{1,0},{0,1},{3,2},{2,3},{5,4},{4,5},{7,6},{6,7},{9,8},{8,9},{11,10... | collective-permute-start | bytes 10223624 | tf_op jit(solution)/shard_map/ppermute | solution.py:28
  53.3 12.9 %collective-permute-start.15 = (bf16[64,3328]{1,0:T(8,128)(2,1)S(1)}, bf16[64,3328]{1,0:T(8,128)(2,1)S(1)}, u32[]{:S(2)}, u32[]{:S(2)}) collective-permute-start(bf16[64,3328]{1,0:T(8,128)(2,1)S(1)} %get-tuple-element.88), channel_id=1, source_target_pairs={{2,0},{3,1},{0,2},{1,3},{6,4},{7,5},{4,6},{5,7},{10,8},{11,9},{8,1... | collective-permute-start | bytes 1277960 | tf_op jit(solution)/shard_map/ppermute | solution.py:24
  55.0 13.9 %collective-permute-start.16 = (bf16[64,3328]{1,0:T(8,128)(2,1)S(1)}, bf16[64,3328]{1,0:T(8,128)(2,1)S(1)}, u32[]{:S(2)}, u32[]{:S(2)}) collective-permute-start(bf16[64,3328]{1,0:T(8,128)(2,1)S(1)} %get-tuple-element.89), channel_id=1, source_target_pairs={{6,0},{7,1},{4,2},{5,3},{2,4},{3,5},{0,6},{1,7},{14,8},{15,9},{12,... | collective-permute-start | bytes 1277960 | tf_op jit(solution)/shard_map/ppermute | solution.py:24
  61.1 14.1 %collective-permute-start.20 = (bf16[64,3328]{1,0:T(8,128)(2,1)S(1)}, bf16[64,3328]{1,0:T(8,128)(2,1)S(1)}, u32[]{:S(2)}, u32[]{:S(2)}) collective-permute-start(bf16[64,3328]{1,0:T(8,128)(2,1)S(1)} %get-tuple-element.101), channel_id=1, source_target_pairs={{2,0},{3,1},{0,2},{1,3},{6,4},{7,5},{4,6},{5,7},{10,8},{11,9},{8,1... | collective-permute-start | bytes 1277960 | tf_op jit(solution)/shard_map/ppermute | solution.py:24
  61.8 16.2 %collective-permute-start.21 = (bf16[64,3328]{1,0:T(8,128)(2,1)S(1)}, bf16[64,3328]{1,0:T(8,128)(2,1)S(1)}, u32[]{:S(2)}, u32[]{:S(2)}) collective-permute-start(bf16[64,3328]{1,0:T(8,128)(2,1)S(1)} %get-tuple-element.102), channel_id=1, source_target_pairs={{6,0},{7,1},{4,2},{5,3},{2,4},{3,5},{0,6},{1,7},{14,8},{15,9},{12,... | collective-permute-start | bytes 1277960 | tf_op jit(solution)/shard_map/ppermute | solution.py:24
  69.0 11.5 %collective-permute-start.18 = (bf16[32,3328]{1,0:T(8,128)(2,1)S(1)}, bf16[32,3328]{1,0:T(8,128)(2,1)S(1)}, u32[]{:S(2)}, u32[]{:S(2)}) collective-permute-start(bf16[32,3328]{1,0:T(8,128)(2,1)S(1)} %get-tuple-element.97), channel_id=1, source_target_pairs={{2,0},{3,1},{0,2},{1,3},{6,4},{7,5},{4,6},{5,7},{10,8},{11,9},{8,1... | collective-permute-start | bytes 638984 | tf_op jit(solution)/shard_map/ppermute | solution.py:24
  69.1 13.5 %collective-permute-start.19 = (bf16[32,3328]{1,0:T(8,128)(2,1)S(1)}, bf16[32,3328]{1,0:T(8,128)(2,1)S(1)}, u32[]{:S(2)}, u32[]{:S(2)}) collective-permute-start(bf16[32,3328]{1,0:T(8,128)(2,1)S(1)} %get-tuple-element.98), channel_id=1, source_target_pairs={{6,0},{7,1},{4,2},{5,3},{2,4},{3,5},{0,6},{1,7},{14,8},{15,9},{12,... | collective-permute-start | bytes 638984 | tf_op jit(solution)/shard_map/ppermute | solution.py:24
  78.1 7.0 %collective-permute-start.24 = (bf16[32,3328]{1,0:T(8,128)(2,1)S(1)}, bf16[32,3328]{1,0:T(8,128)(2,1)S(1)}, u32[]{:S(2)}, u32[]{:S(2)}) collective-permute-start(bf16[32,3328]{1,0:T(8,128)(2,1)S(1)} %get-tuple-element.103), channel_id=1, source_target_pairs={{2,0},{3,1},{0,2},{1,3},{6,4},{7,5},{4,6},{5,7},{10,8},{11,9},{8,1... | collective-permute-start | bytes 638984 | tf_op jit(solution)/shard_map/ppermute | solution.py:24
  78.2 9.1 %collective-permute-start.25 = (bf16[32,3328]{1,0:T(8,128)(2,1)S(1)}, bf16[32,3328]{1,0:T(8,128)(2,1)S(1)}, u32[]{:S(2)}, u32[]{:S(2)}) collective-permute-start(bf16[32,3328]{1,0:T(8,128)(2,1)S(1)} %get-tuple-element.106), channel_id=1, source_target_pairs={{6,0},{7,1},{4,2},{5,3},{2,4},{3,5},{0,6},{1,7},{14,8},{15,9},{12,... | collective-permute-start | bytes 638984 | tf_op jit(solution)/shard_map/ppermute | solution.py:24
  82.8 7.3 %collective-permute-start.22 = (bf16[64,1664]{1,0:T(8,128)(2,1)S(1)}, bf16[64,1664]{1,0:T(8,128)(2,1)S(1)}, u32[]{:S(2)}, u32[]{:S(2)}) collective-permute-start(bf16[64,1664]{1,0:T(8,128)(2,1)S(1)} %hidden.2), channel_id=1, source_target_pairs={{2,0},{3,1},{0,2},{1,3},{6,4},{7,5},{4,6},{5,7},{10,8},{11,9},{8,1... | collective-permute-start | bytes 638984 | tf_op jit(solution)/shard_map/ppermute | solution.py:24
  82.9 9.5 %collective-permute-start.23 = (bf16[64,1664]{1,0:T(8,128)(2,1)S(1)}, bf16[64,1664]{1,0:T(8,128)(2,1)S(1)}, u32[]{:S(2)}, u32[]{:S(2)}) collective-permute-start(bf16[64,1664]{1,0:T(8,128)(2,1)S(1)} %hidden.2), channel_id=1, source_target_pairs={{6,0},{7,1},{4,2},{5,3},{2,4},{3,5},{0,6},{1,7},{14,8},{15,9},{12,... | collective-permute-start | bytes 638984 | tf_op jit(solution)/shard_map/ppermute | solution.py:24
  87.6 7.4 %collective-permute-start.26 = (bf16[64,1664]{1,0:T(8,128)(2,1)S(1)}, bf16[64,1664]{1,0:T(8,128)(2,1)S(1)}, u32[]{:S(2)}, u32[]{:S(2)}) collective-permute-start(bf16[64,1664]{1,0:T(8,128)(2,1)S(1)} %hidden.3), channel_id=1, source_target_pairs={{2,0},{3,1},{0,2},{1,3},{6,4},{7,5},{4,6},{5,7},{10,8},{11,9},{8,1... | collective-permute-start | bytes 638984 | tf_op jit(solution)/shard_map/ppermute | solution.py:24
  87.6 8.6 %collective-permute-start.27 = (bf16[64,1664]{1,0:T(8,128)(2,1)S(1)}, bf16[64,1664]{1,0:T(8,128)(2,1)S(1)}, u32[]{:S(2)}, u32[]{:S(2)}) collective-permute-start(bf16[64,1664]{1,0:T(8,128)(2,1)S(1)} %hidden.3), channel_id=1, source_target_pairs={{6,0},{7,1},{4,2},{5,3},{2,4},{3,5},{0,6},{1,7},{14,8},{15,9},{12,... | collective-permute-start | bytes 638984 | tf_op jit(solution)/shard_map/ppermute | solution.py:24
  92.4 4.8 %collective-permute-start.28 = (bf16[32,1664]{1,0:T(8,128)(2,1)S(1)}, bf16[32,1664]{1,0:T(8,128)(2,1)S(1)}, u32[]{:S(2)}, u32[]{:S(2)}) collective-permute-start(bf16[32,1664]{1,0:T(8,128)(2,1)S(1)} %slice.36), channel_id=1, source_target_pairs={{2,0},{3,1},{0,2},{1,3},{6,4},{7,5},{4,6},{5,7},{10,8},{11,9},{8,1... | collective-permute-start | bytes 319496 | tf_op jit(solution)/shard_map/ppermute | solution.py:24
  92.6 6.0 %collective-permute-start.29 = (bf16[32,1664]{1,0:T(8,128)(2,1)S(1)}, bf16[32,1664]{1,0:T(8,128)(2,1)S(1)}, u32[]{:S(2)}, u32[]{:S(2)}) collective-permute-start(bf16[32,1664]{1,0:T(8,128)(2,1)S(1)} %slice.37), channel_id=1, source_target_pairs={{6,0},{7,1},{4,2},{5,3},{2,4},{3,5},{0,6},{1,7},{14,8},{15,9},{12,... | collective-permute-start | bytes 319496 | tf_op jit(solution)/shard_map/ppermute | solution.py:24
  98.7 3.5 %collective-permute-start.30 = (bf16[256,1664]{1,0:T(8,128)(2,1)S(1)}, bf16[256,1664]{1,0:T(8,128)(2,1)S(1)}, u32[]{:S(2)}, u32[]{:S(2)}) collective-permute-start(bf16[256,1664]{1,0:T(8,128)(2,1)S(1)} %get-tuple-element.148), channel_id=1, source_target_pairs={{1,0},{0,1},{3,2},{2,3},{5,4},{4,5},{7,6},{6,7},{9,8},{8,9},{11,10... | collective-permute-start | bytes 2555912 | tf_op jit(solution)/shard_map/ppermute | solution.py:28
  98.8 7.4 %collective-permute-start.33 = (bf16[32,1664]{1,0:T(8,128)(2,1)S(1)}, bf16[32,1664]{1,0:T(8,128)(2,1)S(1)}, u32[]{:S(2)}, u32[]{:S(2)}) collective-permute-start(bf16[32,1664]{1,0:T(8,128)(2,1)S(1)} %slice.38), channel_id=1, source_target_pairs={{2,0},{3,1},{0,2},{1,3},{6,4},{7,5},{4,6},{5,7},{10,8},{11,9},{8,1... | collective-permute-start | bytes 319496 | tf_op jit(solution)/shard_map/ppermute | solution.py:24
  99.6 6.6 %collective-permute-start.34 = (bf16[32,1664]{1,0:T(8,128)(2,1)S(1)}, bf16[32,1664]{1,0:T(8,128)(2,1)S(1)}, u32[]{:S(2)}, u32[]{:S(2)}) collective-permute-start(bf16[32,1664]{1,0:T(8,128)(2,1)S(1)} %slice.39), channel_id=1, source_target_pairs={{6,0},{7,1},{4,2},{5,3},{2,4},{3,5},{0,6},{1,7},{14,8},{15,9},{12,... | collective-permute-start | bytes 319496 | tf_op jit(solution)/shard_map/ppermute | solution.py:24
  106.4 2.5 %collective-permute-start.35 = (bf16[256,1664]{1,0:T(8,128)(2,1)S(1)}, bf16[256,1664]{1,0:T(8,128)(2,1)S(1)}, u32[]{:S(2)}, u32[]{:S(2)}) collective-permute-start(bf16[256,1664]{1,0:T(8,128)(2,1)S(1)} %get-tuple-element.142), channel_id=1, source_target_pairs={{1,0},{0,1},{3,2},{2,3},{5,4},{4,5},{7,6},{6,7},{9,8},{8,9},{11,10... | collective-permute-start | bytes 2555912 | tf_op jit(solution)/shard_map/ppermute | solution.py:28
  106.5 14.3 %collective-permute-start.31 = (bf16[512,512]{1,0:T(8,128)(2,1)S(1)}, bf16[512,512]{1,0:T(8,128)(2,1)S(1)}, u32[]{:S(2)}, u32[]{:S(2)}) collective-permute-start(bf16[512,512]{1,0:T(8,128)(2,1)S(1)} %get-tuple-element.112), channel_id=1, source_target_pairs={{32,0},{40,8},{48,16},{56,24},{0,32},{8,40},{16,48},{24,56},{96,64... | collective-permute-start | bytes 1572872 | tf_op jit(solution)/shard_map/ppermute | solution.py:20
  106.6 15.4 %collective-permute-start.32 = (bf16[512,512]{1,0:T(8,128)(2,1)S(1)}, bf16[512,512]{1,0:T(8,128)(2,1)S(1)}, u32[]{:S(2)}, u32[]{:S(2)}) collective-permute-start(bf16[512,512]{1,0:T(8,128)(2,1)S(1)} %get-tuple-element.113), channel_id=1, source_target_pairs={{96,0},{104,8},{112,16},{120,24},{64,32},{72,40},{80,48},{88,56},{... | collective-permute-start | bytes 1572872 | tf_op jit(solution)/shard_map/ppermute | solution.py:20
  112.9 14.0 %collective-permute-start.41 = (bf16[512,512]{1,0:T(8,128)(2,1)S(1)}, bf16[512,512]{1,0:T(8,128)(2,1)S(1)}, u32[]{:S(2)}, u32[]{:S(2)}) collective-permute-start(bf16[512,512]{1,0:T(8,128)(2,1)S(1)} %get-tuple-element.129), channel_id=1, source_target_pairs={{8,0},{0,8},{24,16},{16,24},{40,32},{32,40},{56,48},{48,56},{72,64... | collective-permute-start | bytes 1572872 | tf_op jit(solution)/shard_map/ppermute | solution.py:20
  113.9 14.6 %collective-permute-start.42 = (bf16[512,512]{1,0:T(8,128)(2,1)S(1)}, bf16[512,512]{1,0:T(8,128)(2,1)S(1)}, u32[]{:S(2)}, u32[]{:S(2)}) collective-permute-start(bf16[512,512]{1,0:T(8,128)(2,1)S(1)} %get-tuple-element.130), channel_id=1, source_target_pairs={{24,0},{16,8},{8,16},{0,24},{56,32},{48,40},{40,48},{32,56},{88,64... | collective-permute-start | bytes 1572872 | tf_op jit(solution)/shard_map/ppermute | solution.py:20
  122.1 9.3 %collective-permute-start.36 = (bf16[256,512]{1,0:T(8,128)(2,1)S(1)}, bf16[256,512]{1,0:T(8,128)(2,1)S(1)}, u32[]{:S(2)}, u32[]{:S(2)}) collective-permute-start(bf16[256,512]{1,0:T(8,128)(2,1)S(1)} %get-tuple-element.123), channel_id=1, source_target_pairs={{32,0},{40,8},{48,16},{56,24},{0,32},{8,40},{16,48},{24,56},{96,64... | collective-permute-start | bytes 786440 | tf_op jit(solution)/shard_map/ppermute | solution.py:20
  122.7 8.7 %collective-permute-start.37 = (bf16[256,512]{1,0:T(8,128)(2,1)S(1)}, bf16[256,512]{1,0:T(8,128)(2,1)S(1)}, u32[]{:S(2)}, u32[]{:S(2)}) collective-permute-start(bf16[256,512]{1,0:T(8,128)(2,1)S(1)} %get-tuple-element.124), channel_id=1, source_target_pairs={{96,0},{104,8},{112,16},{120,24},{64,32},{72,40},{80,48},{88,56},{... | collective-permute-start | bytes 786440 | tf_op jit(solution)/shard_map/ppermute | solution.py:20
  128.6 9.3 %collective-permute-start.43 = (bf16[256,512]{1,0:T(8,128)(2,1)S(1)}, bf16[256,512]{1,0:T(8,128)(2,1)S(1)}, u32[]{:S(2)}, u32[]{:S(2)}) collective-permute-start(bf16[256,512]{1,0:T(8,128)(2,1)S(1)} %get-tuple-element.133), channel_id=1, source_target_pairs={{8,0},{0,8},{24,16},{16,24},{40,32},{32,40},{56,48},{48,56},{72,64... | collective-permute-start | bytes 786440 | tf_op jit(solution)/shard_map/ppermute | solution.py:20
  129.0 9.8 %collective-permute-start.44 = (bf16[256,512]{1,0:T(8,128)(2,1)S(1)}, bf16[256,512]{1,0:T(8,128)(2,1)S(1)}, u32[]{:S(2)}, u32[]{:S(2)}) collective-permute-start(bf16[256,512]{1,0:T(8,128)(2,1)S(1)} %get-tuple-element.134), channel_id=1, source_target_pairs={{24,0},{16,8},{8,16},{0,24},{56,32},{48,40},{40,48},{32,56},{88,64... | collective-permute-start | bytes 786440 | tf_op jit(solution)/shard_map/ppermute | solution.py:20
  131.6 10.6 %collective-permute-start.38 = (bf16[512,128]{1,0:T(8,128)(2,1)S(1)}, bf16[512,128]{1,0:T(8,128)(2,1)S(1)}, u32[]{:S(2)}, u32[]{:S(2)}) collective-permute-start(bf16[512,128]{1,0:T(8,128)(2,1)S(1)} %get-tuple-element.126), channel_id=1, source_target_pairs={{8,0},{0,8},{24,16},{16,24},{40,32},{32,40},{56,48},{48,56},{72,64... | collective-permute-start | bytes 393224 | tf_op jit(solution)/shard_map/ppermute | solution.py:20
  133.0 10.8 %collective-permute-start.39 = (bf16[512,128]{1,0:T(8,128)(2,1)S(1)}, bf16[512,128]{1,0:T(8,128)(2,1)S(1)}, u32[]{:S(2)}, u32[]{:S(2)}) collective-permute-start(bf16[512,128]{1,0:T(8,128)(2,1)S(1)} %get-tuple-element.127), channel_id=1, source_target_pairs={{16,0},{24,8},{0,16},{8,24},{48,32},{56,40},{32,48},{40,56},{80,64... | collective-permute-start | bytes 393224 | tf_op jit(solution)/shard_map/ppermute | solution.py:20
  135.4 8.4 %collective-permute-start.40 = (bf16[512,128]{1,0:T(8,128)(2,1)S(1)}, bf16[512,128]{1,0:T(8,128)(2,1)S(1)}, u32[]{:S(2)}, u32[]{:S(2)}) collective-permute-start(bf16[512,128]{1,0:T(8,128)(2,1)S(1)} %get-tuple-element.128), channel_id=1, source_target_pairs={{24,0},{16,8},{8,16},{0,24},{56,32},{48,40},{40,48},{32,56},{88,64... | collective-permute-start | bytes 393224 | tf_op jit(solution)/shard_map/ppermute | solution.py:20
  139.0 5.0 %collective-permute-start.45 = (bf16[512,128]{1,0:T(8,128)(2,1)S(1)}, bf16[512,128]{1,0:T(8,128)(2,1)S(1)}, u32[]{:S(2)}, u32[]{:S(2)}) collective-permute-start(bf16[512,128]{1,0:T(8,128)(2,1)S(1)} %get-tuple-element.136), channel_id=1, source_target_pairs={{32,0},{40,8},{48,16},{56,24},{0,32},{8,40},{16,48},{24,56},{96,64... | collective-permute-start | bytes 393224 | tf_op jit(solution)/shard_map/ppermute | solution.py:20
  139.1 7.4 %collective-permute-start.46 = (bf16[512,128]{1,0:T(8,128)(2,1)S(1)}, bf16[512,128]{1,0:T(8,128)(2,1)S(1)}, u32[]{:S(2)}, u32[]{:S(2)}) collective-permute-start(bf16[512,128]{1,0:T(8,128)(2,1)S(1)} %get-tuple-element.137), channel_id=1, source_target_pairs={{64,0},{72,8},{80,16},{88,24},{96,32},{104,40},{112,48},{120,56},{... | collective-permute-start | bytes 393224 | tf_op jit(solution)/shard_map/ppermute | solution.py:20
  142.2 6.2 %collective-permute-start.47 = (bf16[512,128]{1,0:T(8,128)(2,1)S(1)}, bf16[512,128]{1,0:T(8,128)(2,1)S(1)}, u32[]{:S(2)}, u32[]{:S(2)}) collective-permute-start(bf16[512,128]{1,0:T(8,128)(2,1)S(1)} %get-tuple-element.138), channel_id=1, source_target_pairs={{96,0},{104,8},{112,16},{120,24},{64,32},{72,40},{80,48},{88,56},{... | collective-permute-start | bytes 393224 | tf_op jit(solution)/shard_map/ppermute | solution.py:20
